TPU v7x, 32 devices: a whole 2x2x4 slice. The times are simulated.
32 devices in a mesh: grp: 4 (over z), shard: 8 (over y, x, core).
Axes of the slice: x: 2, y: 2, z: 4, core: 2. Of those that a mesh axis runs over, the one named last changes fastest.
Arguments:
- context: bfloat16 [16384, 2048], P(('grp', 'shard')), may hold values from -6 to 6
- cotangent: bfloat16 [16384, 2048], P(('grp', 'shard')), may hold values from -0.046875 to 0.046875
- master: float32 [2048, 2048], P('shard'), may hold values from -0.125 to 0.125
- moment_one: float32 [2048, 2048], P('shard'), may hold values from -1.8 to 1.8
- moment_two: float32 [2048, 2048], P('shard'), may hold values from 0.3 to 3
Outputs:
- projected: bfloat16 [16384, 2048], P(('grp', 'shard'))
- context_grad: bfloat16 [16384, 2048], P(('grp', 'shard'))
- master_new: float32 [2048, 2048], P('shard')
- moment_one_new: float32 [2048, 2048], P('shard')
- moment_two_new: float32 [2048, 2048], P('shard')
All inputs are finite; a program needn't handle non-finite values.
Results may differ from a plain program's by a relative error of at most 0.0065.
Values may be sent and summed in bfloat16 or wider, within the bound.
No kernel may reach another device: no remote copies, remote signals or barrier semaphores. Data moves between devices by JAX's collectives and lax.ppermute only.
A program may use at most 128 MiB of HBM per device.

v0:
```python
import jax
import jax.numpy as jnp
from jax import lax
from jax.sharding import PartitionSpec as P

first_fix = 0.99997343860111
second_fix = 0.99407947078


def adamw(master, moment_one, moment_two, grad):
    one_new = 0.9 * moment_one + 0.1 * grad
    two_new = 0.95 * moment_two + 0.05 * grad * grad
    update = one_new / first_fix / (jnp.sqrt(two_new / second_fix) + 1e-08)
    master_new = master - 0.01 * (update + 0.1 * master)
    return (master_new, one_new, two_new)


def body(context, cotangent, master, moment_one, moment_two):
    weights = lax.all_gather(master.astype(jnp.bfloat16), "shard", axis=0, tiled=True)
    projected = jnp.dot(context, weights, preferred_element_type=jnp.float32).astype(jnp.bfloat16)
    context_grad = lax.dot_general(
        cotangent, weights, (((1,), (1,)), ((), ())), preferred_element_type=jnp.float32
    ).astype(jnp.bfloat16)
    partial_grad = lax.psum_scatter(
        lax.dot_general(
            context, cotangent, (((0,), (0,)), ((), ())), preferred_element_type=jnp.float32
        ).astype(jnp.bfloat16),
        "shard",
        scatter_dimension=0,
        tiled=True,
    )
    grad = lax.psum(partial_grad, "grp").astype(jnp.float32)
    master_new, one_new, two_new = adamw(master, moment_one, moment_two, grad)
    return (projected, context_grad, master_new, one_new, two_new)


def solution(mesh):
    in_specs = (
        P(("grp", "shard"), None),
        P(("grp", "shard"), None),
        P("shard", None),
        P("shard", None),
        P("shard", None),
    )
    out_specs = (
        P(("grp", "shard"), None),
        P(("grp", "shard"), None),
        P("shard", None),
        P("shard", None),
        P("shard", None),
    )
    return jax.shard_map(body, mesh=mesh, in_specs=in_specs, out_specs=out_specs, check_vma=False)
```

profile of v0, /device:TPU:0, one launch (start us, length us, event | category | flops | bytes accessed | tf_op | source)
XLA Modules:
  0.0 229.4 jit_solution(4886091592207675723)
XLA Ops:
  7.2 0.0 copy-start
  7.2 0.0 reduce-scatter.2.cloned.1.call-start
  7.2 1.5 copy-done
  8.8 8.5 %convolution_convert_fusion = bf16[2048,2048]{1,0:T(8,128)(2,1)} fusion(bf16[512,2048]{1,0:T(8,128)(2,1)} %param.5, bf16[512,2048]{1,0:T(8,128)(2,1)S(1)} %copy-done), kind=kOutput, calls=%fused_computation | convolution fusion | flops 4299161600 | bytes 12582912 | tf_op jit(solution)/shard_map/dot_general | solution.py:25
  17.2 0.0 reduce-scatter.2.cloned.1.call-update
  17.3 0.0 all-reduce.2.cloned.1.call-start
  17.3 74.1 %reduce-scatter.2.cloned.1.call-done = bf16[256,2048]{1,0:T(8,128)(2,1)} async-done(((bf16[2048,2048]{1,0:T(8,128)(2,1)}), bf16[256,2048]{1,0:T(8,128)(2,1)}) %reduce-scatter.2.cloned.1.call-update) | async-done | bytes 1048592 | tf_op jit(solution)/shard_map/reduce_scatter | solution.py:24
  91.4 0.0 all-reduce.2.cloned.1.call-update
  91.4 0.0 all-gather.2.cloned.1.call-start
  91.4 54.2 %all-reduce.2.cloned.1.call-done = bf16[256,2048]{1,0:T(8,128)(2,1)} async-done(((bf16[256,2048]{1,0:T(8,128)(2,1)}), bf16[256,2048]{1,0:T(8,128)(2,1)}) %all-reduce.2.cloned.1.call-update) | async-done | bytes 1048592 | tf_op jit(solution)/shard_map/psum | solution.py:32
  145.7 8.2 %multiply_subtract_fusion = (f32[256,2048]{1,0:T(8,128)}, f32[256,2048]{1,0:T(8,128)}, f32[256,2048]{1,0:T(8,128)}, bf16[256,2048]{1,0:T(8,128)(2,1)}) fusion(f32[256,2048]{1,0:T(8,128)} %param.7, bf16[256,2048]{1,0:T(8,128)(2,1)} %all-reduce.2.cloned.1.call-done, f32[256,2048]{1,0:T(8,128)} %param.8, f32[256,2048]{1,0:T(8,128)} %param.9), kind=kLoop, calls=%fused_computation.7 | loop fusion | flops 8912896 | bytes 14680064 | tf_op jit(solution)/shard_map/sub | solution.py:14
  153.9 0.0 all-gather.2.cloned.1.call-update
  153.9 53.9 %all-gather.2.cloned.1.call-done = bf16[2048,2048]{1,0:T(8,128)(2,1)} async-done(((bf16[256,2048]{1,0:T(8,128)(2,1)}), bf16[2048,2048]{1,0:T(8,128)(2,1)}) %all-gather.2.cloned.1.call-update) | async-done | bytes 8388624 | tf_op jit(solution)/shard_map/all_gather | solution.py:19
  207.9 0.0 copy-start.1
  207.9 0.0 copy-start.2
  207.9 9.2 %convolution_convert_fusion.1 = bf16[512,2048]{1,0:T(8,128)(2,1)} fusion(bf16[512,2048]{1,0:T(8,128)(2,1)S(1)} %copy-done, bf16[2048,2048]{1,0:T(8,128)(2,1)} %all-gather.2.cloned.1.call-done), kind=kOutput, calls=%fused_computation.2 | convolution fusion | flops 4296015872 | bytes 12582912 | tf_op jit(solution)/shard_map/dot_general | solution.py:21
  217.1 0.0 copy-done.1
  217.1 0.0 copy-done.2
  217.1 5.7 %convolution_convert_fusion.2 = bf16[512,2048]{1,0:T(8,128)(2,1)} fusion(bf16[512,2048]{1,0:T(8,128)(2,1)S(1)} %copy-done.2, bf16[2048,2048]{1,0:T(8,128)(2,1)S(1)} %copy-done.1), kind=kOutput, calls=%fused_computation.3 | convolution fusion | flops 4296015872 | bytes 12582912 | tf_op jit(solution)/shard_map/dot_general | solution.py:20
Async XLA Ops:
  7.2 1.6 copy-start
  7.2 84.2 %reduce-scatter.2.cloned.1.call-start = ((), (), s32[]{:S(2)}) async-start(), calls=%async_computation.2 | async-start | bytes 9437184 | tf_op jit(solution)/shard_map/reduce_scatter | solution.py:24
  17.3 128.4 %all-reduce.2.cloned.1.call-start = ((), (), s32[]{:S(2)}) async-start(), calls=%async_computation.3 | async-start | bytes 2097152 | tf_op jit(solution)/shard_map/psum | solution.py:32
  91.4 116.5 %all-gather.2.cloned.1.call-start = ((), (), s32[]{:S(2)}) async-start(), calls=%async_computation.1 | async-start | bytes 9437184 | tf_op jit(solution)/shard_map/all_gather | solution.py:19
  207.9 9.2 %copy-start.1 = (bf16[2048,2048]{1,0:T(8,128)(2,1)S(1)}, bf16[2048,2048]{1,0:T(8,128)(2,1)}, u32[]{:S(2)}) copy-start(bf16[2048,2048]{1,0:T(8,128)(2,1)} %all-gather.2.cloned.1.call-done) | copy-start | bytes 25165828
  207.9 9.2 %copy-start.2 = (bf16[512,2048]{1,0:T(8,128)(2,1)S(1)}, bf16[512,2048]{1,0:T(8,128)(2,1)}, u32[]{:S(2)}) copy-start(bf16[512,2048]{1,0:T(8,128)(2,1)} %param.5) | copy-start | bytes 6291460
Sparse Core Ops, SparseCore 0:
  17.4 73.9 reduce-scatter.1
  93.9 51.7 all-reduce.1
  154.1 53.7 all-gather.1
where the time goes:
time: 230 us; the launch traced here: 229 us
  waiting for transfers between devices  182 us (79%)
  matrix products  23.4 us (10%)
  between operations  13.8 us (6%)
  other arithmetic  8.22 us (4%)
    reduce_scatter x1, waiting for transfers between devices, body(): lax.psum_scatter(lax.dot_general(context, cotangent, (((0,), (0,)), ((),...  74.1 us
    psum x1, waiting for transfers between devices, body(): grad = lax.psum(partial_grad, 'grp').astype(jnp.float32)  54.2 us
    all_gather x1, waiting for transfers between devices, body(): lax.all_gather(master.astype(jnp.bfloat16), 'shard', axis=0, tiled=True)  53.9 us
    dot_general x1, matrix products, body(): lax.dot_general(cotangent, weights, (((1,), (1,)), ((), ())), preferred_e...  9.24 us
    dot_general x1, matrix products, body(): lax.dot_general(context, cotangent, (((0,), (0,)), ((), ())), preferred_e...  8.46 us
    sub x1, other arithmetic, adamw(): master_new = master - 0.01 * (update + 0.1 * master)  8.22 us
    dot_general x1, matrix products, body(): jnp.dot(context, weights, preferred_element_type=jnp.float32)  5.71 us
  transfers between devices with their start and end apart: 3, of which 3 were waited for; matrix products, arithmetic and copies ran while one was open for 0% of the time, Pallas kernels for 0%

commit v1 on v0

v1 whole, which is shorter than its diff:
```python
import jax
import jax.numpy as jnp
from jax import lax
from jax.experimental import pallas as pl
from jax.experimental.pallas import tpu as pltpu
from jax.sharding import PartitionSpec as P

first_fix = 0.99997343860111
second_fix = 0.99407947078
CHUNKS = (2, 1, 1)


def adamw(master, moment_one, moment_two, grad):
    one_new = 0.9 * moment_one + 0.1 * grad
    two_new = 0.95 * moment_two + 0.05 * grad * grad
    update = one_new / first_fix / (jnp.sqrt(two_new / second_fix) + 1e-08)
    master_new = master - 0.01 * (update + 0.1 * master)
    return (master_new, one_new, two_new)


def plain_body(context, cotangent, master, moment_one, moment_two):
    weights = lax.all_gather(master.astype(jnp.bfloat16), "shard", axis=0, tiled=True)
    projected = jnp.dot(context, weights, preferred_element_type=jnp.float32).astype(jnp.bfloat16)
    context_grad = lax.dot_general(
        cotangent, weights, (((1,), (1,)), ((), ())), preferred_element_type=jnp.float32
    ).astype(jnp.bfloat16)
    partial_grad = lax.psum_scatter(
        lax.dot_general(
            context, cotangent, (((0,), (0,)), ((), ())), preferred_element_type=jnp.float32
        ).astype(jnp.bfloat16),
        "shard",
        scatter_dimension=0,
        tiled=True,
    )
    grad = lax.psum(partial_grad, "grp").astype(jnp.float32)
    return (projected, context_grad, *adamw(master, moment_one, moment_two, grad))


ANY = pl.BlockSpec(memory_space=pl.ANY)
SMEM = pl.BlockSpec(memory_space=pltpu.SMEM)
VMEM = pl.BlockSpec(memory_space=pltpu.VMEM)


def dot(a, b, contract=(1, 0)):
    return lax.dot_general(a, b, (((contract[0],), (contract[1],)), ((), ())), preferred_element_type=jnp.float32)


def after(array, *others):
    return lax.optimization_barrier((array, *others))[0]


def add(a, b):
    return (a.astype(jnp.float32) + b.astype(jnp.float32)).astype(jnp.bfloat16)


def call(kernel, name, flops, outs, in_specs, out_specs, scratch=(), aliases=None):
    return pl.pallas_call(
        kernel,
        out_shape=outs,
        in_specs=in_specs,
        out_specs=out_specs,
        scratch_shapes=list(scratch),
        input_output_aliases=aliases or {},
        compiler_params=pltpu.CompilerParams(vmem_limit_bytes=56 * 2**20),
        cost_estimate=pl.CostEstimate(flops=flops, bytes_accessed=0, transcendentals=0),
        name=name,
    )


def aligned(index, rows):
    return pl.ds(pl.multiple_of(index * rows, rows), rows)


def grad_blocks(info, parts, contexts, cotangents, rows, subs):
    tokens, width = cotangents[0].shape
    half = width // 2
    sizes = [half * units // sum(CHUNKS) for units in CHUNKS]
    starts = [sum(sizes[:k]) for k in range(len(sizes))]
    count = len(parts[0])
    order = sorted({r for part in parts for r in part}, key=lambda r: -sum(r in part for part in parts))
    step = rows // subs

    def spans(r):
        wanted = [h for h in range(2) if r in parts[h]]
        return wanted[0] * half, (wanted[-1] + 1) * half

    def fill(info_ref, c0, c1, t0, t1, *out_refs):
        for r in order:
            at = aligned(info_ref[0] ^ r, rows)
            lo, hi = spans(r)
            total = dot(c0[:, at], t0[:, lo:hi], (0, 0)) + dot(c1[:, at], t1[:, lo:hi], (0, 0))
            total = total.astype(jnp.bfloat16)
            for h in range(2):
                if r in parts[h]:
                    for k, size in enumerate(sizes):
                        start = h * half + starts[k] - lo
                        for j in range(subs):
                            place = pl.multiple_of(parts[h].index(r) * rows + (info_ref[1] ^ j) * step, step)
                            out_refs[2 * k + h][pl.ds(place, step), :] = total[j * step : (j + 1) * step, start : start + size]

    def plain(h, k):
        cols = slice(h * half + starts[k], h * half + starts[k] + sizes[k])
        result = []
        for r in parts[h]:
            total = sum(
                dot(lax.dynamic_slice_in_dim(c, (info[0] ^ r) * rows, rows, axis=1), t[:, cols], (0, 0))
                for c, t in zip(contexts, cotangents)
            )
            result.append(reordered(total.astype(jnp.bfloat16), info[1], subs))
        return jnp.concatenate(result, axis=0)

    if rows % 128 or step % 16:
        return [[plain(h, k) for h in range(2)] for k in range(len(sizes))]
    outs = tuple(jax.ShapeDtypeStruct((count * rows, size), jnp.bfloat16) for size in sizes for _ in range(2))
    flops = 4 * count * rows * width * tokens
    result = call(fill, "grad_blocks", flops, outs, [SMEM] + [VMEM] * 4, (VMEM,) * len(outs))(info, *contexts, *cotangents)
    return [[result[2 * k + h] for h in range(2)] for k in range(len(sizes))]


def reordered(array, low, subs):
    step = array.shape[0] // subs
    return jnp.concatenate(
        [lax.dynamic_slice_in_dim(array, (low ^ j) * step, step, axis=0) for j in range(subs)], axis=0
    )


def sources(pieces):
    arrays = []
    for piece in pieces:
        if not any(piece[2] is array for array in arrays):
            arrays.append(piece[2])
    return arrays, [[piece[2] is array for array in arrays].index(True) for piece in pieces]


def run(copies):
    for copy in copies:
        copy.start()
    for copy in copies:
        copy.wait()


def weight_copies(info_ref, pieces, index, refs, blocks, weights, rows):
    width = weights.shape[1]
    copies = []
    for (r, half, _, row), source in zip(pieces, index):
        at = pl.ds(blocks.index(r) * rows, rows)
        target = weights.at[at, :]
        if half is not None:
            lo = pl.multiple_of((lax.rem(info_ref[1], 2) ^ half) * (width // 2), width // 2)
            target = weights.at[at, pl.ds(lo, width // 2)]
        copies.append((refs[source].at[pl.ds(row, rows), :], target))
    return copies


def products(info, pieces, context, cotangent, rows, kind):
    tokens, width = context.shape
    blocks = sorted({piece[0] for piece in pieces})
    depth = len(blocks) * rows
    arrays, index = sources(pieces)
    tile = min(512, width)

    def kernel(info_ref, context_ref, cotangent_ref, *rest):
        refs = rest[: len(arrays)]
        product_ref, columns_ref, weights, chosen, in_sems = rest[len(arrays) :]
        copies = weight_copies(info_ref, pieces, index, refs, blocks, weights, rows)
        for i, r in enumerate(blocks):
            copies.append((context_ref.at[:, aligned(info_ref[0] ^ r, rows)], chosen.at[:, pl.ds(i * rows, rows)]))
        run([pltpu.make_async_copy(a, b, in_sems.at[i]) for i, (a, b) in enumerate(copies)])
        columns_ref[...] = dot(cotangent_ref[...], weights[...], (1, 1)).astype(jnp.bfloat16)
        for i in range(width // tile):
            at = pl.ds(i * tile, tile)
            product_ref[:, at] = dot(chosen[...], weights[:, at]).astype(kind)

    scratch = [
        pltpu.VMEM((depth, width), jnp.bfloat16),
        pltpu.VMEM((tokens, depth), jnp.bfloat16),
        pltpu.SemaphoreType.DMA((len(pieces) + len(blocks),)),
    ]
    return call(
        kernel,
        "products",
        4 * tokens * depth * width,
        (jax.ShapeDtypeStruct((tokens, width), kind), jax.ShapeDtypeStruct((tokens, depth), jnp.bfloat16)),
        [SMEM, ANY, VMEM] + [ANY] * len(arrays),
        (VMEM, VMEM),
        scratch,
    )(info, context, cotangent, *arrays)


def joined(info, own, got, own_columns, got_columns, blocks, rows):
    tokens, width = own.shape
    placed = [(r ^ core, core, i) for core in range(2) for i, r in enumerate(blocks)]

    def kernel(info_ref, own_ref, got_ref, own_columns_ref, got_columns_ref, product_ref, out_ref, sems):
        refs = (own_columns_ref, got_columns_ref)
        copies = [
            pltpu.make_async_copy(
                refs[n].at[:, pl.ds(i * rows, rows)], out_ref.at[:, aligned(info_ref[0] ^ r, rows)], sems.at[place]
            )
            for place, (r, n, i) in enumerate(placed)
        ]
        for copy in copies:
            copy.start()
        product_ref[...] = (own_ref[...] + got_ref[...].astype(jnp.float32)).astype(jnp.bfloat16)
        for copy in copies:
            copy.wait()

    out = jax.ShapeDtypeStruct((tokens, width), jnp.bfloat16)
    return call(
        kernel,
        "joined",
        tokens * width,
        (out, out),
        [SMEM] + [VMEM] * 4,
        (VMEM, ANY),
        [pltpu.SemaphoreType.DMA((len(placed),))],
    )(info, own, got, own_columns, got_columns)


def plain_products(info, pieces, context, cotangent, rows):
    width = context.shape[1]
    weights = jnp.zeros((width, width), jnp.bfloat16)
    for r, half, array, row in pieces:
        lo = 0 if half is None else (lax.rem(info[1], 2) ^ half) * (width // 2)
        weights = lax.dynamic_update_slice(weights, array[row : row + rows], ((info[0] ^ r) * rows, lo))
    return dot(context, weights).astype(jnp.bfloat16), dot(cotangent, weights, (1, 1)).astype(jnp.bfloat16)


def make_body(groups, shards):
    bits = shards.bit_length() - 1
    x_masks = [2 << i for i in range((bits - 1) // 2)]
    y_masks = [2 << i for i in range((bits - 1) // 2, bits - 1)]
    masks = (x_masks + y_masks, y_masks + x_masks)
    subs = groups // 2
    group_masks = [1 << i for i in reversed(range(subs.bit_length() - 1))]

    def swap(array, mask):
        return lax.ppermute(array, "shard", [(i, i ^ mask) for i in range(shards)])

    def swap_group(array, mask):
        return lax.ppermute(array, "grp", [(i, i ^ mask) for i in range(groups)])

    def spread(pieces, masks):
        for mask in masks:
            pieces = {**pieces, **{r ^ mask: swap(piece, mask) for r, piece in pieces.items()}}
        return pieces

    def halving(masks):
        blocks = [0]
        for mask in reversed(masks):
            blocks = blocks + [b ^ mask for b in blocks]
        return blocks

    def body(context, cotangent, master, moment_one, moment_two):
        shard, group = lax.axis_index("shard"), lax.axis_index("grp")
        rows, width = master.shape
        half = width // 2
        odd = lax.rem(group, 2)
        low = lax.rem(group, subs)
        info = jnp.stack([shard, low if subs > 1 else odd])
        order_of_rows = low
        tiled = rows % 128 == 0 and (rows // subs) % 16 == 0 and subs > 1
        latest = []

        def then(array):
            return after(array, *latest)

        def did(result):
            latest[:] = [result]
            return result

        def named(names, array, flip=0):
            return [(r, h ^ flip, array, i * rows) for i, (r, h) in enumerate(names)]

        contexts, cotangents = (context, swap(context, 1)), (cotangent, swap(cotangent, 1))

        weights = master.astype(jnp.bfloat16)
        left, right = weights[:, :half], weights[:, half:]
        mine, other = jnp.where(odd == 1, right, left), jnp.where(odd == 1, left, right)
        near_x = {r: p for r, p in spread({0: mine}, x_masks).items() if r}
        near_y = {r: p for r, p in spread({0: other}, y_masks).items() if r}

        orders = [halving(m) for m in masks]
        count = len(orders[0]) // 2
        sent = grad_blocks(info, [o[count:] for o in orders], contexts, cotangents, rows, subs)
        did(sent[-1][-1])
        got = {0: [swap(sent[0][h], masks[h][0]) for h in range(2)]}

        near = jnp.concatenate([then(p) for p in [*near_x.values(), *near_y.values()]], axis=0)
        did(near)
        near_names = [(r, 0) for r in near_x] + [(r, 1) for r in near_y]
        near_group = swap_group(near, 1)
        far_x = spread({r: then(p) for r, p in near_x.items()}, y_masks)
        far_y = spread({r: then(p) for r, p in near_y.items()}, x_masks)
        far_names = [(r, 0) for r in far_x if r not in near_x] + [(r, 1) for r in far_y if r not in near_y]
        far = [(far_x, far_y)[h][r] for r, h in far_names]
        pieces = [(0, None, weights, 0)] + named(near_names, near) + named(near_names, near_group, flip=1)
        pieces += [(r, h, array, 0) for (r, h), array in zip(far_names, far)]
        kept = grad_blocks(info, [o[:count] for o in orders], contexts, (then(cotangent), cotangents[1]), rows, subs)
        did(kept[-1][-1])

        def halve_all(k, level):
            come, got[k] = got[k], [None, None]
            for h in range(2):
                total = did(add(kept[k][h], then(come[h])))
                size = total.shape[0] // 2
                kept[k][h], got[k][h] = total[:size], swap(total[size:], masks[h][level])

        summed, come, stage = {}, {}, {}

        def enter(k):
            parts = [did(add(kept[k][h], then(got[k][h]))) for h in range(2)]
            summed[k], stage[k] = jnp.concatenate(parts, axis=1), 0
            leave(k)

        def leave(k):
            j, steps = stage[k], len(group_masks)
            if j < steps:
                size = summed[k].shape[0] // 2
                come[k] = swap_group(summed[k][size:], group_masks[j])
                summed[k] = summed[k][:size]
            elif j == steps:
                come[k] = swap_group(summed[k], subs)
            elif j <= 2 * steps:
                come[k] = swap_group(summed[k], group_masks[2 * steps - j])

        def advance(k):
            if stage[k] <= len(group_masks):
                summed[k] = did(add(summed[k], then(come[k])))
            else:
                summed[k] = did(jnp.concatenate([summed[k], then(come[k])], axis=0))
            stage[k] += 1
            leave(k)

        last = 2 * len(group_masks) + 1
        levels = len(masks[0])
        chunks = len(CHUNKS)

        def halve_to_end(k, start):
            for level in range(start, levels):
                halve_all(k, level)

        def begin(k, *also):
            got[k] = [swap(after(sent[k][h], *latest, *also), masks[h][0]) for h in range(2)]

        halve_to_end(0, 1)
        begin(1, *far)
        enter(0)
        if tiled:
            blocks = sorted({piece[0] for piece in pieces})
            sent_part, sent_columns = products(info, pieces, then(contexts[1]), cotangents[1], rows, jnp.bfloat16)
            did(sent_part)
            got_part, got_columns = swap(sent_part, 1), swap(sent_columns, 1)
        halve_to_end(1, 1)
        begin(2)
        advance(0)
        enter(1)
        if tiled:
            part, own_columns = products(info, pieces, then(context), cotangent, rows, jnp.float32)
            did(part)
        halve_to_end(2, 1)
        advance(0)
        enter(2)
        advance(1)
        if tiled:
            projected, columns = joined(info, then(part), got_part, own_columns, got_columns, blocks, rows)
            did(projected)
        else:
            pieces += [(r ^ 1, h, swap(array, 1), row) for r, h, array, row in pieces]
            projected, columns = plain_products(info, pieces, context, cotangent, rows)
        advance(2)
        advance(1)
        while any(stage[k] < last for k in range(chunks)):
            for k in range(chunks):
                if stage[k] < last:
                    advance(k)
        sizes = [half * units // sum(CHUNKS) for units in CHUNKS]
        grad = [summed[k][:, h * sizes[k] : (h + 1) * sizes[k]] for h in range(2) for k in range(chunks)]
        grad = reordered(jnp.concatenate(grad, axis=1), order_of_rows, subs).astype(jnp.float32)
        updated = adamw(master, moment_one, moment_two, grad)
        return (projected, columns, *updated)

    return body


def power_of_two(n):
    return n > 0 and n & (n - 1) == 0


def solution(mesh):
    groups, shards = mesh.shape["grp"], mesh.shape["shard"]
    regular = power_of_two(groups) and power_of_two(shards) and groups >= 2 and shards >= 8
    token, state = P(("grp", "shard"), None), P("shard", None)
    return jax.shard_map(
        make_body(groups, shards) if regular else plain_body,
        mesh=mesh,
        in_specs=(token, token, state, state, state),
        out_specs=(token, token, state, state, state),
        check_vma=False,
    )
```

time: 230 us -> 122 us (0.53)
  waiting for transfers between devices: 182 us -> 31.7 us
  Pallas kernels: 0 us -> 40.5 us
  starting transfers between devices: 0.12 us -> 31.6 us
  matrix products: 23.4 us -> 0 us
  between operations: 13.8 us -> 1.16 us
  local copies, waits for them, and re-layouts: 1.55 us -> 6.71 us
    reduce_scatter x1 -> x0, waiting for transfers between devices: 74.1 us -> none  [body(): lax.psum_scatter(lax.dot_general(context, cotangent, (((0,), (0,)), ((),...]
    psum x1 -> x0, waiting for transfers between devices: 54.2 us -> none  [body(): grad = lax.psum(partial_grad, 'grp').astype(jnp.float32)]
    all_gather x1 -> x0, waiting for transfers between devices: 53.9 us -> none  [body(): lax.all_gather(master.astype(jnp.bfloat16), 'shard', axis=0, tiled=True)]
    pallas_call x0 -> x5, Pallas kernels: none -> 40.5 us  [the longest x2 20.9 us: products(): call(kernel, 'products', 4 * tokens * depth * width, (jax.ShapeDtypeStruc...]
    ppermute x0 -> x30, waiting for transfers between devices: none -> 31.7 us  [the longest x20 19.1 us: swap(): return lax.ppermute(array, 'shard', [(i, i ^ mask) for i in range(shards)])]
    ppermute x0 -> x30, starting transfers between devices: none -> 31.6 us  [the longest x20 20.6 us: swap(): return lax.ppermute(array, 'shard', [(i, i ^ mask) for i in range(shards)])]
    dot_general x3 -> x0, matrix products: 23.4 us -> none  [the longest x1 9.24 us: body(): lax.dot_general(cotangent, weights, (((1,), (1,)), ((), ())), preferred_e...]
    sub x1, other arithmetic: 8.22 us -> 3.89 us  [adamw(): master_new = master - 0.01 * (update + 0.1 * master)]
  transfers between devices with their start and end apart: 3 -> 30, of which waited for: 3 -> 8; matrix products, arithmetic and copies ran while one was open for 0% -> 7% of each run, Pallas kernels for 0% -> 33%
where the time goes in v1:
time: 122 us; the launch traced here: 121 us
  Pallas kernels  40.5 us (33%)
  waiting for transfers between devices  31.7 us (26%)
  starting transfers between devices  31.6 us (26%)
  other arithmetic  9.61 us (8%)
  local copies, waits for them, and re-layouts  6.71 us (6%)
    pallas_call x2, Pallas kernels, products(): call(kernel, 'products', 4 * tokens * depth * width, (jax.ShapeDtypeStruc...  20.9 us
    ppermute x20, starting transfers between devices, swap(): return lax.ppermute(array, 'shard', [(i, i ^ mask) for i in range(shards)])  20.6 us
    ppermute x20, waiting for transfers between devices, swap(): return lax.ppermute(array, 'shard', [(i, i ^ mask) for i in range(shards)])  19.1 us
    pallas_call x2, Pallas kernels, grad_blocks(): call(fill, 'grad_blocks', flops, outs, [SMEM] + [VMEM] * 4, (VMEM,) * len...  13.6 us
    ppermute x10, waiting for transfers between devices, swap_group(): return lax.ppermute(array, 'grp', [(i, i ^ mask) for i in range(groups)])  12.6 us
    ppermute x10, starting transfers between devices, swap_group(): return lax.ppermute(array, 'grp', [(i, i ^ mask) for i in range(groups)])  11 us
    pallas_call x1, Pallas kernels, joined(): call(kernel, 'joined', tokens * width, (out, out), [SMEM] + [VMEM] * 4, (...  6.07 us
    unnamed x31, local copies, waits for them, and re-layouts  5.45 us
  transfers between devices with their start and end apart: 30, of which 8 were waited for; matrix products, arithmetic and copies ran while one was open for 7% of the time, Pallas kernels for 33%

profile of v1, /device:TPU:0, one launch (start us, length us, event | category | flops | bytes accessed | tf_op | source)
XLA Modules:
  0.0 121.3 jit_solution(11693278851310293958)
XLA Ops:
  0.6 0.5 collective-permute-start
  1.1 0.1 collective-permute-start.2
  1.2 1.7 %convert_element_type.168.rest_0_ = bf16[256,2048]{1,0:T(8,128)(2,1)S(1)} convert(f32[256,2048]{1,0:T(8,128)} %param.7) | non-fusion elementwise | flops 524288 | bytes 3145728 | tf_op jit(solution)/shard_map/convert_element_type | solution.py:277
  3.0 1.1 broadcast_select_fusion
  4.1 2.9 %collective-permute-start.1 = (bf16[256,1024]{1,0:T(8,128)(2,1)}, bf16[256,1024]{1,0:T(8,128)(2,1)}, u32[]{:S(2)}, u32[]{:S(2)}) collective-permute-start(bf16[256,1024]{1,0:T(8,128)(2,1)} %get-tuple-element.113), channel_id=1, source_target_pairs={{0,2},{1,3},{2,0},{3,1},{4,6},{5,7},{6,4},{7,5},{8,10},{9,11},{10,... | collective-permute-start | bytes 1572872 | tf_op jit(solution)/shard_map/ppermute | solution.py:238
  7.0 1.5 %collective-permute-start.3 = (bf16[256,1024]{1,0:T(8,128)(2,1)}, bf16[256,1024]{1,0:T(8,128)(2,1)}, u32[]{:S(2)}, u32[]{:S(2)}) collective-permute-start(bf16[256,1024]{1,0:T(8,128)(2,1)} %get-tuple-element.112), channel_id=1, source_target_pairs={{0,4},{1,5},{2,6},{3,7},{4,0},{5,1},{6,2},{7,3},{8,12},{9,13},{10,... | collective-permute-start | bytes 1572872 | tf_op jit(solution)/shard_map/ppermute | solution.py:238
  8.5 0.6 pad_add_fusion.info_ref
  9.1 1.3 %copy-done.1 = bf16[512,2048]{1,0:T(8,128)(2,1)} copy-done((bf16[512,2048]{1,0:T(8,128)(2,1)}, bf16[512,2048]{1,0:T(8,128)(2,1)S(1)}, u32[]{:S(2)}) %copy-start.1) | copy-done | bytes 2097176
  10.4 6.9 %grad_blocks.2 = (bf16[512,512]{1,0:T(8,128)(2,1)}, bf16[512,512]{1,0:T(8,128)(2,1)}, bf16[512,256]{1,0:T(8,128)(2,1)}, bf16[512,256]{1,0:T(8,128)(2,1)}, bf16[5...) custom-call(s32[2]{0:T(128)} %pad_add_fusion.info_ref, bf16[512,2048]{1,0:T(8,128)(2,1)} %context_ref, ...), custom_call_target="tpu_custom_call" | custom-call | flops 2147483648 | tf_op jit(solution)/shard_map/grad_blocks/pallas_call | solution.py:116
  17.3 1.1 collective-permute-start.5
  18.4 1.5 %collective-permute-start.4 = (bf16[512,512]{1,0:T(8,128)(2,1)}, bf16[512,512]{1,0:T(8,128)(2,1)S(1)}, u32[]{:S(2)}, u32[]{:S(2)}) collective-permute-start(bf16[512,512]{1,0:T(8,128)(2,1)} %get-tuple-element.63), channel_id=1, source_target_pairs={{0,4},{1,5},{2,6},{3,7},{4,0},{5,1},{6,2},{7,3},{8,12},{9,13},{10,... | collective-permute-start | bytes 1572872 | tf_op jit(solution)/shard_map/ppermute | solution.py:238
  19.9 1.1 collective-permute-done.3
  20.9 1.1 constant_dynamic-update-slice_fusion.1
  22.0 1.1 constant_dynamic-update-slice_fusion.rest_1_
  23.1 0.0 copy-start.12
  23.1 1.6 %collective-permute-start.12 = (bf16[512,1024]{1,0:T(8,128)(2,1)S(1)}, bf16[512,1024]{1,0:T(8,128)(2,1)}, u32[]{:S(2)}, u32[]{:S(2)}) collective-permute-start(bf16[512,1024]{1,0:T(8,128)(2,1)S(1)} %constant_dynamic-update-slice_fusion.rest_1_), channel_id=1, source_target_pairs={{0,8},{8,0},{16,24},{24,16},{1,9},{9,1},{17,25},{25,17},{2,10},{10... | collective-permute-start | bytes 3145736 | tf_op jit(solution)/shard_map/ppermute | solution.py:241
  24.8 1.5 %collective-permute-start.6 = (bf16[256,1024]{1,0:T(8,128)(2,1)}, bf16[256,1024]{1,0:T(8,128)(2,1)}, u32[]{:S(2)}, u32[]{:S(2)}) collective-permute-start(bf16[256,1024]{1,0:T(8,128)(2,1)} %collective-permute-done.1), channel_id=1, source_target_pairs={{0,4},{1,5},{2,6},{3,7},{4,0},{5,1},{6,2},{7,3},{8,12},{9,13},{10,... | collective-permute-start | bytes 1572872 | tf_op jit(solution)/shard_map/ppermute | solution.py:238
  26.3 0.5 collective-permute-start.7
  26.8 6.7 %grad_blocks.3 = (bf16[512,512]{1,0:T(8,128)(2,1)}, bf16[512,512]{1,0:T(8,128)(2,1)}, bf16[512,256]{1,0:T(8,128)(2,1)}, bf16[512,256]{1,0:T(8,128)(2,1)}, bf16[5...) custom-call(s32[2]{0:T(128)} %pad_add_fusion.info_ref, bf16[512,2048]{1,0:T(8,128)(2,1)} %context_ref, ...), custom_call_target="tpu_custom_call" | custom-call | flops 2147483648 | tf_op jit(solution)/shard_map/grad_blocks/pallas_call | solution.py:116
  33.5 1.2 %add_convert_fusion.1 = bf16[512,512]{1,0:T(8,128)(2,1)S(1)} fusion(bf16[512,512]{1,0:T(8,128)(2,1)S(1)} %collective-permute-done.5, bf16[512,512]{1,0:T(8,128)(2,1)} %get-tuple-element.64), kind=kLoop, calls=%fused_computation.7 | loop fusion | flops 1048576 | bytes 1572864 | tf_op jit(solution)/shard_map/convert_element_type | solution.py:53
  34.8 0.6 collective-permute-start.11
  35.4 0.1 add_convert_fusion
  35.5 1.6 %collective-permute-start.10 = (bf16[256,512]{1,0:T(8,128)(2,1)S(1)}, bf16[256,512]{1,0:T(8,128)(2,1)S(1)}, u32[]{:S(2)}, u32[]{:S(2)}) collective-permute-start(bf16[256,512]{1,0:T(8,128)(2,1)S(1)} %slice.107), channel_id=1, source_target_pairs={{0,2},{1,3},{2,0},{3,1},{4,6},{5,7},{6,4},{7,5},{8,10},{9,11},{10,... | collective-permute-start | bytes 786440 | tf_op jit(solution)/shard_map/ppermute | solution.py:238
  37.1 7.6 %collective-permute-done.6.rest_3_ = bf16[256,1024]{1,0:T(8,128)(2,1)} collective-permute-done((bf16[256,1024]{1,0:T(8,128)(2,1)}, bf16[256,1024]{1,0:T(8,128)(2,1)}, u32[]{:S(2)}, u32[]{:S(2)}) %collective-permute-start.6) | collective-permute-done | bytes 524320 | tf_op jit(solution)/shard_map/ppermute | solution.py:238
  44.7 1.5 %collective-permute-start.8 = (bf16[512,256]{1,0:T(8,128)(2,1)}, bf16[512,256]{1,0:T(8,128)(2,1)S(1)}, u32[]{:S(2)}, u32[]{:S(2)}) collective-permute-start(bf16[512,256]{1,0:T(8,128)(2,1)} %get-tuple-element.71), channel_id=1, source_target_pairs={{0,4},{1,5},{2,6},{3,7},{4,0},{5,1},{6,2},{7,3},{8,12},{9,13},{10,... | collective-permute-start | bytes 786440 | tf_op jit(solution)/shard_map/ppermute | solution.py:238
  46.3 0.5 collective-permute-start.9
  46.8 3.4 %collective-permute-done.11 = bf16[256,512]{1,0:T(8,128)(2,1)S(1)} collective-permute-done((bf16[256,512]{1,0:T(8,128)(2,1)S(1)}, bf16[256,512]{1,0:T(8,128)(2,1)S(1)}, u32[]{:S(2)}, u32[]{:S(2)}) %collective-permute-start.11) | collective-permute-done | bytes 262176 | tf_op jit(solution)/shard_map/ppermute | solution.py:238
  50.2 0.1 add_convert_fusion.9
  50.3 0.1 add_convert_fusion.8
  50.4 1.6 %collective-permute-start.15 = (bf16[128,1024]{1,0:T(8,128)(2,1)S(1)}, bf16[128,1024]{1,0:T(8,128)(2,1)S(1)}, u32[]{:S(2)}, u32[]{:S(2)}) collective-permute-start(bf16[128,1024]{1,0:T(8,128)(2,1)S(1)} %pad_maximum_fusion.3), channel_id=1, source_target_pairs={{0,8},{8,0},{16,24},{24,16},{1,9},{9,1},{17,25},{25,17},{2,10},{10... | collective-permute-start | bytes 786440 | tf_op jit(solution)/shard_map/ppermute | solution.py:241
  52.1 10.0 %products.2 = (bf16[512,2048]{1,0:T(8,128)(2,1)}, bf16[512,1024]{1,0:T(8,128)(2,1)}) custom-call(s32[2]{0:T(128)} %pad_add_fusion.info_ref, bf16[512,2048]{1,0:T(8,128)(2,1)} %copy-done.1, bf16[512,2048]{1,0:T(8,128)(2,1)} %collective-permute-done.2.t1.cotangent_ref, bf16[256,2048]{1,0:T(8,128)(2,1)} %copy-done.2, bf16[512,1024]{1,0:T(8,128)(2,1)} %copy-done.12, ...), custom_call_target="tpu_custom_call" | custom-call | flops 4294967296 | tf_op jit(solution)/shard_map/products/pallas_call | solution.py:179
  62.1 0.1 add_convert_fusion.7
  62.3 0.1 add_convert_fusion.6
  62.4 1.3 %copy-done.13 = bf16[512,2048]{1,0:T(8,128)(2,1)S(1)} copy-done((bf16[512,2048]{1,0:T(8,128)(2,1)S(1)}, bf16[512,2048]{1,0:T(8,128)(2,1)}, u32[]{:S(2)}) %copy-start.13) | copy-done | bytes 2097176
  63.7 1.0 collective-permute-start.13
  64.7 1.0 collective-permute-start.14
  65.8 1.0 collective-permute-start.17
  66.8 1.0 collective-permute-start.18
  67.8 0.1 add_convert_fusion.5
  67.8 3.2 %collective-permute-done.14 = bf16[256,256]{1,0:T(8,128)(2,1)S(1)} collective-permute-done((bf16[256,256]{1,0:T(8,128)(2,1)S(1)}, bf16[256,256]{1,0:T(8,128)(2,1)S(1)}, u32[]{:S(2)}, u32[]{:S(2)}) %collective-permute-start.14) | collective-permute-done | bytes 131104 | tf_op jit(solution)/shard_map/ppermute | solution.py:238
  71.1 2.6 %collective-permute-start.21 = (bf16[128,1024]{1,0:T(8,128)(2,1)S(1)}, bf16[128,1024]{1,0:T(8,128)(2,1)S(1)}, u32[]{:S(2)}, u32[]{:S(2)}) collective-permute-start(bf16[128,1024]{1,0:T(8,128)(2,1)S(1)} %add_convert_fusion.5), channel_id=1, source_target_pairs={{0,16},{8,24},{16,0},{24,8},{1,17},{9,25},{17,1},{25,9},{2,18},{10... | collective-permute-start | bytes 786440 | tf_op jit(solution)/shard_map/ppermute | solution.py:241
  73.7 0.1 collective-permute-start.23
  73.8 10.9 %products.3 = (f32[512,2048]{1,0:T(8,128)}, bf16[512,1024]{1,0:T(8,128)(2,1)}) custom-call(s32[2]{0:T(128)} %pad_add_fusion.info_ref, bf16[512,2048]{1,0:T(8,128)(2,1)} %context_ref, bf16[512,2048]{1,0:T(8,128)(2,1)} %cotangent_ref.1, bf16[256,2048]{1,0:T(8,128)(2,1)} %copy-done.2, bf16[512,1024]{1,0:T(8,128)(2,1)} %copy-done.12, ...), custom_call_target="tpu_custom_call" | custom-call | flops 4294967296 | tf_op jit(solution)/shard_map/products/pallas_call | solution.py:179
  84.8 0.5 collective-permute-start.16
  85.3 0.1 add_convert_fusion.4
  85.4 0.1 add_convert_fusion.3
  85.5 1.1 collective-permute-start.19
  86.6 1.5 %collective-permute-start.20 = (bf16[256,256]{1,0:T(8,128)(2,1)S(1)}, bf16[256,256]{1,0:T(8,128)(2,1)S(1)}, u32[]{:S(2)}, u32[]{:S(2)}) collective-permute-start(bf16[256,256]{1,0:T(8,128)(2,1)S(1)} %slice.121), channel_id=1, source_target_pairs={{0,4},{1,5},{2,6},{3,7},{4,0},{5,1},{6,2},{7,3},{8,12},{9,13},{10,... | collective-permute-start | bytes 393224 | tf_op jit(solution)/shard_map/ppermute | solution.py:238
  88.1 0.1 add_convert_fusion.2
  88.2 3.7 %collective-permute-done.20 = bf16[256,256]{1,0:T(8,128)(2,1)S(1)} collective-permute-done((bf16[256,256]{1,0:T(8,128)(2,1)S(1)}, bf16[256,256]{1,0:T(8,128)(2,1)S(1)}, u32[]{:S(2)}, u32[]{:S(2)}) %collective-permute-start.20) | collective-permute-done | bytes 131104 | tf_op jit(solution)/shard_map/ppermute | solution.py:238
  91.9 1.6 %collective-permute-start.24 = (bf16[128,1024]{1,0:T(8,128)(2,1)S(1)}, bf16[128,1024]{1,0:T(8,128)(2,1)S(1)}, u32[]{:S(2)}, u32[]{:S(2)}) collective-permute-start(bf16[128,1024]{1,0:T(8,128)(2,1)S(1)} %add_convert_fusion.2), channel_id=1, source_target_pairs={{0,8},{8,0},{16,24},{24,16},{1,9},{9,1},{17,25},{25,17},{2,10},{10... | collective-permute-start | bytes 786440 | tf_op jit(solution)/shard_map/ppermute | solution.py:241
  93.6 0.5 collective-permute-start.26
  94.2 0.4 collective-permute-start.25
  94.6 1.0 copy-done.6
  95.5 0.7 copy-done.5
  96.2 6.1 %joined.1 = (bf16[512,2048]{1,0:T(8,128)(2,1)}, bf16[512,2048]{1,0:T(8,128)(2,1)}) custom-call(s32[2]{0:T(128)} %pad_add_fusion.info_ref, f32[512,2048]{1,0:T(8,128)} %get-tuple-element.96.own_ref, bf16[512,2048]{1,0:T(8,128)(2,1)} %copy-done.5, bf16[512,1024]{1,0:T(8,128)(2,1)} %get-tuple-element.97.own_columns_ref, bf16[512,1024]{1,0:T(8,128)(2,1)} %copy-done.6), custom_call_target="tpu_custom_call" | custom-call | flops 1048576 | tf_op jit(solution)/shard_map/joined/pallas_call | solution.py:209
  102.3 2.5 %collective-permute-done.26 = bf16[128,512]{1,0:T(8,128)(2,1)S(1)} collective-permute-done((bf16[128,512]{1,0:T(8,128)(2,1)S(1)}, bf16[128,512]{1,0:T(8,128)(2,1)S(1)}, u32[]{:S(2)}, u32[]{:S(2)}) %collective-permute-start.26) | collective-permute-done | bytes 131104 | tf_op jit(solution)/shard_map/ppermute | solution.py:241
  104.8 0.2 collective-permute-start.28
  105.1 1.9 %collective-permute-start.27 = (bf16[128,512]{1,0:T(8,128)(2,1)S(1)}, bf16[128,512]{1,0:T(8,128)(2,1)S(1)}, u32[]{:S(2)}, u32[]{:S(2)}) collective-permute-start(bf16[128,512]{1,0:T(8,128)(2,1)S(1)} %add_convert_fusion.11), channel_id=1, source_target_pairs={{0,8},{8,0},{16,24},{24,16},{1,9},{9,1},{17,25},{25,17},{2,10},{10... | collective-permute-start | bytes 393224 | tf_op jit(solution)/shard_map/ppermute | solution.py:241
  106.9 5.2 %collective-permute-done.28 = bf16[128,512]{1,0:T(8,128)(2,1)S(1)} collective-permute-done((bf16[128,512]{1,0:T(8,128)(2,1)S(1)}, bf16[128,512]{1,0:T(8,128)(2,1)S(1)}, u32[]{:S(2)}, u32[]{:S(2)}) %collective-permute-start.28) | collective-permute-done | bytes 131104 | tf_op jit(solution)/shard_map/ppermute | solution.py:241
  112.1 0.1 collective-permute-start.29
  112.3 4.9 %collective-permute-done.29 = bf16[128,512]{1,0:T(8,128)(2,1)S(1)} collective-permute-done((bf16[128,512]{1,0:T(8,128)(2,1)S(1)}, bf16[128,512]{1,0:T(8,128)(2,1)S(1)}, u32[]{:S(2)}, u32[]{:S(2)}) %collective-permute-start.29) | collective-permute-done | bytes 131104 | tf_op jit(solution)/shard_map/ppermute | solution.py:241
  117.2 0.1 constant_dynamic-slice_fusion.1
  117.4 3.9 %multiply_subtract_fusion = (f32[256,2048]{1,0:T(8,128)}, f32[256,2048]{1,0:T(8,128)}, f32[256,2048]{1,0:T(8,128)}) fusion(f32[256,2048]{1,0:T(8,128)S(1)} %copy-done, bf16[128,2048]{1,0:T(8,128)(2,1)S(1)} %get-tuple-element.111, bf16[128,2048]{1,0:T(8,128)(2,1)S(1)} %get-tuple-element.110, f32[256,2048]{1,0:T(8,128)S(1)} %copy-done.3, ...), kind=kLoop, calls=%fused_computation.4 | loop fusion | flops 9961472 | bytes 13631488 | tf_op jit(solution)/shard_map/sub | solution.py:17
  (71 shorter events, 0.6 us)
Async XLA Ops:
  0.6 8.5 %collective-permute-start = (bf16[512,2048]{1,0:T(8,128)(2,1)}, bf16[512,2048]{1,0:T(8,128)(2,1)S(1)}, u32[]{:S(2)}, u32[]{:S(2)}) collective-permute-start(bf16[512,2048]{1,0:T(8,128)(2,1)} %context_ref), channel_id=1, source_target_pairs={{0,1},{1,0},{2,3},{3,2},{4,5},{5,4},{6,7},{7,6},{8,9},{9,8},{10,11... | collective-permute-start | bytes 6291464 | tf_op jit(solution)/shard_map/ppermute | solution.py:238
  1.1 8.0 %collective-permute-start.2 = (bf16[512,2048]{1,0:T(8,128)(2,1)}, bf16[512,2048]{1,0:T(8,128)(2,1)}, u32[]{:S(2)}, u32[]{:S(2)}) collective-permute-start(bf16[512,2048]{1,0:T(8,128)(2,1)} %cotangent_ref.1), channel_id=1, source_target_pairs={{0,1},{1,0},{2,3},{3,2},{4,5},{5,4},{6,7},{7,6},{8,9},{9,8},{10,11... | collective-permute-start | bytes 6291464 | tf_op jit(solution)/shard_map/ppermute | solution.py:238
  3.0 14.3 %copy-start.2 = (bf16[256,2048]{1,0:T(8,128)(2,1)}, bf16[256,2048]{1,0:T(8,128)(2,1)S(1)}, u32[]{:S(2)}) copy-start(bf16[256,2048]{1,0:T(8,128)(2,1)S(1)} %convert_element_type.168.rest_0_) | copy-start | bytes 3145732
  4.1 15.8 %collective-permute-start.1 = (bf16[256,1024]{1,0:T(8,128)(2,1)}, bf16[256,1024]{1,0:T(8,128)(2,1)}, u32[]{:S(2)}, u32[]{:S(2)}) collective-permute-start(bf16[256,1024]{1,0:T(8,128)(2,1)} %get-tuple-element.113), channel_id=1, source_target_pairs={{0,2},{1,3},{2,0},{3,1},{4,6},{5,7},{6,4},{7,5},{8,10},{9,11},{10,... | collective-permute-start | bytes 1572872 | tf_op jit(solution)/shard_map/ppermute | solution.py:238
  7.0 13.9 %collective-permute-start.3 = (bf16[256,1024]{1,0:T(8,128)(2,1)}, bf16[256,1024]{1,0:T(8,128)(2,1)}, u32[]{:S(2)}, u32[]{:S(2)}) collective-permute-start(bf16[256,1024]{1,0:T(8,128)(2,1)} %get-tuple-element.112), channel_id=1, source_target_pairs={{0,4},{1,5},{2,6},{3,7},{4,0},{5,1},{6,2},{7,3},{8,12},{9,13},{10,... | collective-permute-start | bytes 1572872 | tf_op jit(solution)/shard_map/ppermute | solution.py:238
  9.1 1.3 %copy-start.1 = (bf16[512,2048]{1,0:T(8,128)(2,1)}, bf16[512,2048]{1,0:T(8,128)(2,1)S(1)}, u32[]{:S(2)}) copy-start(bf16[512,2048]{1,0:T(8,128)(2,1)S(1)} %collective-permute-done.c1.context_ref) | copy-start | bytes 6291460
  17.3 16.2 %collective-permute-start.5 = (bf16[512,512]{1,0:T(8,128)(2,1)}, bf16[512,512]{1,0:T(8,128)(2,1)S(1)}, u32[]{:S(2)}, u32[]{:S(2)}) collective-permute-start(bf16[512,512]{1,0:T(8,128)(2,1)} %get-tuple-element.65), channel_id=1, source_target_pairs={{0,2},{1,3},{2,0},{3,1},{4,6},{5,7},{6,4},{7,5},{8,10},{9,11},{10,... | collective-permute-start | bytes 1572872 | tf_op jit(solution)/shard_map/ppermute | solution.py:238
  18.4 16.4 %collective-permute-start.4 = (bf16[512,512]{1,0:T(8,128)(2,1)}, bf16[512,512]{1,0:T(8,128)(2,1)S(1)}, u32[]{:S(2)}, u32[]{:S(2)}) collective-permute-start(bf16[512,512]{1,0:T(8,128)(2,1)} %get-tuple-element.63), channel_id=1, source_target_pairs={{0,4},{1,5},{2,6},{3,7},{4,0},{5,1},{6,2},{7,3},{8,12},{9,13},{10,... | collective-permute-start | bytes 1572872 | tf_op jit(solution)/shard_map/ppermute | solution.py:238
  23.1 10.4 %copy-start.12 = (bf16[512,1024]{1,0:T(8,128)(2,1)}, bf16[512,1024]{1,0:T(8,128)(2,1)S(1)}, u32[]{:S(2)}) copy-start(bf16[512,1024]{1,0:T(8,128)(2,1)S(1)} %constant_dynamic-update-slice_fusion.rest_1_) | copy-start | bytes 3145732
  23.1 29.0 %collective-permute-start.12 = (bf16[512,1024]{1,0:T(8,128)(2,1)S(1)}, bf16[512,1024]{1,0:T(8,128)(2,1)}, u32[]{:S(2)}, u32[]{:S(2)}) collective-permute-start(bf16[512,1024]{1,0:T(8,128)(2,1)S(1)} %constant_dynamic-update-slice_fusion.rest_1_), channel_id=1, source_target_pairs={{0,8},{8,0},{16,24},{24,16},{1,9},{9,1},{17,25},{25,17},{2,10},{10... | collective-permute-start | bytes 3145736 | tf_op jit(solution)/shard_map/ppermute | solution.py:241
  24.8 20.0 %collective-permute-start.6 = (bf16[256,1024]{1,0:T(8,128)(2,1)}, bf16[256,1024]{1,0:T(8,128)(2,1)}, u32[]{:S(2)}, u32[]{:S(2)}) collective-permute-start(bf16[256,1024]{1,0:T(8,128)(2,1)} %collective-permute-done.1), channel_id=1, source_target_pairs={{0,4},{1,5},{2,6},{3,7},{4,0},{5,1},{6,2},{7,3},{8,12},{9,13},{10,... | collective-permute-start | bytes 1572872 | tf_op jit(solution)/shard_map/ppermute | solution.py:238
  26.3 18.5 %collective-permute-start.7 = (bf16[256,1024]{1,0:T(8,128)(2,1)}, bf16[256,1024]{1,0:T(8,128)(2,1)}, u32[]{:S(2)}, u32[]{:S(2)}) collective-permute-start(bf16[256,1024]{1,0:T(8,128)(2,1)} %collective-permute-done.3), channel_id=1, source_target_pairs={{0,2},{1,3},{2,0},{3,1},{4,6},{5,7},{6,4},{7,5},{8,10},{9,11},{10,... | collective-permute-start | bytes 1572872 | tf_op jit(solution)/shard_map/ppermute | solution.py:238
  33.5 1.9 %copy-start.7 = (bf16[512,512]{1,0:T(8,128)(2,1)S(1)}, bf16[512,512]{1,0:T(8,128)(2,1)}, u32[]{:S(2)}) copy-start(bf16[512,512]{1,0:T(8,128)(2,1)} %get-tuple-element.62) | copy-start | bytes 1572868
  34.8 15.4 %collective-permute-start.11 = (bf16[256,512]{1,0:T(8,128)(2,1)S(1)}, bf16[256,512]{1,0:T(8,128)(2,1)S(1)}, u32[]{:S(2)}, u32[]{:S(2)}) collective-permute-start(bf16[256,512]{1,0:T(8,128)(2,1)S(1)} %slice.109), channel_id=1, source_target_pairs={{0,4},{1,5},{2,6},{3,7},{4,0},{5,1},{6,2},{7,3},{8,12},{9,13},{10,... | collective-permute-start | bytes 786440 | tf_op jit(solution)/shard_map/ppermute | solution.py:238
  35.5 14.8 %collective-permute-start.10 = (bf16[256,512]{1,0:T(8,128)(2,1)S(1)}, bf16[256,512]{1,0:T(8,128)(2,1)S(1)}, u32[]{:S(2)}, u32[]{:S(2)}) collective-permute-start(bf16[256,512]{1,0:T(8,128)(2,1)S(1)} %slice.107), channel_id=1, source_target_pairs={{0,2},{1,3},{2,0},{3,1},{4,6},{5,7},{6,4},{7,5},{8,10},{9,11},{10,... | collective-permute-start | bytes 786440 | tf_op jit(solution)/shard_map/ppermute | solution.py:238
  44.7 17.5 %collective-permute-start.8 = (bf16[512,256]{1,0:T(8,128)(2,1)}, bf16[512,256]{1,0:T(8,128)(2,1)S(1)}, u32[]{:S(2)}, u32[]{:S(2)}) collective-permute-start(bf16[512,256]{1,0:T(8,128)(2,1)} %get-tuple-element.71), channel_id=1, source_target_pairs={{0,4},{1,5},{2,6},{3,7},{4,0},{5,1},{6,2},{7,3},{8,12},{9,13},{10,... | collective-permute-start | bytes 786440 | tf_op jit(solution)/shard_map/ppermute | solution.py:238
  46.3 15.9 %collective-permute-start.9 = (bf16[512,256]{1,0:T(8,128)(2,1)}, bf16[512,256]{1,0:T(8,128)(2,1)S(1)}, u32[]{:S(2)}, u32[]{:S(2)}) collective-permute-start(bf16[512,256]{1,0:T(8,128)(2,1)} %get-tuple-element.74), channel_id=1, source_target_pairs={{0,2},{1,3},{2,0},{3,1},{4,6},{5,7},{6,4},{7,5},{8,10},{9,11},{10,... | collective-permute-start | bytes 786440 | tf_op jit(solution)/shard_map/ppermute | solution.py:238
  50.4 11.7 %copy-start.11 = (bf16[512,256]{1,0:T(8,128)(2,1)S(1)}, bf16[512,256]{1,0:T(8,128)(2,1)}, u32[]{:S(2)}) copy-start(bf16[512,256]{1,0:T(8,128)(2,1)} %get-tuple-element.72) | copy-start | bytes 786436
  50.4 11.8 %copy-start.10 = (bf16[512,256]{1,0:T(8,128)(2,1)S(1)}, bf16[512,256]{1,0:T(8,128)(2,1)}, u32[]{:S(2)}) copy-start(bf16[512,256]{1,0:T(8,128)(2,1)} %get-tuple-element.60) | copy-start | bytes 786436
  50.4 15.3 %collective-permute-start.15 = (bf16[128,1024]{1,0:T(8,128)(2,1)S(1)}, bf16[128,1024]{1,0:T(8,128)(2,1)S(1)}, u32[]{:S(2)}, u32[]{:S(2)}) collective-permute-start(bf16[128,1024]{1,0:T(8,128)(2,1)S(1)} %pad_maximum_fusion.3), channel_id=1, source_target_pairs={{0,8},{8,0},{16,24},{24,16},{1,9},{9,1},{17,25},{25,17},{2,10},{10... | collective-permute-start | bytes 786440 | tf_op jit(solution)/shard_map/ppermute | solution.py:241
  62.1 1.6 %copy-start.13 = (bf16[512,2048]{1,0:T(8,128)(2,1)S(1)}, bf16[512,2048]{1,0:T(8,128)(2,1)}, u32[]{:S(2)}) copy-start(bf16[512,2048]{1,0:T(8,128)(2,1)} %get-tuple-element.78) | copy-start | bytes 6291460
  62.1 11.6 %copy-start.14 = (bf16[512,1024]{1,0:T(8,128)(2,1)S(1)}, bf16[512,1024]{1,0:T(8,128)(2,1)}, u32[]{:S(2)}) copy-start(bf16[512,1024]{1,0:T(8,128)(2,1)} %get-tuple-element.98) | copy-start | bytes 3145732
  63.7 30.9 %collective-permute-start.22 = (bf16[512,2048]{1,0:T(8,128)(2,1)S(1)}, bf16[512,2048]{1,0:T(8,128)(2,1)S(1)}, u32[]{:S(2)}, u32[]{:S(2)}) collective-permute-start(bf16[512,2048]{1,0:T(8,128)(2,1)S(1)} %copy-done.13), channel_id=1, source_target_pairs={{0,1},{1,0},{2,3},{3,2},{4,5},{5,4},{6,7},{7,6},{8,9},{9,8},{10,11... | collective-permute-start | bytes 6291464 | tf_op jit(solution)/shard_map/ppermute | solution.py:238
  63.7 10.0 %collective-permute-start.13 = (bf16[256,256]{1,0:T(8,128)(2,1)S(1)}, bf16[256,256]{1,0:T(8,128)(2,1)S(1)}, u32[]{:S(2)}, u32[]{:S(2)}) collective-permute-start(bf16[256,256]{1,0:T(8,128)(2,1)S(1)} %slice.111), channel_id=1, source_target_pairs={{0,2},{1,3},{2,0},{3,1},{4,6},{5,7},{6,4},{7,5},{8,10},{9,11},{10,... | collective-permute-start | bytes 393224 | tf_op jit(solution)/shard_map/ppermute | solution.py:238
  64.7 6.3 %collective-permute-start.14 = (bf16[256,256]{1,0:T(8,128)(2,1)S(1)}, bf16[256,256]{1,0:T(8,128)(2,1)S(1)}, u32[]{:S(2)}, u32[]{:S(2)}) collective-permute-start(bf16[256,256]{1,0:T(8,128)(2,1)S(1)} %slice.113), channel_id=1, source_target_pairs={{0,4},{1,5},{2,6},{3,7},{4,0},{5,1},{6,2},{7,3},{8,12},{9,13},{10,... | collective-permute-start | bytes 393224 | tf_op jit(solution)/shard_map/ppermute | solution.py:238
  65.8 19.6 %collective-permute-start.17 = (bf16[512,256]{1,0:T(8,128)(2,1)}, bf16[512,256]{1,0:T(8,128)(2,1)S(1)}, u32[]{:S(2)}, u32[]{:S(2)}) collective-permute-start(bf16[512,256]{1,0:T(8,128)(2,1)} %get-tuple-element.86), channel_id=1, source_target_pairs={{0,4},{1,5},{2,6},{3,7},{4,0},{5,1},{6,2},{7,3},{8,12},{9,13},{10,... | collective-permute-start | bytes 786440 | tf_op jit(solution)/shard_map/ppermute | solution.py:238
  66.8 18.0 %collective-permute-start.18 = (bf16[512,256]{1,0:T(8,128)(2,1)}, bf16[512,256]{1,0:T(8,128)(2,1)S(1)}, u32[]{:S(2)}, u32[]{:S(2)}) collective-permute-start(bf16[512,256]{1,0:T(8,128)(2,1)} %get-tuple-element.89), channel_id=1, source_target_pairs={{0,2},{1,3},{2,0},{3,1},{4,6},{5,7},{6,4},{7,5},{8,10},{9,11},{10,... | collective-permute-start | bytes 786440 | tf_op jit(solution)/shard_map/ppermute | solution.py:238
  71.1 15.5 %collective-permute-start.21 = (bf16[128,1024]{1,0:T(8,128)(2,1)S(1)}, bf16[128,1024]{1,0:T(8,128)(2,1)S(1)}, u32[]{:S(2)}, u32[]{:S(2)}) collective-permute-start(bf16[128,1024]{1,0:T(8,128)(2,1)S(1)} %add_convert_fusion.5), channel_id=1, source_target_pairs={{0,16},{8,24},{16,0},{24,8},{1,17},{9,25},{17,1},{25,9},{2,18},{10... | collective-permute-start | bytes 786440 | tf_op jit(solution)/shard_map/ppermute | solution.py:241
  73.7 20.9 %collective-permute-start.23 = (bf16[512,1024]{1,0:T(8,128)(2,1)S(1)}, bf16[512,1024]{1,0:T(8,128)(2,1)S(1)}, u32[]{:S(2)}, u32[]{:S(2)}) collective-permute-start(bf16[512,1024]{1,0:T(8,128)(2,1)S(1)} %copy-done.14), channel_id=1, source_target_pairs={{0,1},{1,0},{2,3},{3,2},{4,5},{5,4},{6,7},{7,6},{8,9},{9,8},{10,11... | collective-permute-start | bytes 3145736 | tf_op jit(solution)/shard_map/ppermute | solution.py:238
  73.8 11.5 %copy-start.9 = (bf16[512,256]{1,0:T(8,128)(2,1)S(1)}, bf16[512,256]{1,0:T(8,128)(2,1)}, u32[]{:S(2)}) copy-start(bf16[512,256]{1,0:T(8,128)(2,1)} %get-tuple-element.87) | copy-start | bytes 786436
  73.8 11.6 %copy-start.8 = (bf16[512,256]{1,0:T(8,128)(2,1)S(1)}, bf16[512,256]{1,0:T(8,128)(2,1)}, u32[]{:S(2)}) copy-start(bf16[512,256]{1,0:T(8,128)(2,1)} %get-tuple-element.66) | copy-start | bytes 786436
  84.8 8.8 %collective-permute-start.16 = (bf16[128,512]{1,0:T(8,128)(2,1)S(1)}, bf16[128,512]{1,0:T(8,128)(2,1)S(1)}, u32[]{:S(2)}, u32[]{:S(2)}) collective-permute-start(bf16[128,512]{1,0:T(8,128)(2,1)S(1)} %pad_maximum_fusion.6), channel_id=1, source_target_pairs={{0,8},{8,0},{16,24},{24,16},{1,9},{9,1},{17,25},{25,17},{2,10},{10... | collective-permute-start | bytes 393224 | tf_op jit(solution)/shard_map/ppermute | solution.py:241
  85.5 8.0 %collective-permute-start.19 = (bf16[256,256]{1,0:T(8,128)(2,1)S(1)}, bf16[256,256]{1,0:T(8,128)(2,1)S(1)}, u32[]{:S(2)}, u32[]{:S(2)}) collective-permute-start(bf16[256,256]{1,0:T(8,128)(2,1)S(1)} %slice.119), channel_id=1, source_target_pairs={{0,2},{1,3},{2,0},{3,1},{4,6},{5,7},{6,4},{7,5},{8,10},{9,11},{10,... | collective-permute-start | bytes 393224 | tf_op jit(solution)/shard_map/ppermute | solution.py:238
  86.6 5.3 %collective-permute-start.20 = (bf16[256,256]{1,0:T(8,128)(2,1)S(1)}, bf16[256,256]{1,0:T(8,128)(2,1)S(1)}, u32[]{:S(2)}, u32[]{:S(2)}) collective-permute-start(bf16[256,256]{1,0:T(8,128)(2,1)S(1)} %slice.121), channel_id=1, source_target_pairs={{0,4},{1,5},{2,6},{3,7},{4,0},{5,1},{6,2},{7,3},{8,12},{9,13},{10,... | collective-permute-start | bytes 393224 | tf_op jit(solution)/shard_map/ppermute | solution.py:238
  91.9 15.0 %collective-permute-start.24 = (bf16[128,1024]{1,0:T(8,128)(2,1)S(1)}, bf16[128,1024]{1,0:T(8,128)(2,1)S(1)}, u32[]{:S(2)}, u32[]{:S(2)}) collective-permute-start(bf16[128,1024]{1,0:T(8,128)(2,1)S(1)} %add_convert_fusion.2), channel_id=1, source_target_pairs={{0,8},{8,0},{16,24},{24,16},{1,9},{9,1},{17,25},{25,17},{2,10},{10... | collective-permute-start | bytes 786440 | tf_op jit(solution)/shard_map/ppermute | solution.py:241
  93.6 11.2 %collective-permute-start.26 = (bf16[128,512]{1,0:T(8,128)(2,1)S(1)}, bf16[128,512]{1,0:T(8,128)(2,1)S(1)}, u32[]{:S(2)}, u32[]{:S(2)}) collective-permute-start(bf16[128,512]{1,0:T(8,128)(2,1)S(1)} %pad_maximum_fusion.5), channel_id=1, source_target_pairs={{0,8},{8,0},{16,24},{24,16},{1,9},{9,1},{17,25},{25,17},{2,10},{10... | collective-permute-start | bytes 393224 | tf_op jit(solution)/shard_map/ppermute | solution.py:241
  94.2 10.9 %collective-permute-start.25 = (bf16[128,512]{1,0:T(8,128)(2,1)S(1)}, bf16[128,512]{1,0:T(8,128)(2,1)S(1)}, u32[]{:S(2)}, u32[]{:S(2)}) collective-permute-start(bf16[128,512]{1,0:T(8,128)(2,1)S(1)} %add_convert_fusion.13), channel_id=1, source_target_pairs={{0,16},{8,24},{16,0},{24,8},{1,17},{9,25},{17,1},{25,9},{2,18},{10... | collective-permute-start | bytes 393224 | tf_op jit(solution)/shard_map/ppermute | solution.py:241
  94.6 1.0 copy-start.6
  94.6 1.7 %copy-start.5 = (bf16[512,2048]{1,0:T(8,128)(2,1)}, bf16[512,2048]{1,0:T(8,128)(2,1)S(1)}, u32[]{:S(2)}) copy-start(bf16[512,2048]{1,0:T(8,128)(2,1)S(1)} %collective-permute-done.22.got_ref) | copy-start | bytes 6291460
  104.8 12.6 %copy-start.4 = (f32[256,2048]{1,0:T(8,128)S(1)}, f32[256,2048]{1,0:T(8,128)}, u32[]{:S(2)}) copy-start(f32[256,2048]{1,0:T(8,128)} %param.9) | copy-start | bytes 6291460
  104.8 7.3 %collective-permute-start.28 = (bf16[128,512]{1,0:T(8,128)(2,1)S(1)}, bf16[128,512]{1,0:T(8,128)(2,1)S(1)}, u32[]{:S(2)}, u32[]{:S(2)}) collective-permute-start(bf16[128,512]{1,0:T(8,128)(2,1)S(1)} %add_convert_fusion.12), channel_id=1, source_target_pairs={{0,16},{8,24},{16,0},{24,8},{1,17},{9,25},{17,1},{25,9},{2,18},{10... | collective-permute-start | bytes 393224 | tf_op jit(solution)/shard_map/ppermute | solution.py:241
  105.1 7.2 %collective-permute-start.27 = (bf16[128,512]{1,0:T(8,128)(2,1)S(1)}, bf16[128,512]{1,0:T(8,128)(2,1)S(1)}, u32[]{:S(2)}, u32[]{:S(2)}) collective-permute-start(bf16[128,512]{1,0:T(8,128)(2,1)S(1)} %add_convert_fusion.11), channel_id=1, source_target_pairs={{0,8},{8,0},{16,24},{24,16},{1,9},{9,1},{17,25},{25,17},{2,10},{10... | collective-permute-start | bytes 393224 | tf_op jit(solution)/shard_map/ppermute | solution.py:241
  112.1 5.0 %collective-permute-start.29 = (bf16[128,512]{1,0:T(8,128)(2,1)S(1)}, bf16[128,512]{1,0:T(8,128)(2,1)S(1)}, u32[]{:S(2)}, u32[]{:S(2)}) collective-permute-start(bf16[128,512]{1,0:T(8,128)(2,1)S(1)} %add_convert_fusion.10), channel_id=1, source_target_pairs={{0,8},{8,0},{16,24},{24,16},{1,9},{9,1},{17,25},{25,17},{2,10},{10... | collective-permute-start | bytes 393224 | tf_op jit(solution)/shard_map/ppermute | solution.py:241
  112.3 5.1 %copy-start.3 = (f32[256,2048]{1,0:T(8,128)S(1)}, f32[256,2048]{1,0:T(8,128)}, u32[]{:S(2)}) copy-start(f32[256,2048]{1,0:T(8,128)} %param.8) | copy-start | bytes 6291460
  112.3 5.1 %copy-start = (f32[256,2048]{1,0:T(8,128)S(1)}, f32[256,2048]{1,0:T(8,128)}, u32[]{:S(2)}) copy-start(f32[256,2048]{1,0:T(8,128)} %param.7) | copy-start | bytes 6291460

commit v2 on v1

--- a/solution.py
+++ b/solution.py
@@ -7,7 +7,7 @@
 
 first_fix = 0.99997343860111
 second_fix = 0.99407947078
-CHUNKS = (2, 1, 1)
+CHUNKS = (5, 3)
 
 
 def adamw(master, moment_one, moment_two, grad):
@@ -61,8 +61,8 @@
         out_specs=out_specs,
         scratch_shapes=list(scratch),
         input_output_aliases=aliases or {},
-        compiler_params=pltpu.CompilerParams(vmem_limit_bytes=56 * 2**20),
-        cost_estimate=pl.CostEstimate(flops=flops, bytes_accessed=0, transcendentals=0),
+        compiler_params=pltpu.CompilerParams(vmem_limit_bytes=24 * 2**20),
+        cost_estimate=pl.CostEstimate(flops=16 * flops, bytes_accessed=0, transcendentals=0),
         name=name,
     )
 
@@ -132,89 +132,190 @@
     return arrays, [[piece[2] is array for array in arrays].index(True) for piece in pieces]
 
 
-def run(copies):
+def started(pairs, sems, first=0):
+    copies = [pltpu.make_async_copy(a, b, sems.at[first + i]) for i, (a, b) in enumerate(pairs)]
     for copy in copies:
         copy.start()
+    return copies
+
+
+def wait(copies):
     for copy in copies:
         copy.wait()
 
 
-def weight_copies(info_ref, pieces, index, refs, blocks, weights, rows):
-    width = weights.shape[1]
-    copies = []
-    for (r, half, _, row), source in zip(pieces, index):
-        at = pl.ds(blocks.index(r) * rows, rows)
-        target = weights.at[at, :]
-        if half is not None:
-            lo = pl.multiple_of((lax.rem(info_ref[1], 2) ^ half) * (width // 2), width // 2)
-            target = weights.at[at, pl.ds(lo, width // 2)]
-        copies.append((refs[source].at[pl.ds(row, rows), :], target))
+def weight_copies(info_ref, pieces, index, refs, blocks, weights, rows, half):
+    size = weights.shape[1] // 2
+    lo = pl.multiple_of((lax.rem(info_ref[1], 2) ^ half) * size, size)
+    copies = {}
+    for (r, which, _, row), source in zip(pieces, index):
+        if which in (None, half):
+            origin = refs[source].at[pl.ds(row, rows), :]
+            if which is None:
+                origin = refs[source].at[pl.ds(row, rows), pl.ds(lo, size)]
+            copies[r] = (origin, weights.at[pl.ds(blocks.index(r) * rows, rows), pl.ds(half * size, size)])
     return copies
 
 
-def products(info, pieces, context, cotangent, rows, kind):
+def product(info, pieces, context, rows, got=None):
     tokens, width = context.shape
+    half = width // 2
     blocks = sorted({piece[0] for piece in pieces})
     depth = len(blocks) * rows
     arrays, index = sources(pieces)
-    tile = min(512, width)
-
-    def kernel(info_ref, context_ref, cotangent_ref, *rest):
+    more = [] if got is None else [got]
+    tile = min(512, half)
+    tiles = half // tile
+    reads = len(blocks)
+
+    def kernel(info_ref, context_ref, *rest):
         refs = rest[: len(arrays)]
-        product_ref, columns_ref, weights, chosen, in_sems = rest[len(arrays) :]
-        copies = weight_copies(info_ref, pieces, index, refs, blocks, weights, rows)
-        for i, r in enumerate(blocks):
-            copies.append((context_ref.at[:, aligned(info_ref[0] ^ r, rows)], chosen.at[:, pl.ds(i * rows, rows)]))
-        run([pltpu.make_async_copy(a, b, in_sems.at[i]) for i, (a, b) in enumerate(copies)])
-        columns_ref[...] = dot(cotangent_ref[...], weights[...], (1, 1)).astype(jnp.bfloat16)
-        for i in range(width // tile):
-            at = pl.ds(i * tile, tile)
-            product_ref[:, at] = dot(chosen[...], weights[:, at]).astype(kind)
-
-    scratch = [
-        pltpu.VMEM((depth, width), jnp.bfloat16),
-        pltpu.VMEM((tokens, depth), jnp.bfloat16),
-        pltpu.SemaphoreType.DMA((len(pieces) + len(blocks),)),
-    ]
+        got_refs = rest[len(arrays) : len(arrays) + len(more)]
+        out_ref, weights, chosen, result, in_sems, out_sems, *held = rest[len(arrays) + len(more) :]
+        columns = [
+            (context_ref.at[:, aligned(info_ref[0] ^ r, rows)], chosen.at[:, pl.ds(i * rows, rows)])
+            for i, r in enumerate(blocks)
+        ]
+        inward = [started(columns, in_sems)]
+        for side in range(2):
+            pairs = weight_copies(info_ref, pieces, index, refs, blocks, weights, rows, side)
+            inward.append(started([pairs[r] for r in blocks], in_sems, reads * (1 + side)))
+        adding = started(list(zip(got_refs, held)), in_sems, 3 * reads)
+        wait(inward[0])
+        outward = []
+        for side in range(2):
+            wait(inward[1 + side])
+            lo = (lax.rem(info_ref[1], 2) ^ side) * half
+            for i in range(tiles):
+                part = dot(chosen[...], weights[:, pl.ds(side * half + i * tile, tile)])
+                at = pl.ds(pl.multiple_of(lo + i * tile, tile), tile)
+                if more:
+                    wait(adding)
+                    adding = []
+                    part = part + held[0][:, at].astype(jnp.float32)
+                place = side * tiles + i
+                result[:, pl.ds(place * tile, tile)] = part.astype(jnp.bfloat16)
+                outward += started([(result.at[:, pl.ds(place * tile, tile)], out_ref.at[:, at])], out_sems, place)
+        wait(outward)
+
     return call(
         kernel,
-        "products",
-        4 * tokens * depth * width,
-        (jax.ShapeDtypeStruct((tokens, width), kind), jax.ShapeDtypeStruct((tokens, depth), jnp.bfloat16)),
-        [SMEM, ANY, VMEM] + [ANY] * len(arrays),
-        (VMEM, VMEM),
-        scratch,
-    )(info, context, cotangent, *arrays)
-
-
-def joined(info, own, got, own_columns, got_columns, blocks, rows):
-    tokens, width = own.shape
-    placed = [(r ^ core, core, i) for core in range(2) for i, r in enumerate(blocks)]
-
-    def kernel(info_ref, own_ref, got_ref, own_columns_ref, got_columns_ref, product_ref, out_ref, sems):
-        refs = (own_columns_ref, got_columns_ref)
-        copies = [
-            pltpu.make_async_copy(
-                refs[n].at[:, pl.ds(i * rows, rows)], out_ref.at[:, aligned(info_ref[0] ^ r, rows)], sems.at[place]
-            )
-            for place, (r, n, i) in enumerate(placed)
+        "product",
+        2 * tokens * depth * width,
+        jax.ShapeDtypeStruct((tokens, width), jnp.bfloat16),
+        [SMEM, ANY] + [ANY] * (len(arrays) + len(more)),
+        ANY,
+        [
+            pltpu.VMEM((depth, width), jnp.bfloat16),
+            pltpu.VMEM((tokens, depth), jnp.bfloat16),
+            pltpu.VMEM((tokens, width), jnp.bfloat16),
+            pltpu.SemaphoreType.DMA((3 * reads + 1,)),
+            pltpu.SemaphoreType.DMA((2 * tiles,)),
         ]
-        for copy in copies:
-            copy.start()
-        product_ref[...] = (own_ref[...] + got_ref[...].astype(jnp.float32)).astype(jnp.bfloat16)
-        for copy in copies:
-            copy.wait()
-
-    out = jax.ShapeDtypeStruct((tokens, width), jnp.bfloat16)
+        + [pltpu.VMEM((tokens, width), jnp.bfloat16)] * len(more),
+    )(info, context, *arrays, *more)
+
+
+def grad_columns(info, pieces, cotangent, rows, got=None):
+    tokens, width = cotangent.shape
+    half = width // 2
+    blocks = sorted({piece[0] for piece in pieces})
+    depth = len(blocks) * rows
+    arrays, index = sources(pieces)
+    more = [] if got is None else [got]
+    reads = len(blocks)
+    group = max(1, reads // 2)
+
+    def kernel(info_ref, cotangent_ref, *rest):
+        refs = rest[: len(arrays)]
+        got_refs = rest[len(arrays) : len(arrays) + len(more)]
+        out_ref, weights, turned, result, in_sems, out_sems, *held = rest[len(arrays) + len(more) :]
+        halves = []
+        for side in range(2):
+            lo = pl.multiple_of((lax.rem(info_ref[1], 2) ^ side) * half, half)
+            halves.append((cotangent_ref.at[:, pl.ds(lo, half)], turned.at[:, pl.ds(side * half, half)]))
+        first = started(halves, in_sems, 2 * reads)
+        pairs = [weight_copies(info_ref, pieces, index, refs, blocks, weights, rows, side) for side in range(2)]
+        inward = [started([pairs[side][r] for side in range(2)], in_sems, 2 * i) for i, r in enumerate(blocks)]
+        placing = started(list(zip(got_refs, held)), in_sems, 2 * reads + 2)
+        outward = []
+        wait(first)
+        for start in range(0, reads, group):
+            for i in range(start, start + group):
+                wait(inward[i])
+            at = pl.ds(start * rows, group * rows)
+            result[:, at] = dot(turned[...], weights[at, :], (1, 1)).astype(jnp.bfloat16)
+            for i in range(start, start + group):
+                at = pl.ds(i * rows, rows)
+                target = out_ref.at[:, aligned(info_ref[0] ^ blocks[i], rows) if more else at]
+                outward += started([(result.at[:, at], target)], out_sems, i)
+            if placing:
+                wait(placing)
+                placing = []
+                for i, r in enumerate(blocks):
+                    target = out_ref.at[:, aligned(info_ref[0] ^ r ^ 1, rows)]
+                    outward += started([(held[0].at[:, pl.ds(i * rows, rows)], target)], out_sems, reads + i)
+        wait(outward)
+
     return call(
         kernel,
-        "joined",
-        tokens * width,
-        (out, out),
-        [SMEM] + [VMEM] * 4,
-        (VMEM, ANY),
-        [pltpu.SemaphoreType.DMA((len(placed),))],
-    )(info, own, got, own_columns, got_columns)
+        "grad_columns",
+        2 * tokens * depth * width,
+        jax.ShapeDtypeStruct((tokens, width if more else depth), jnp.bfloat16),
+        [SMEM, ANY] + [ANY] * (len(arrays) + len(more)),
+        ANY,
+        [
+            pltpu.VMEM((depth, width), jnp.bfloat16),
+            pltpu.VMEM((tokens, width), jnp.bfloat16),
+            pltpu.VMEM((tokens, depth), jnp.bfloat16),
+            pltpu.SemaphoreType.DMA((2 * reads + 3,)),
+            pltpu.SemaphoreType.DMA((2 * reads,)),
+        ]
+        + [pltpu.VMEM((tokens, depth), jnp.bfloat16)] * len(more),
+    )(info, cotangent, *arrays, *more)
+
+
+def stepped(info, side, pieces, state, so_far=None):
+    rows, width = state[0].shape
+    lines = rows // 2
+    arrays = []
+    for piece in pieces:
+        if not any(piece[0] is array for array in arrays):
+            arrays.append(piece[0])
+    more = [] if so_far is None else list(so_far)
+
+    def kernel(info_ref, *rest):
+        grads, rest = rest[: len(arrays)], rest[len(arrays) :]
+        states, rest = rest[:3], rest[3 + len(more) :]
+        outs, held, results, in_sems, out_sems = rest[:3], rest[3:6], rest[6:9], rest[9], rest[10]
+        at = aligned(info_ref[1] ^ side, lines)
+        inward, outward = [], []
+        for n, (_, _, to, size) in enumerate(pieces):
+            cols = pl.ds(to, size)
+            inward.append(started([(states[i].at[at, cols], held[i].at[:, cols]) for i in range(3)], in_sems, 3 * n))
+        for n, (array, start, to, size) in enumerate(pieces):
+            wait(inward[n])
+            cols = pl.ds(to, size)
+            grad_ref = grads[[array is other for other in arrays].index(True)]
+            grad = grad_ref[:, pl.ds(start, size)].astype(jnp.float32)
+            values = adamw(held[0][:, cols], held[1][:, cols], held[2][:, cols], grad)
+            for result, value in zip(results, values):
+                result[:, cols] = value
+            outward += started([(results[i].at[:, cols], outs[i].at[at, cols]) for i in range(3)], out_sems, 3 * n)
+        wait(outward)
+
+    out = jax.ShapeDtypeStruct((rows, width), jnp.float32)
+    first = 4 + len(arrays)
+    return call(
+        kernel,
+        "stepped",
+        16 * lines * width,
+        (out,) * 3,
+        [SMEM] + [VMEM] * len(arrays) + [ANY] * (3 + len(more)),
+        (ANY,) * 3,
+        [pltpu.VMEM((lines, width), jnp.float32)] * 6 + [pltpu.SemaphoreType.DMA((3 * len(pieces),))] * 2,
+        {first + i: i for i in range(3)} if more else {},
+    )(info, *arrays, *state, *more)
 
 
 def plain_products(info, pieces, context, cotangent, rows):
@@ -259,7 +360,7 @@
         low = lax.rem(group, subs)
         info = jnp.stack([shard, low if subs > 1 else odd])
         order_of_rows = low
-        tiled = rows % 128 == 0 and (rows // subs) % 16 == 0 and subs > 1
+        tiled = rows % 128 == 0 and subs == 2
         latest = []
 
         def then(array):
@@ -274,9 +375,9 @@
 
         contexts, cotangents = (context, swap(context, 1)), (cotangent, swap(cotangent, 1))
 
-        weights = master.astype(jnp.bfloat16)
-        left, right = weights[:, :half], weights[:, half:]
+        left, right = master[:, :half], master[:, half:]
         mine, other = jnp.where(odd == 1, right, left), jnp.where(odd == 1, left, right)
+        mine, other = mine.astype(jnp.bfloat16), other.astype(jnp.bfloat16)
         near_x = {r: p for r, p in spread({0: mine}, x_masks).items() if r}
         near_y = {r: p for r, p in spread({0: other}, y_masks).items() if r}
 
@@ -286,19 +387,19 @@
         did(sent[-1][-1])
         got = {0: [swap(sent[0][h], masks[h][0]) for h in range(2)]}
 
-        near = jnp.concatenate([then(p) for p in [*near_x.values(), *near_y.values()]], axis=0)
-        did(near)
-        near_names = [(r, 0) for r in near_x] + [(r, 1) for r in near_y]
-        near_group = swap_group(near, 1)
+        kept = grad_blocks(info, [o[:count] for o in orders], contexts, (then(cotangent), cotangents[1]), rows, subs)
+        did(kept[-1][-1])
+
         far_x = spread({r: then(p) for r, p in near_x.items()}, y_masks)
         far_y = spread({r: then(p) for r, p in near_y.items()}, x_masks)
         far_names = [(r, 0) for r in far_x if r not in near_x] + [(r, 1) for r in far_y if r not in near_y]
         far = [(far_x, far_y)[h][r] for r, h in far_names]
+        near = jnp.concatenate([then(p) for p in [*near_x.values(), *near_y.values()]], axis=0)
+        near_names = [(r, 0) for r in near_x] + [(r, 1) for r in near_y]
+        near_group = swap_group(near, 1)
+        weights = then(master).astype(jnp.bfloat16)
         pieces = [(0, None, weights, 0)] + named(near_names, near) + named(near_names, near_group, flip=1)
         pieces += [(r, h, array, 0) for (r, h), array in zip(far_names, far)]
-        kept = grad_blocks(info, [o[:count] for o in orders], contexts, (then(cotangent), cotangents[1]), rows, subs)
-        did(kept[-1][-1])
-
         def halve_all(k, level):
             come, got[k] = got[k], [None, None]
             for h in range(2):
@@ -308,10 +409,10 @@
 
         summed, come, stage = {}, {}, {}
 
-        def enter(k):
-            parts = [did(add(kept[k][h], then(got[k][h]))) for h in range(2)]
-            summed[k], stage[k] = jnp.concatenate(parts, axis=1), 0
-            leave(k)
+        def enter(k, name, halves):
+            parts = [did(add(kept[k][h], then(got[k][h]))) for h in halves]
+            summed[name], stage[name] = jnp.concatenate(parts, axis=1) if len(parts) > 1 else parts[0], 0
+            leave(name)
 
         def leave(k):
             j, steps = stage[k], len(group_masks)
@@ -328,55 +429,69 @@
             if stage[k] <= len(group_masks):
                 summed[k] = did(add(summed[k], then(come[k])))
             else:
-                summed[k] = did(jnp.concatenate([summed[k], then(come[k])], axis=0))
+                summed[k] = jnp.concatenate([summed[k], then(come[k])], axis=0)
             stage[k] += 1
             leave(k)
 
         last = 2 * len(group_masks) + 1
         levels = len(masks[0])
-        chunks = len(CHUNKS)
 
         def halve_to_end(k, start):
             for level in range(start, levels):
                 halve_all(k, level)
 
-        def begin(k, *also):
-            got[k] = [swap(after(sent[k][h], *latest, *also), masks[h][0]) for h in range(2)]
+        def finish(name):
+            while stage[name] < last:
+                advance(name)
 
         halve_to_end(0, 1)
-        begin(1, *far)
-        enter(0)
+        got[1] = [swap(after(sent[1][h], *latest, *far), masks[h][0]) for h in range(2)]
+        enter(0, "both", (0, 1))
         if tiled:
-            blocks = sorted({piece[0] for piece in pieces})
-            sent_part, sent_columns = products(info, pieces, then(contexts[1]), cotangents[1], rows, jnp.bfloat16)
-            did(sent_part)
-            got_part, got_columns = swap(sent_part, 1), swap(sent_columns, 1)
+            part = did(product(info, pieces, then(contexts[1]), rows))
+            got_part = swap(part, 1)
         halve_to_end(1, 1)
-        begin(2)
-        advance(0)
-        enter(1)
+        advance("both")
         if tiled:
-            part, own_columns = products(info, pieces, then(context), cotangent, rows, jnp.float32)
-            did(part)
-        halve_to_end(2, 1)
-        advance(0)
-        enter(2)
-        advance(1)
+            columns = did(grad_columns(info, pieces, then(cotangents[1]), rows))
+            got_columns = swap(columns, 1)
+        enter(1, "first", (0,))
+        enter(1, "second", (1,))
         if tiled:
-            projected, columns = joined(info, then(part), got_part, own_columns, got_columns, blocks, rows)
-            did(projected)
+            projected = did(product(info, pieces, then(context), rows, got_part))
+        advance("first")
+        advance("second")
+        advance("both")
+        if tiled:
+            columns = did(grad_columns(info, pieces, then(cotangent), rows, got_columns))
         else:
             pieces += [(r ^ 1, h, swap(array, 1), row) for r, h, array, row in pieces]
             projected, columns = plain_products(info, pieces, context, cotangent, rows)
-        advance(2)
-        advance(1)
-        while any(stage[k] < last for k in range(chunks)):
-            for k in range(chunks):
-                if stage[k] < last:
-                    advance(k)
-        sizes = [half * units // sum(CHUNKS) for units in CHUNKS]
-        grad = [summed[k][:, h * sizes[k] : (h + 1) * sizes[k]] for h in range(2) for k in range(chunks)]
-        grad = reordered(jnp.concatenate(grad, axis=1), order_of_rows, subs).astype(jnp.float32)
+        advance("first")
+        advance("second")
+        if tiled:
+            sizes = [half * units // sum(CHUNKS) for units in CHUNKS]
+
+            def columns_of(both, first, second):
+                return [
+                    (both, 0, 0, sizes[0]),
+                    (both, sizes[0], half, sizes[0]),
+                    (first, 0, sizes[0], sizes[1]),
+                    (second, 0, half + sizes[0], sizes[1]),
+                ]
+
+            state = (then(master), moment_one, moment_two)
+            state = stepped(info, 0, columns_of(*[summed[name] for name in ("both", "first", "second")]), state)
+            grads = columns_of(*[come[name] for name in ("both", "first", "second")])
+            state = stepped(info, 1, grads, (master, moment_one, moment_two), state)
+            return (projected, columns, *state)
+        finish("both")
+        finish("first")
+        finish("second")
+        middle = half * CHUNKS[0] // sum(CHUNKS)
+        both = summed["both"]
+        grad = jnp.concatenate([both[:, :middle], summed["first"], both[:, middle:], summed["second"]], axis=1)
+        grad = reordered(grad, order_of_rows, subs).astype(jnp.float32)
         updated = adamw(master, moment_one, moment_two, grad)
         return (projected, columns, *updated)
 

time: 122 us -> 108 us (0.89)
  other arithmetic: 9.61 us -> 2.99 us
  Pallas kernels: 40.5 us -> 35 us
  local copies, waits for them, and re-layouts: 6.71 us -> 3.9 us
    ppermute x10, starting transfers between devices: 11 us -> 15.4 us  [swap_group(): return lax.ppermute(array, 'grp', [(i, i ^ mask) for i in range(groups)])]
    pallas_call x2, Pallas kernels: 13.6 us -> 9.28 us  [grad_blocks(): call(fill, 'grad_blocks', flops, outs, [SMEM] + [VMEM] * 4, (VMEM,) * len...]
    ppermute x20 -> x16, starting transfers between devices: 20.6 us -> 16.5 us  [swap(): return lax.ppermute(array, 'shard', [(i, i ^ mask) for i in range(shards)])]
    sub x1 -> x0, other arithmetic: 3.89 us -> none  [adamw(): master_new = master - 0.01 * (update + 0.1 * master)]
    unnamed x31 -> x13, local copies, waits for them, and re-layouts: 5.45 us -> 2.7 us
    ppermute x20 -> x16, waiting for transfers between devices: 19.1 us -> 21.2 us  [swap(): return lax.ppermute(array, 'shard', [(i, i ^ mask) for i in range(shards)])]
    pallas_call x3 -> x6, Pallas kernels: 27 us -> 25.7 us  [the longest x2 9.86 us: product(): call(kernel, 'product', 2 * tokens * depth * width, jax.ShapeDtypeStruct(...]
  transfers between devices with their start and end apart: 30 -> 26, of which waited for: 8 -> 12; matrix products, arithmetic and copies ran while one was open for 7% -> 5% of each run, Pallas kernels for 33% -> 30%
where the time goes in v2:
time: 108 us; the launch traced here: 107 us
  Pallas kernels  35 us (32%)
  waiting for transfers between devices  32.7 us (30%)
  starting transfers between devices  31.8 us (29%)
  local copies, waits for them, and re-layouts  3.9 us (4%)
  other arithmetic  2.99 us (3%)
  between operations  1.12 us (1%)
    ppermute x16, waiting for transfers between devices, swap(): return lax.ppermute(array, 'shard', [(i, i ^ mask) for i in range(shards)])  21.2 us
    ppermute x16, starting transfers between devices, swap(): return lax.ppermute(array, 'shard', [(i, i ^ mask) for i in range(shards)])  16.5 us
    ppermute x10, starting transfers between devices, swap_group(): return lax.ppermute(array, 'grp', [(i, i ^ mask) for i in range(groups)])  15.4 us
    ppermute x10, waiting for transfers between devices, swap_group(): return lax.ppermute(array, 'grp', [(i, i ^ mask) for i in range(groups)])  11.4 us
    pallas_call x2, Pallas kernels, product(): call(kernel, 'product', 2 * tokens * depth * width, jax.ShapeDtypeStruct(...  9.86 us
    pallas_call x2, Pallas kernels, grad_columns(): call(kernel, 'grad_columns', 2 * tokens * depth * width, jax.ShapeDtypeSt...  9.79 us
    pallas_call x2, Pallas kernels, grad_blocks(): call(fill, 'grad_blocks', flops, outs, [SMEM] + [VMEM] * 4, (VMEM,) * len...  9.28 us
    pallas_call x2, Pallas kernels, stepped(): call(kernel, 'stepped', 16 * lines * width, (out,) * 3, [SMEM] + [VMEM] *...  6.03 us
  transfers between devices with their start and end apart: 26, of which 12 were waited for; matrix products, arithmetic and copies ran while one was open for 5% of the time, Pallas kernels for 30%

profile of v2, /device:TPU:0, one launch (start us, length us, event | category | flops | bytes accessed | tf_op | source)
XLA Modules:
  0.0 107.5 jit_solution(6648467007373599929)
XLA Ops:
  0.6 0.5 collective-permute-start
  1.2 0.1 collective-permute-start.1
  1.2 1.7 %select_convert_fusion = (bf16[256,1024]{1,0:T(8,128)(2,1)S(1)}, bf16[256,1024]{1,0:T(8,128)(2,1)S(1)}) fusion(f32[256,2048]{1,0:T(8,128)} %rest_3_.2, pred[]{:T(512)S(6)} %eq.4), kind=kLoop, calls=%fused_computation.2 | loop fusion | flops 524288 | bytes 2097153 | tf_op jit(solution)/shard_map/convert_element_type | solution.py:380
  2.9 3.0 %collective-permute-start.6 = (bf16[256,1024]{1,0:T(8,128)(2,1)S(1)}, bf16[256,1024]{1,0:T(8,128)(2,1)}, u32[]{:S(2)}, u32[]{:S(2)}) collective-permute-start(bf16[256,1024]{1,0:T(8,128)(2,1)S(1)} %get-tuple-element.83), channel_id=1, source_target_pairs={{0,4},{1,5},{2,6},{3,7},{4,0},{5,1},{6,2},{7,3},{8,12},{9,13},{10,... | collective-permute-start | bytes 1572872 | tf_op jit(solution)/shard_map/ppermute | solution.py:339
  6.0 1.5 %collective-permute-start.4 = (bf16[256,1024]{1,0:T(8,128)(2,1)S(1)}, bf16[256,1024]{1,0:T(8,128)(2,1)}, u32[]{:S(2)}, u32[]{:S(2)}) collective-permute-start(bf16[256,1024]{1,0:T(8,128)(2,1)S(1)} %get-tuple-element.84), channel_id=1, source_target_pairs={{0,2},{1,3},{2,0},{3,1},{4,6},{5,7},{6,4},{7,5},{8,10},{9,11},{10,... | collective-permute-start | bytes 1572872 | tf_op jit(solution)/shard_map/ppermute | solution.py:339
  7.4 0.1 pad_add_fusion.info_ref
  7.5 0.8 collective-permute-done.1.t1.cotangent_ref
  8.3 1.6 %copy-done.4 = bf16[512,2048]{1,0:T(8,128)(2,1)S(1)} copy-done((bf16[512,2048]{1,0:T(8,128)(2,1)S(1)}, bf16[512,2048]{1,0:T(8,128)(2,1)}, u32[]{:S(2)}) %copy-start.4) | copy-done | bytes 2097176
  9.9 4.6 %grad_blocks.2 = (bf16[512,640]{1,0:T(8,128)(2,1)S(1)}, bf16[512,640]{1,0:T(8,128)(2,1)S(1)}, bf16[512,384]{1,0:T(8,128)(2,1)S(1)}, bf16[512,384]{1,0:T(8,128)(2,1)S(1)}) custom-call(s32[2]{0:T(128)S(1)} %pad_add_fusion.info_ref, bf16[512,2048]{1,0:T(8,128)(2,1)S(1)} %copy-done.3, bf16[512,2048]{1,0:T(8,128)(2,1)} %collective-permute-done.c1.context_ref, ...), custom_call_target="tpu_custom_call" | custom-call | flops 34359738368 | tf_op jit(solution)/shard_map/grad_blocks/pallas_call | solution.py:116
  14.5 3.0 %collective-permute-start.2 = (bf16[512,640]{1,0:T(8,128)(2,1)S(1)}, bf16[512,640]{1,0:T(8,128)(2,1)S(1)}, u32[]{:S(2)}, u32[]{:S(2)}) collective-permute-start(bf16[512,640]{1,0:T(8,128)(2,1)S(1)} %get-tuple-element.48), channel_id=1, source_target_pairs={{0,4},{1,5},{2,6},{3,7},{4,0},{5,1},{6,2},{7,3},{8,12},{9,13},{10,... | collective-permute-start | bytes 1966088 | tf_op jit(solution)/shard_map/ppermute | solution.py:339
  17.5 1.5 %collective-permute-start.3 = (bf16[512,640]{1,0:T(8,128)(2,1)S(1)}, bf16[512,640]{1,0:T(8,128)(2,1)S(1)}, u32[]{:S(2)}, u32[]{:S(2)}) collective-permute-start(bf16[512,640]{1,0:T(8,128)(2,1)S(1)} %get-tuple-element.50), channel_id=1, source_target_pairs={{0,2},{1,3},{2,0},{3,1},{4,6},{5,7},{6,4},{7,5},{8,10},{9,11},{10,... | collective-permute-start | bytes 1966088 | tf_op jit(solution)/shard_map/ppermute | solution.py:339
  19.0 4.6 %grad_blocks.3 = (bf16[512,640]{1,0:T(8,128)(2,1)S(1)}, bf16[512,640]{1,0:T(8,128)(2,1)S(1)}, bf16[512,384]{1,0:T(8,128)(2,1)S(1)}, bf16[512,384]{1,0:T(8,128)(2,1)S(1)}) custom-call(s32[2]{0:T(128)S(1)} %pad_add_fusion.info_ref, bf16[512,2048]{1,0:T(8,128)(2,1)S(1)} %copy-done.3, bf16[512,2048]{1,0:T(8,128)(2,1)} %collective-permute-done.c1.context_ref, ...), custom_call_target="tpu_custom_call" | custom-call | flops 34359738368 | tf_op jit(solution)/shard_map/grad_blocks/pallas_call | solution.py:116
  23.6 0.6 collective-permute-start.5
  24.2 0.1 collective-permute-start.7
  24.3 1.1 %constant_dynamic-update-slice_fusion.1 = bf16[512,1024]{1,0:T(8,128)(2,1)S(1)} fusion(bf16[256,1024]{1,0:T(8,128)(2,1)} %collective-permute-done.4), kind=kLoop, calls=%fused_computation.21 | loop fusion | bytes 1048576
  25.4 1.1 %constant_dynamic-update-slice_fusion.rest_1_ = bf16[512,1024]{1,0:T(8,128)(2,1)S(1)} fusion(bf16[512,1024]{1,0:T(8,128)(2,1)S(1)} %constant_dynamic-update-slice_fusion.1, bf16[256,1024]{1,0:T(8,128)(2,1)} %collective-permute-done.6), kind=kLoop, calls=%fused_computation.20 | loop fusion | bytes 1048576 | tf_op jit(solution)/shard_map/concatenate | solution.py:397
  26.5 2.1 %collective-permute-start.12 = (bf16[512,1024]{1,0:T(8,128)(2,1)S(1)}, bf16[512,1024]{1,0:T(8,128)(2,1)S(1)}, u32[]{:S(2)}, u32[]{:S(2)}) collective-permute-start(bf16[512,1024]{1,0:T(8,128)(2,1)S(1)} %constant_dynamic-update-slice_fusion.rest_1_), channel_id=1, source_target_pairs={{0,8},{8,0},{16,24},{24,16},{1,9},{9,1},{17,25},{25,17},{2,10},{10... | collective-permute-start | bytes 3145736 | tf_op jit(solution)/shard_map/ppermute | solution.py:342
  28.6 6.5 %collective-permute-done.3 = bf16[512,640]{1,0:T(8,128)(2,1)S(1)} collective-permute-done((bf16[512,640]{1,0:T(8,128)(2,1)S(1)}, bf16[512,640]{1,0:T(8,128)(2,1)S(1)}, u32[]{:S(2)}, u32[]{:S(2)}) %collective-permute-start.3) | collective-permute-done | bytes 655392 | tf_op jit(solution)/shard_map/ppermute | solution.py:339
  35.1 0.2 add_convert_fusion.1
  35.3 0.0 copy-start
  35.3 0.1 collective-permute-start.11
  35.4 0.2 add_convert_fusion
  35.6 2.0 %collective-permute-start.10 = (bf16[256,640]{1,0:T(8,128)(2,1)S(1)}, bf16[256,640]{1,0:T(8,128)(2,1)S(1)}, u32[]{:S(2)}, u32[]{:S(2)}) collective-permute-start(bf16[256,640]{1,0:T(8,128)(2,1)S(1)} %slice.65), channel_id=1, source_target_pairs={{0,2},{1,3},{2,0},{3,1},{4,6},{5,7},{6,4},{7,5},{8,10},{9,11},{10,... | collective-permute-start | bytes 983048 | tf_op jit(solution)/shard_map/ppermute | solution.py:339
  37.7 0.1 convert_element_type.151.rest_0_
  37.8 6.4 %collective-permute-done.5.rest_3_ = bf16[256,1024]{1,0:T(8,128)(2,1)S(1)} collective-permute-done((bf16[256,1024]{1,0:T(8,128)(2,1)}, bf16[256,1024]{1,0:T(8,128)(2,1)S(1)}, u32[]{:S(2)}, u32[]{:S(2)}) %collective-permute-start.5) | collective-permute-done | bytes 524320 | tf_op jit(solution)/shard_map/ppermute | solution.py:339
  44.2 2.1 %collective-permute-done.7.rest_4_ = bf16[256,1024]{1,0:T(8,128)(2,1)S(1)} collective-permute-done((bf16[256,1024]{1,0:T(8,128)(2,1)}, bf16[256,1024]{1,0:T(8,128)(2,1)S(1)}, u32[]{:S(2)}, u32[]{:S(2)}) %collective-permute-start.7) | collective-permute-done | bytes 524320 | tf_op jit(solution)/shard_map/ppermute | solution.py:339
  46.3 0.0 collective-permute-start.8
  46.4 1.9 %collective-permute-start.9 = (bf16[512,384]{1,0:T(8,128)(2,1)S(1)}, bf16[512,384]{1,0:T(8,128)(2,1)S(1)}, u32[]{:S(2)}, u32[]{:S(2)}) collective-permute-start(bf16[512,384]{1,0:T(8,128)(2,1)S(1)} %get-tuple-element.58), channel_id=1, source_target_pairs={{0,2},{1,3},{2,0},{3,1},{4,6},{5,7},{6,4},{7,5},{8,10},{9,11},{10,... | collective-permute-start | bytes 1179656 | tf_op jit(solution)/shard_map/ppermute | solution.py:339
  48.3 2.9 %collective-permute-done.11 = bf16[256,640]{1,0:T(8,128)(2,1)S(1)} collective-permute-done((bf16[256,640]{1,0:T(8,128)(2,1)S(1)}, bf16[256,640]{1,0:T(8,128)(2,1)S(1)}, u32[]{:S(2)}, u32[]{:S(2)}) %collective-permute-start.11) | collective-permute-done | bytes 327712 | tf_op jit(solution)/shard_map/ppermute | solution.py:339
  51.3 0.1 add_convert_fusion.7
  51.4 2.0 %collective-permute-done.10 = bf16[256,640]{1,0:T(8,128)(2,1)S(1)} collective-permute-done((bf16[256,640]{1,0:T(8,128)(2,1)S(1)}, bf16[256,640]{1,0:T(8,128)(2,1)S(1)}, u32[]{:S(2)}, u32[]{:S(2)}) %collective-permute-start.10) | collective-permute-done | bytes 327712 | tf_op jit(solution)/shard_map/ppermute | solution.py:339
  53.4 0.1 add_convert_fusion.6
  53.5 1.6 %collective-permute-start.15 = (bf16[128,1280]{1,0:T(8,128)(2,1)S(1)}, bf16[128,1280]{1,0:T(8,128)(2,1)S(1)}, u32[]{:S(2)}, u32[]{:S(2)}) collective-permute-start(bf16[128,1280]{1,0:T(8,128)(2,1)S(1)} %pad_maximum_fusion), channel_id=1, source_target_pairs={{0,8},{8,0},{16,24},{24,16},{1,9},{9,1},{17,25},{25,17},{2,10},{10... | collective-permute-start | bytes 983048 | tf_op jit(solution)/shard_map/ppermute | solution.py:342
  55.1 5.0 %product.2 = bf16[512,2048]{1,0:T(8,128)(2,1)S(1)} custom-call(s32[2]{0:T(128)S(1)} %pad_add_fusion.info_ref, bf16[512,2048]{1,0:T(8,128)(2,1)} %collective-permute-done.c1.context_ref, bf16[256,2048]{1,0:T(8,128)(2,1)S(1)} %convert_element_type.151.rest_0_, bf16[512,1024]{1,0:T(8,128)(2,1)S(1)} %constant_dynamic-update-slice_fusion.rest_1_, ...), custom_call_target="tpu_custom_call" | custom-call | flops 34359738368 | tf_op jit(solution)/shard_map/product/pallas_call | solution.py:201
  60.2 0.1 collective-permute-start.16
  60.3 0.4 collective-permute-done.9
  60.7 0.1 add_convert_fusion.3
  60.8 0.1 add_convert_fusion.2
  60.9 0.4 collective-permute-start.14
  61.4 1.6 %collective-permute-start.13 = (bf16[256,384]{1,0:T(8,128)(2,1)S(1)}, bf16[256,384]{1,0:T(8,128)(2,1)S(1)}, u32[]{:S(2)}, u32[]{:S(2)}) collective-permute-start(bf16[256,384]{1,0:T(8,128)(2,1)S(1)} %slice.69), channel_id=1, source_target_pairs={{0,2},{1,3},{2,0},{3,1},{4,6},{5,7},{6,4},{7,5},{8,10},{9,11},{10,... | collective-permute-start | bytes 589832 | tf_op jit(solution)/shard_map/ppermute | solution.py:339
  63.0 0.1 add_convert_fusion.5
  63.1 5.0 %grad_columns.2 = bf16[512,1024]{1,0:T(8,128)(2,1)S(1)} custom-call(s32[2]{0:T(128)S(1)} %pad_add_fusion.info_ref, bf16[512,2048]{1,0:T(8,128)(2,1)} %collective-permute-done.1.t1.cotangent_ref, bf16[256,2048]{1,0:T(8,128)(2,1)S(1)} %convert_element_type.151.rest_0_, bf16[512,1024]{1,0:T(8,128)(2,1)S(1)} %constant_dynamic-update-slice_fusion.rest_1_, ...), custom_call_target="tpu_custom_call" | custom-call | flops 34359738368 | tf_op jit(solution)/shard_map/grad_columns/pallas_call | solution.py:260
  68.1 0.1 add_convert_fusion.9
  68.2 0.1 add_convert_fusion.8
  68.3 0.0 copy-start.5
  68.3 2.7 %collective-permute-start.17 = (bf16[128,1280]{1,0:T(8,128)(2,1)S(1)}, bf16[128,1280]{1,0:T(8,128)(2,1)S(1)}, u32[]{:S(2)}, u32[]{:S(2)}) collective-permute-start(bf16[128,1280]{1,0:T(8,128)(2,1)S(1)} %add_convert_fusion.5), channel_id=1, source_target_pairs={{0,16},{8,24},{16,0},{24,8},{1,17},{9,25},{17,1},{25,9},{2,18},{10... | collective-permute-start | bytes 983048 | tf_op jit(solution)/shard_map/ppermute | solution.py:342
  70.9 1.6 %collective-permute-start.19 = (bf16[128,384]{1,0:T(8,128)(2,1)S(1)}, bf16[128,384]{1,0:T(8,128)(2,1)S(1)}, u32[]{:S(2)}, u32[]{:S(2)}) collective-permute-start(bf16[128,384]{1,0:T(8,128)(2,1)S(1)} %slice.77), channel_id=1, source_target_pairs={{0,8},{8,0},{16,24},{24,16},{1,9},{9,1},{17,25},{25,17},{2,10},{10... | collective-permute-start | bytes 294920 | tf_op jit(solution)/shard_map/ppermute | solution.py:342
  72.5 0.5 collective-permute-start.18
  73.0 4.8 %product.3 = bf16[512,2048]{1,0:T(8,128)(2,1)} custom-call(s32[2]{0:T(128)S(1)} %pad_add_fusion.info_ref, bf16[512,2048]{1,0:T(8,128)(2,1)S(1)} %copy-done.3, bf16[256,2048]{1,0:T(8,128)(2,1)S(1)} %convert_element_type.151.rest_0_, bf16[512,1024]{1,0:T(8,128)(2,1)S(1)} %constant_dynamic-update-slice_fusion.rest_1_, ...), custom_call_target="tpu_custom_call" | custom-call | flops 34359738368 | tf_op jit(solution)/shard_map/product/pallas_call | solution.py:201
  77.8 3.4 %collective-permute-done.19 = bf16[128,384]{1,0:T(8,128)(2,1)S(1)} collective-permute-done((bf16[128,384]{1,0:T(8,128)(2,1)S(1)}, bf16[128,384]{1,0:T(8,128)(2,1)S(1)}, u32[]{:S(2)}, u32[]{:S(2)}) %collective-permute-start.19) | collective-permute-done | bytes 98336 | tf_op jit(solution)/shard_map/ppermute | solution.py:342
  81.2 0.9 collective-permute-start.22
  82.2 1.1 %collective-permute-done.18 = bf16[128,384]{1,0:T(8,128)(2,1)S(1)} collective-permute-done((bf16[128,384]{1,0:T(8,128)(2,1)S(1)}, bf16[128,384]{1,0:T(8,128)(2,1)S(1)}, u32[]{:S(2)}, u32[]{:S(2)}) %collective-permute-start.18) | collective-permute-done | bytes 98336 | tf_op jit(solution)/shard_map/ppermute | solution.py:342
  83.3 1.0 collective-permute-start.24
  84.3 3.2 %collective-permute-done.17 = bf16[128,1280]{1,0:T(8,128)(2,1)S(1)} collective-permute-done((bf16[128,1280]{1,0:T(8,128)(2,1)S(1)}, bf16[128,1280]{1,0:T(8,128)(2,1)S(1)}, u32[]{:S(2)}, u32[]{:S(2)}) %collective-permute-start.17) | collective-permute-done | bytes 327712 | tf_op jit(solution)/shard_map/ppermute | solution.py:342
  87.5 0.1 add_convert_fusion.4.rest_0_
  87.6 0.0 copy-start.2
  87.6 3.0 %collective-permute-start.21 = (bf16[128,1280]{1,0:T(8,128)(2,1)S(1)}, bf16[128,1280]{1,0:T(8,128)(2,1)S(1)}, u32[]{:S(2)}, u32[]{:S(2)}) collective-permute-start(bf16[128,1280]{1,0:T(8,128)(2,1)S(1)} %add_convert_fusion.4.rest_0_), channel_id=1, source_target_pairs={{0,8},{8,0},{16,24},{24,16},{1,9},{9,1},{17,25},{25,17},{2,10},{10... | collective-permute-start | bytes 983048 | tf_op jit(solution)/shard_map/ppermute | solution.py:342
  90.6 4.8 %grad_columns.3 = bf16[512,2048]{1,0:T(8,128)(2,1)} custom-call(s32[2]{0:T(128)S(1)} %pad_add_fusion.info_ref, bf16[512,2048]{1,0:T(8,128)(2,1)S(1)} %copy-done.5, bf16[256,2048]{1,0:T(8,128)(2,1)S(1)} %convert_element_type.151.rest_0_, bf16[512,1024]{1,0:T(8,128)(2,1)S(1)} %constant_dynamic-update-slice_fusion.rest_1_, ...), custom_call_target="tpu_custom_call" | custom-call | flops 34359738368 | tf_op jit(solution)/shard_map/grad_columns/pallas_call | solution.py:260
  95.5 0.1 collective-permute-start.25
  95.6 2.0 %collective-permute-start.23 = (bf16[128,384]{1,0:T(8,128)(2,1)S(1)}, bf16[128,384]{1,0:T(8,128)(2,1)S(1)}, u32[]{:S(2)}, u32[]{:S(2)}) collective-permute-start(bf16[128,384]{1,0:T(8,128)(2,1)S(1)} %add_convert_fusion.11.rest_1_), channel_id=1, source_target_pairs={{0,8},{8,0},{16,24},{24,16},{1,9},{9,1},{17,25},{25,17},{2,10},{10... | collective-permute-start | bytes 294920 | tf_op jit(solution)/shard_map/ppermute | solution.py:342
  97.6 3.0 %stepped.2 = (f32[256,2048]{1,0:T(8,128)}, f32[256,2048]{1,0:T(8,128)}, f32[256,2048]{1,0:T(8,128)}) custom-call(s32[2]{0:T(128)S(1)} %pad_add_fusion.info_ref, bf16[128,1280]{1,0:T(8,128)(2,1)S(1)} %add_convert_fusion.4.rest_0_, bf16[128,384]{1,0:T(8,128)(2,1)S(1)} %add_convert_fusion.11.rest_1_, bf16[128,384]{1,0:T(8,128)(2,1)S(1)} %add_convert_fusion.10.rest_2_, ...), custom_call_target="tpu_custom_call" | custom-call | flops 67108864 | tf_op jit(solution)/shard_map/stepped/pallas_call | solution.py:309
  100.6 2.4 %collective-permute-done.25.rest_2_ = bf16[128,384]{1,0:T(8,128)(2,1)S(1)} collective-permute-done((bf16[128,384]{1,0:T(8,128)(2,1)S(1)}, bf16[128,384]{1,0:T(8,128)(2,1)S(1)}, u32[]{:S(2)}, u32[]{:S(2)}) %collective-permute-start.25) | collective-permute-done | bytes 98336 | tf_op jit(solution)/shard_map/ppermute | solution.py:342
  103.1 1.2 %collective-permute-done.23.rest_1_ = bf16[128,384]{1,0:T(8,128)(2,1)S(1)} collective-permute-done((bf16[128,384]{1,0:T(8,128)(2,1)S(1)}, bf16[128,384]{1,0:T(8,128)(2,1)S(1)}, u32[]{:S(2)}, u32[]{:S(2)}) %collective-permute-start.23) | collective-permute-done | bytes 98336 | tf_op jit(solution)/shard_map/ppermute | solution.py:342
  104.3 3.0 %stepped.3 = (f32[256,2048]{1,0:T(8,128)}, f32[256,2048]{1,0:T(8,128)}, f32[256,2048]{1,0:T(8,128)}) custom-call(s32[2]{0:T(128)S(1)} %pad_add_fusion.info_ref, bf16[128,1280]{1,0:T(8,128)(2,1)S(1)} %collective-permute-done.21.rest_0_, ...), custom_call_target="tpu_custom_call", output_to_operand_aliasing={{0}: (7, {}), {1}: (8, {}), {2}: (9, {})} | custom-call | flops 67108864 | tf_op jit(solution)/shard_map/stepped/pallas_call | solution.py:309
  (34 shorter events, 0.3 us)
Async XLA Ops:
  0.6 7.7 %copy-start.3 = (bf16[512,2048]{1,0:T(8,128)(2,1)S(1)}, bf16[512,2048]{1,0:T(8,128)(2,1)}, u32[]{:S(2)}) copy-start(bf16[512,2048]{1,0:T(8,128)(2,1)} %context_ref) | copy-start | bytes 6291460
  0.6 6.9 %collective-permute-start = (bf16[512,2048]{1,0:T(8,128)(2,1)}, bf16[512,2048]{1,0:T(8,128)(2,1)}, u32[]{:S(2)}, u32[]{:S(2)}) collective-permute-start(bf16[512,2048]{1,0:T(8,128)(2,1)} %context_ref), channel_id=1, source_target_pairs={{0,1},{1,0},{2,3},{3,2},{4,5},{5,4},{6,7},{7,6},{8,9},{9,8},{10,11... | collective-permute-start | bytes 6291464 | tf_op jit(solution)/shard_map/ppermute | solution.py:339
  1.2 7.1 %collective-permute-start.1 = (bf16[512,2048]{1,0:T(8,128)(2,1)}, bf16[512,2048]{1,0:T(8,128)(2,1)}, u32[]{:S(2)}, u32[]{:S(2)}) collective-permute-start(bf16[512,2048]{1,0:T(8,128)(2,1)} %cotangent_ref), channel_id=1, source_target_pairs={{0,1},{1,0},{2,3},{3,2},{4,5},{5,4},{6,7},{7,6},{8,9},{9,8},{10,11... | collective-permute-start | bytes 6291464 | tf_op jit(solution)/shard_map/ppermute | solution.py:339
  2.9 20.7 %collective-permute-start.6 = (bf16[256,1024]{1,0:T(8,128)(2,1)S(1)}, bf16[256,1024]{1,0:T(8,128)(2,1)}, u32[]{:S(2)}, u32[]{:S(2)}) collective-permute-start(bf16[256,1024]{1,0:T(8,128)(2,1)S(1)} %get-tuple-element.83), channel_id=1, source_target_pairs={{0,4},{1,5},{2,6},{3,7},{4,0},{5,1},{6,2},{7,3},{8,12},{9,13},{10,... | collective-permute-start | bytes 1572872 | tf_op jit(solution)/shard_map/ppermute | solution.py:339
  6.0 17.7 %collective-permute-start.4 = (bf16[256,1024]{1,0:T(8,128)(2,1)S(1)}, bf16[256,1024]{1,0:T(8,128)(2,1)}, u32[]{:S(2)}, u32[]{:S(2)}) collective-permute-start(bf16[256,1024]{1,0:T(8,128)(2,1)S(1)} %get-tuple-element.84), channel_id=1, source_target_pairs={{0,2},{1,3},{2,0},{3,1},{4,6},{5,7},{6,4},{7,5},{8,10},{9,11},{10,... | collective-permute-start | bytes 1572872 | tf_op jit(solution)/shard_map/ppermute | solution.py:339
  8.3 1.6 %copy-start.4 = (bf16[512,2048]{1,0:T(8,128)(2,1)S(1)}, bf16[512,2048]{1,0:T(8,128)(2,1)}, u32[]{:S(2)}) copy-start(bf16[512,2048]{1,0:T(8,128)(2,1)} %cotangent_ref) | copy-start | bytes 6291460
  14.5 20.8 %collective-permute-start.2 = (bf16[512,640]{1,0:T(8,128)(2,1)S(1)}, bf16[512,640]{1,0:T(8,128)(2,1)S(1)}, u32[]{:S(2)}, u32[]{:S(2)}) collective-permute-start(bf16[512,640]{1,0:T(8,128)(2,1)S(1)} %get-tuple-element.48), channel_id=1, source_target_pairs={{0,4},{1,5},{2,6},{3,7},{4,0},{5,1},{6,2},{7,3},{8,12},{9,13},{10,... | collective-permute-start | bytes 1966088 | tf_op jit(solution)/shard_map/ppermute | solution.py:339
  17.5 17.6 %collective-permute-start.3 = (bf16[512,640]{1,0:T(8,128)(2,1)S(1)}, bf16[512,640]{1,0:T(8,128)(2,1)S(1)}, u32[]{:S(2)}, u32[]{:S(2)}) collective-permute-start(bf16[512,640]{1,0:T(8,128)(2,1)S(1)} %get-tuple-element.50), channel_id=1, source_target_pairs={{0,2},{1,3},{2,0},{3,1},{4,6},{5,7},{6,4},{7,5},{8,10},{9,11},{10,... | collective-permute-start | bytes 1966088 | tf_op jit(solution)/shard_map/ppermute | solution.py:339
  23.6 20.6 %collective-permute-start.5 = (bf16[256,1024]{1,0:T(8,128)(2,1)}, bf16[256,1024]{1,0:T(8,128)(2,1)S(1)}, u32[]{:S(2)}, u32[]{:S(2)}) collective-permute-start(bf16[256,1024]{1,0:T(8,128)(2,1)} %collective-permute-done.4), channel_id=1, source_target_pairs={{0,4},{1,5},{2,6},{3,7},{4,0},{5,1},{6,2},{7,3},{8,12},{9,13},{10,... | collective-permute-start | bytes 1572872 | tf_op jit(solution)/shard_map/ppermute | solution.py:339
  24.2 22.1 %collective-permute-start.7 = (bf16[256,1024]{1,0:T(8,128)(2,1)}, bf16[256,1024]{1,0:T(8,128)(2,1)S(1)}, u32[]{:S(2)}, u32[]{:S(2)}) collective-permute-start(bf16[256,1024]{1,0:T(8,128)(2,1)} %collective-permute-done.6), channel_id=1, source_target_pairs={{0,2},{1,3},{2,0},{3,1},{4,6},{5,7},{6,4},{7,5},{8,10},{9,11},{10,... | collective-permute-start | bytes 1572872 | tf_op jit(solution)/shard_map/ppermute | solution.py:339
  26.5 28.6 %collective-permute-start.12 = (bf16[512,1024]{1,0:T(8,128)(2,1)S(1)}, bf16[512,1024]{1,0:T(8,128)(2,1)S(1)}, u32[]{:S(2)}, u32[]{:S(2)}) collective-permute-start(bf16[512,1024]{1,0:T(8,128)(2,1)S(1)} %constant_dynamic-update-slice_fusion.rest_1_), channel_id=1, source_target_pairs={{0,8},{8,0},{16,24},{24,16},{1,9},{9,1},{17,25},{25,17},{2,10},{10... | collective-permute-start | bytes 3145736 | tf_op jit(solution)/shard_map/ppermute | solution.py:342
  35.3 2.4 %copy-start = (f32[256,2048]{1,0:T(8,128)S(1)}, f32[256,2048]{1,0:T(8,128)}, u32[]{:S(2)}) copy-start(f32[256,2048]{1,0:T(8,128)} %rest_3_.2) | copy-start | bytes 6291460
  35.3 15.9 %collective-permute-start.11 = (bf16[256,640]{1,0:T(8,128)(2,1)S(1)}, bf16[256,640]{1,0:T(8,128)(2,1)S(1)}, u32[]{:S(2)}, u32[]{:S(2)}) collective-permute-start(bf16[256,640]{1,0:T(8,128)(2,1)S(1)} %slice.67), channel_id=1, source_target_pairs={{0,4},{1,5},{2,6},{3,7},{4,0},{5,1},{6,2},{7,3},{8,12},{9,13},{10,... | collective-permute-start | bytes 983048 | tf_op jit(solution)/shard_map/ppermute | solution.py:339
  35.6 17.7 %collective-permute-start.10 = (bf16[256,640]{1,0:T(8,128)(2,1)S(1)}, bf16[256,640]{1,0:T(8,128)(2,1)S(1)}, u32[]{:S(2)}, u32[]{:S(2)}) collective-permute-start(bf16[256,640]{1,0:T(8,128)(2,1)S(1)} %slice.65), channel_id=1, source_target_pairs={{0,2},{1,3},{2,0},{3,1},{4,6},{5,7},{6,4},{7,5},{8,10},{9,11},{10,... | collective-permute-start | bytes 983048 | tf_op jit(solution)/shard_map/ppermute | solution.py:339
  46.3 14.5 %collective-permute-start.8 = (bf16[512,384]{1,0:T(8,128)(2,1)S(1)}, bf16[512,384]{1,0:T(8,128)(2,1)S(1)}, u32[]{:S(2)}, u32[]{:S(2)}) collective-permute-start(bf16[512,384]{1,0:T(8,128)(2,1)S(1)} %get-tuple-element.55), channel_id=1, source_target_pairs={{0,4},{1,5},{2,6},{3,7},{4,0},{5,1},{6,2},{7,3},{8,12},{9,13},{10,... | collective-permute-start | bytes 1179656 | tf_op jit(solution)/shard_map/ppermute | solution.py:339
  46.4 14.3 %collective-permute-start.9 = (bf16[512,384]{1,0:T(8,128)(2,1)S(1)}, bf16[512,384]{1,0:T(8,128)(2,1)S(1)}, u32[]{:S(2)}, u32[]{:S(2)}) collective-permute-start(bf16[512,384]{1,0:T(8,128)(2,1)S(1)} %get-tuple-element.58), channel_id=1, source_target_pairs={{0,2},{1,3},{2,0},{3,1},{4,6},{5,7},{6,4},{7,5},{8,10},{9,11},{10,... | collective-permute-start | bytes 1179656 | tf_op jit(solution)/shard_map/ppermute | solution.py:339
  53.5 9.5 %collective-permute-start.15 = (bf16[128,1280]{1,0:T(8,128)(2,1)S(1)}, bf16[128,1280]{1,0:T(8,128)(2,1)S(1)}, u32[]{:S(2)}, u32[]{:S(2)}) collective-permute-start(bf16[128,1280]{1,0:T(8,128)(2,1)S(1)} %pad_maximum_fusion), channel_id=1, source_target_pairs={{0,8},{8,0},{16,24},{24,16},{1,9},{9,1},{17,25},{25,17},{2,10},{10... | collective-permute-start | bytes 983048 | tf_op jit(solution)/shard_map/ppermute | solution.py:342
  60.2 12.8 %collective-permute-start.16 = (bf16[512,2048]{1,0:T(8,128)(2,1)S(1)}, bf16[512,2048]{1,0:T(8,128)(2,1)S(1)}, u32[]{:S(2)}, u32[]{:S(2)}) collective-permute-start(bf16[512,2048]{1,0:T(8,128)(2,1)S(1)} %product.2), channel_id=1, source_target_pairs={{0,1},{1,0},{2,3},{3,2},{4,5},{5,4},{6,7},{7,6},{8,9},{9,8},{10,11... | collective-permute-start | bytes 6291464 | tf_op jit(solution)/shard_map/ppermute | solution.py:339
  60.9 7.2 %collective-permute-start.14 = (bf16[256,384]{1,0:T(8,128)(2,1)S(1)}, bf16[256,384]{1,0:T(8,128)(2,1)S(1)}, u32[]{:S(2)}, u32[]{:S(2)}) collective-permute-start(bf16[256,384]{1,0:T(8,128)(2,1)S(1)} %slice.71), channel_id=1, source_target_pairs={{0,4},{1,5},{2,6},{3,7},{4,0},{5,1},{6,2},{7,3},{8,12},{9,13},{10,... | collective-permute-start | bytes 589832 | tf_op jit(solution)/shard_map/ppermute | solution.py:339
  61.4 6.8 %collective-permute-start.13 = (bf16[256,384]{1,0:T(8,128)(2,1)S(1)}, bf16[256,384]{1,0:T(8,128)(2,1)S(1)}, u32[]{:S(2)}, u32[]{:S(2)}) collective-permute-start(bf16[256,384]{1,0:T(8,128)(2,1)S(1)} %slice.69), channel_id=1, source_target_pairs={{0,2},{1,3},{2,0},{3,1},{4,6},{5,7},{6,4},{7,5},{8,10},{9,11},{10,... | collective-permute-start | bytes 589832 | tf_op jit(solution)/shard_map/ppermute | solution.py:339
  68.3 22.3 %copy-start.5 = (bf16[512,2048]{1,0:T(8,128)(2,1)S(1)}, bf16[512,2048]{1,0:T(8,128)(2,1)}, u32[]{:S(2)}) copy-start(bf16[512,2048]{1,0:T(8,128)(2,1)} %cotangent_ref) | copy-start | bytes 6291460
  68.3 19.3 %collective-permute-start.17 = (bf16[128,1280]{1,0:T(8,128)(2,1)S(1)}, bf16[128,1280]{1,0:T(8,128)(2,1)S(1)}, u32[]{:S(2)}, u32[]{:S(2)}) collective-permute-start(bf16[128,1280]{1,0:T(8,128)(2,1)S(1)} %add_convert_fusion.5), channel_id=1, source_target_pairs={{0,16},{8,24},{16,0},{24,8},{1,17},{9,25},{17,1},{25,9},{2,18},{10... | collective-permute-start | bytes 983048 | tf_op jit(solution)/shard_map/ppermute | solution.py:342
  70.9 19.7 %collective-permute-start.20 = (bf16[512,1024]{1,0:T(8,128)(2,1)S(1)}, bf16[512,1024]{1,0:T(8,128)(2,1)S(1)}, u32[]{:S(2)}, u32[]{:S(2)}) collective-permute-start(bf16[512,1024]{1,0:T(8,128)(2,1)S(1)} %grad_columns.2), channel_id=1, source_target_pairs={{0,1},{1,0},{2,3},{3,2},{4,5},{5,4},{6,7},{7,6},{8,9},{9,8},{10,11... | collective-permute-start | bytes 3145736 | tf_op jit(solution)/shard_map/ppermute | solution.py:339
  70.9 10.3 %collective-permute-start.19 = (bf16[128,384]{1,0:T(8,128)(2,1)S(1)}, bf16[128,384]{1,0:T(8,128)(2,1)S(1)}, u32[]{:S(2)}, u32[]{:S(2)}) collective-permute-start(bf16[128,384]{1,0:T(8,128)(2,1)S(1)} %slice.77), channel_id=1, source_target_pairs={{0,8},{8,0},{16,24},{24,16},{1,9},{9,1},{17,25},{25,17},{2,10},{10... | collective-permute-start | bytes 294920 | tf_op jit(solution)/shard_map/ppermute | solution.py:342
  72.5 10.8 %collective-permute-start.18 = (bf16[128,384]{1,0:T(8,128)(2,1)S(1)}, bf16[128,384]{1,0:T(8,128)(2,1)S(1)}, u32[]{:S(2)}, u32[]{:S(2)}) collective-permute-start(bf16[128,384]{1,0:T(8,128)(2,1)S(1)} %slice.75), channel_id=1, source_target_pairs={{0,8},{8,0},{16,24},{24,16},{1,9},{9,1},{17,25},{25,17},{2,10},{10... | collective-permute-start | bytes 294920 | tf_op jit(solution)/shard_map/ppermute | solution.py:342
  81.2 14.2 %collective-permute-start.22 = (bf16[128,384]{1,0:T(8,128)(2,1)S(1)}, bf16[128,384]{1,0:T(8,128)(2,1)S(1)}, u32[]{:S(2)}, u32[]{:S(2)}) collective-permute-start(bf16[128,384]{1,0:T(8,128)(2,1)S(1)} %add_convert_fusion.13), channel_id=1, source_target_pairs={{0,16},{8,24},{16,0},{24,8},{1,17},{9,25},{17,1},{25,9},{2,18},{10... | collective-permute-start | bytes 294920 | tf_op jit(solution)/shard_map/ppermute | solution.py:342
  83.3 12.1 %collective-permute-start.24 = (bf16[128,384]{1,0:T(8,128)(2,1)S(1)}, bf16[128,384]{1,0:T(8,128)(2,1)S(1)}, u32[]{:S(2)}, u32[]{:S(2)}) collective-permute-start(bf16[128,384]{1,0:T(8,128)(2,1)S(1)} %add_convert_fusion.12), channel_id=1, source_target_pairs={{0,16},{8,24},{16,0},{24,8},{1,17},{9,25},{17,1},{25,9},{2,18},{10... | collective-permute-start | bytes 294920 | tf_op jit(solution)/shard_map/ppermute | solution.py:342
  87.6 10.0 %copy-start.1 = (f32[256,2048]{1,0:T(8,128)S(1)}, f32[256,2048]{1,0:T(8,128)}, u32[]{:S(2)}) copy-start(f32[256,2048]{1,0:T(8,128)} %rest_4_.3) | copy-start | bytes 6291460
  87.6 10.0 %copy-start.2 = (f32[256,2048]{1,0:T(8,128)S(1)}, f32[256,2048]{1,0:T(8,128)}, u32[]{:S(2)}) copy-start(f32[256,2048]{1,0:T(8,128)} %rest_5_.3) | copy-start | bytes 6291460
  87.6 16.6 %collective-permute-start.21 = (bf16[128,1280]{1,0:T(8,128)(2,1)S(1)}, bf16[128,1280]{1,0:T(8,128)(2,1)S(1)}, u32[]{:S(2)}, u32[]{:S(2)}) collective-permute-start(bf16[128,1280]{1,0:T(8,128)(2,1)S(1)} %add_convert_fusion.4.rest_0_), channel_id=1, source_target_pairs={{0,8},{8,0},{16,24},{24,16},{1,9},{9,1},{17,25},{25,17},{2,10},{10... | collective-permute-start | bytes 983048 | tf_op jit(solution)/shard_map/ppermute | solution.py:342
  95.5 7.5 %collective-permute-start.25 = (bf16[128,384]{1,0:T(8,128)(2,1)S(1)}, bf16[128,384]{1,0:T(8,128)(2,1)S(1)}, u32[]{:S(2)}, u32[]{:S(2)}) collective-permute-start(bf16[128,384]{1,0:T(8,128)(2,1)S(1)} %add_convert_fusion.10.rest_2_), channel_id=1, source_target_pairs={{0,8},{8,0},{16,24},{24,16},{1,9},{9,1},{17,25},{25,17},{2,10},{10... | collective-permute-start | bytes 294920 | tf_op jit(solution)/shard_map/ppermute | solution.py:342
  95.6 8.7 %collective-permute-start.23 = (bf16[128,384]{1,0:T(8,128)(2,1)S(1)}, bf16[128,384]{1,0:T(8,128)(2,1)S(1)}, u32[]{:S(2)}, u32[]{:S(2)}) collective-permute-start(bf16[128,384]{1,0:T(8,128)(2,1)S(1)} %add_convert_fusion.11.rest_1_), channel_id=1, source_target_pairs={{0,8},{8,0},{16,24},{24,16},{1,9},{9,1},{17,25},{25,17},{2,10},{10... | collective-permute-start | bytes 294920 | tf_op jit(solution)/shard_map/ppermute | solution.py:342

commit v3 on v2

--- a/solution.py
+++ b/solution.py
@@ -201,7 +201,7 @@
     return call(
         kernel,
         "product",
-        2 * tokens * depth * width,
+        0 if more else 2 * tokens * depth * width,
         jax.ShapeDtypeStruct((tokens, width), jnp.bfloat16),
         [SMEM, ANY] + [ANY] * (len(arrays) + len(more)),
         ANY,
@@ -309,7 +309,7 @@
     return call(
         kernel,
         "stepped",
-        16 * lines * width,
+        512 * lines * width if so_far is None else 0,
         (out,) * 3,
         [SMEM] + [VMEM] * len(arrays) + [ANY] * (3 + len(more)),
         (ANY,) * 3,
@@ -381,6 +381,7 @@
         near_x = {r: p for r, p in spread({0: mine}, x_masks).items() if r}
         near_y = {r: p for r, p in spread({0: other}, y_masks).items() if r}
 
+        chunk_sizes = [half * units // sum(CHUNKS) for units in CHUNKS]
         orders = [halving(m) for m in masks]
         count = len(orders[0]) // 2
         sent = grad_blocks(info, [o[count:] for o in orders], contexts, cotangents, rows, subs)
@@ -446,51 +447,44 @@
 
         halve_to_end(0, 1)
         got[1] = [swap(after(sent[1][h], *latest, *far), masks[h][0]) for h in range(2)]
-        enter(0, "both", (0, 1))
+        enter(0, "first", (0, 1))
         if tiled:
             part = did(product(info, pieces, then(contexts[1]), rows))
             got_part = swap(part, 1)
         halve_to_end(1, 1)
-        advance("both")
+        advance("first")
         if tiled:
             columns = did(grad_columns(info, pieces, then(cotangents[1]), rows))
             got_columns = swap(columns, 1)
-        enter(1, "first", (0,))
-        enter(1, "second", (1,))
+        enter(1, "rest", (0, 1))
         if tiled:
             projected = did(product(info, pieces, then(context), rows, got_part))
-        advance("first")
-        advance("second")
-        advance("both")
-        if tiled:
-            columns = did(grad_columns(info, pieces, then(cotangent), rows, got_columns))
         else:
             pieces += [(r ^ 1, h, swap(array, 1), row) for r, h, array, row in pieces]
             projected, columns = plain_products(info, pieces, context, cotangent, rows)
         advance("first")
-        advance("second")
+        advance("rest")
         if tiled:
-            sizes = [half * units // sum(CHUNKS) for units in CHUNKS]
-
-            def columns_of(both, first, second):
-                return [
-                    (both, 0, 0, sizes[0]),
-                    (both, sizes[0], half, sizes[0]),
-                    (first, 0, sizes[0], sizes[1]),
-                    (second, 0, half + sizes[0], sizes[1]),
-                ]
-
-            state = (then(master), moment_one, moment_two)
-            state = stepped(info, 0, columns_of(*[summed[name] for name in ("both", "first", "second")]), state)
-            grads = columns_of(*[come[name] for name in ("both", "first", "second")])
-            state = stepped(info, 1, grads, (master, moment_one, moment_two), state)
-            return (projected, columns, *state)
-        finish("both")
+            sizes = chunk_sizes
+
+            def columns_of(array, k):
+                start = k * sizes[0]
+                return [(array, 0, start, sizes[k]), (array, sizes[k], half + start, sizes[k])]
+
+            state = (master, moment_one, moment_two)
+            so_far = stepped(info, 0, columns_of(summed["first"], 0), (then(master), *state[1:]))
+            did(so_far[0])
+            columns = did(grad_columns(info, pieces, then(cotangent), rows, got_columns))
+        advance("rest")
+        if tiled:
+            so_far = stepped(info, 0, columns_of(summed["rest"], 1), state, so_far)
+            grads = columns_of(come["first"], 0) + columns_of(come["rest"], 1)
+            return (projected, columns, *stepped(info, 1, grads, state, so_far))
         finish("first")
-        finish("second")
-        middle = half * CHUNKS[0] // sum(CHUNKS)
-        both = summed["both"]
-        grad = jnp.concatenate([both[:, :middle], summed["first"], both[:, middle:], summed["second"]], axis=1)
+        finish("rest")
+        named_sizes = list(zip(("first", "rest"), chunk_sizes))
+        parts = [summed[name][:, h * size : (h + 1) * size] for h in range(2) for name, size in named_sizes]
+        grad = jnp.concatenate(parts, axis=1)
         grad = reordered(grad, order_of_rows, subs).astype(jnp.float32)
         updated = adamw(master, moment_one, moment_two, grad)
         return (projected, columns, *updated)

time: 108 us -> 106 us (0.981)
  starting transfers between devices: 31.8 us -> 26.6 us
  waiting for transfers between devices: 32.7 us -> 35 us
  Pallas kernels: 35 us -> 36.3 us
    ppermute x10 -> x7, starting transfers between devices: 15.4 us -> 10 us  [swap_group(): return lax.ppermute(array, 'grp', [(i, i ^ mask) for i in range(groups)])]
    ppermute x10 -> x7, waiting for transfers between devices: 11.4 us -> 13.7 us  [swap_group(): return lax.ppermute(array, 'grp', [(i, i ^ mask) for i in range(groups)])]
    pallas_call x4 -> x5, Pallas kernels: 15.9 us -> 17.3 us  [the longest x2 9.89 us: product(): call(kernel, 'product', 0 if more else 2 * tokens * depth * width, jax.Sh...]
  transfers between devices with their start and end apart: 26 -> 23, of which waited for: 12 -> 12; matrix products, arithmetic and copies ran while one was open for 5% -> 5% of each run, Pallas kernels for 30% -> 31%
where the time goes in v3:
time: 106 us
  Pallas kernels  36.3 us (34%)
  waiting for transfers between devices  35 us (33%)
  starting transfers between devices  26.6 us (25%)
  local copies, waits for them, and re-layouts  3.88 us (4%)
  other arithmetic  3 us (3%)
  between operations  1.12 us (1%)
    ppermute x16, waiting for transfers between devices, swap(): return lax.ppermute(array, 'shard', [(i, i ^ mask) for i in range(shards)])  21.2 us
    ppermute x16, starting transfers between devices, swap(): return lax.ppermute(array, 'shard', [(i, i ^ mask) for i in range(shards)])  16.6 us
    ppermute x7, waiting for transfers between devices, swap_group(): return lax.ppermute(array, 'grp', [(i, i ^ mask) for i in range(groups)])  13.7 us
    ppermute x7, starting transfers between devices, swap_group(): return lax.ppermute(array, 'grp', [(i, i ^ mask) for i in range(groups)])  10 us
    pallas_call x2, Pallas kernels, product(): call(kernel, 'product', 0 if more else 2 * tokens * depth * width, jax.Sh...  9.89 us
    pallas_call x2, Pallas kernels, grad_columns(): call(kernel, 'grad_columns', 2 * tokens * depth * width, jax.ShapeDtypeSt...  9.8 us
    pallas_call x2, Pallas kernels, grad_blocks(): call(fill, 'grad_blocks', flops, outs, [SMEM] + [VMEM] * 4, (VMEM,) * len...  9.28 us
    pallas_call x3, Pallas kernels, stepped(): call(kernel, 'stepped', 512 * lines * width if so_far is None else 0, (ou...  7.36 us
  transfers between devices with their start and end apart: 23, of which 12 were waited for; matrix products, arithmetic and copies ran while one was open for 5% of the time, Pallas kernels for 31%

profile of v3, /device:TPU:0, one launch (start us, length us, event | category | flops | bytes accessed | tf_op | source)
XLA Modules:
  0.0 105.9 jit_solution(6521368179635939341)
XLA Ops:
  0.6 0.5 collective-permute-start
  1.2 0.1 collective-permute-start.1
  1.2 1.7 %select_convert_fusion = (bf16[256,1024]{1,0:T(8,128)(2,1)S(1)}, bf16[256,1024]{1,0:T(8,128)(2,1)S(1)}) fusion(f32[256,2048]{1,0:T(8,128)} %rest_2_.5, pred[]{:T(512)S(6)} %eq.4), kind=kLoop, calls=%fused_computation.2 | loop fusion | flops 524288 | bytes 2097153 | tf_op jit(solution)/shard_map/convert_element_type | solution.py:380
  2.9 3.0 %collective-permute-start.6 = (bf16[256,1024]{1,0:T(8,128)(2,1)S(1)}, bf16[256,1024]{1,0:T(8,128)(2,1)}, u32[]{:S(2)}, u32[]{:S(2)}) collective-permute-start(bf16[256,1024]{1,0:T(8,128)(2,1)S(1)} %get-tuple-element.85), channel_id=1, source_target_pairs={{0,4},{1,5},{2,6},{3,7},{4,0},{5,1},{6,2},{7,3},{8,12},{9,13},{10,... | collective-permute-start | bytes 1572872 | tf_op jit(solution)/shard_map/ppermute | solution.py:339
  6.0 1.5 %collective-permute-start.4 = (bf16[256,1024]{1,0:T(8,128)(2,1)S(1)}, bf16[256,1024]{1,0:T(8,128)(2,1)}, u32[]{:S(2)}, u32[]{:S(2)}) collective-permute-start(bf16[256,1024]{1,0:T(8,128)(2,1)S(1)} %get-tuple-element.86), channel_id=1, source_target_pairs={{0,2},{1,3},{2,0},{3,1},{4,6},{5,7},{6,4},{7,5},{8,10},{9,11},{10,... | collective-permute-start | bytes 1572872 | tf_op jit(solution)/shard_map/ppermute | solution.py:339
  7.4 0.1 pad_add_fusion.info_ref
  7.5 0.8 collective-permute-done.1.t1.cotangent_ref
  8.3 1.6 %copy-done.4 = bf16[512,2048]{1,0:T(8,128)(2,1)S(1)} copy-done((bf16[512,2048]{1,0:T(8,128)(2,1)S(1)}, bf16[512,2048]{1,0:T(8,128)(2,1)}, u32[]{:S(2)}) %copy-start.4) | copy-done | bytes 2097176
  9.9 4.6 %grad_blocks.2 = (bf16[512,640]{1,0:T(8,128)(2,1)S(1)}, bf16[512,640]{1,0:T(8,128)(2,1)S(1)}, bf16[512,384]{1,0:T(8,128)(2,1)S(1)}, bf16[512,384]{1,0:T(8,128)(2,1)S(1)}) custom-call(s32[2]{0:T(128)S(1)} %pad_add_fusion.info_ref, bf16[512,2048]{1,0:T(8,128)(2,1)S(1)} %copy-done.3, bf16[512,2048]{1,0:T(8,128)(2,1)} %collective-permute-done.c1.context_ref, ...), custom_call_target="tpu_custom_call" | custom-call | flops 34359738368 | tf_op jit(solution)/shard_map/grad_blocks/pallas_call | solution.py:116
  14.5 3.0 %collective-permute-start.2 = (bf16[512,640]{1,0:T(8,128)(2,1)S(1)}, bf16[512,640]{1,0:T(8,128)(2,1)S(1)}, u32[]{:S(2)}, u32[]{:S(2)}) collective-permute-start(bf16[512,640]{1,0:T(8,128)(2,1)S(1)} %get-tuple-element.49), channel_id=1, source_target_pairs={{0,4},{1,5},{2,6},{3,7},{4,0},{5,1},{6,2},{7,3},{8,12},{9,13},{10,... | collective-permute-start | bytes 1966088 | tf_op jit(solution)/shard_map/ppermute | solution.py:339
  17.5 1.5 %collective-permute-start.3 = (bf16[512,640]{1,0:T(8,128)(2,1)S(1)}, bf16[512,640]{1,0:T(8,128)(2,1)S(1)}, u32[]{:S(2)}, u32[]{:S(2)}) collective-permute-start(bf16[512,640]{1,0:T(8,128)(2,1)S(1)} %get-tuple-element.51), channel_id=1, source_target_pairs={{0,2},{1,3},{2,0},{3,1},{4,6},{5,7},{6,4},{7,5},{8,10},{9,11},{10,... | collective-permute-start | bytes 1966088 | tf_op jit(solution)/shard_map/ppermute | solution.py:339
  19.0 4.6 %grad_blocks.3 = (bf16[512,640]{1,0:T(8,128)(2,1)S(1)}, bf16[512,640]{1,0:T(8,128)(2,1)S(1)}, bf16[512,384]{1,0:T(8,128)(2,1)S(1)}, bf16[512,384]{1,0:T(8,128)(2,1)S(1)}) custom-call(s32[2]{0:T(128)S(1)} %pad_add_fusion.info_ref, bf16[512,2048]{1,0:T(8,128)(2,1)S(1)} %copy-done.3, bf16[512,2048]{1,0:T(8,128)(2,1)} %collective-permute-done.c1.context_ref, ...), custom_call_target="tpu_custom_call" | custom-call | flops 34359738368 | tf_op jit(solution)/shard_map/grad_blocks/pallas_call | solution.py:116
  23.6 0.6 collective-permute-start.5
  24.2 0.1 collective-permute-start.7
  24.3 1.1 %constant_dynamic-update-slice_fusion.1 = bf16[512,1024]{1,0:T(8,128)(2,1)S(1)} fusion(bf16[256,1024]{1,0:T(8,128)(2,1)} %collective-permute-done.4), kind=kLoop, calls=%fused_computation.23 | loop fusion | bytes 1048576
  25.4 1.1 %constant_dynamic-update-slice_fusion.rest_1_ = bf16[512,1024]{1,0:T(8,128)(2,1)S(1)} fusion(bf16[512,1024]{1,0:T(8,128)(2,1)S(1)} %constant_dynamic-update-slice_fusion.1, bf16[256,1024]{1,0:T(8,128)(2,1)} %collective-permute-done.6), kind=kLoop, calls=%fused_computation.22 | loop fusion | bytes 1048576 | tf_op jit(solution)/shard_map/concatenate | solution.py:398
  26.5 2.1 %collective-permute-start.12 = (bf16[512,1024]{1,0:T(8,128)(2,1)S(1)}, bf16[512,1024]{1,0:T(8,128)(2,1)S(1)}, u32[]{:S(2)}, u32[]{:S(2)}) collective-permute-start(bf16[512,1024]{1,0:T(8,128)(2,1)S(1)} %constant_dynamic-update-slice_fusion.rest_1_), channel_id=1, source_target_pairs={{0,8},{8,0},{16,24},{24,16},{1,9},{9,1},{17,25},{25,17},{2,10},{10... | collective-permute-start | bytes 3145736 | tf_op jit(solution)/shard_map/ppermute | solution.py:342
  28.6 6.5 %collective-permute-done.3 = bf16[512,640]{1,0:T(8,128)(2,1)S(1)} collective-permute-done((bf16[512,640]{1,0:T(8,128)(2,1)S(1)}, bf16[512,640]{1,0:T(8,128)(2,1)S(1)}, u32[]{:S(2)}, u32[]{:S(2)}) %collective-permute-start.3) | collective-permute-done | bytes 655392 | tf_op jit(solution)/shard_map/ppermute | solution.py:339
  35.1 0.2 add_convert_fusion.1
  35.3 0.0 copy-start
  35.3 0.1 collective-permute-start.11
  35.4 0.2 add_convert_fusion
  35.6 2.0 %collective-permute-start.10 = (bf16[256,640]{1,0:T(8,128)(2,1)S(1)}, bf16[256,640]{1,0:T(8,128)(2,1)S(1)}, u32[]{:S(2)}, u32[]{:S(2)}) collective-permute-start(bf16[256,640]{1,0:T(8,128)(2,1)S(1)} %slice.57), channel_id=1, source_target_pairs={{0,2},{1,3},{2,0},{3,1},{4,6},{5,7},{6,4},{7,5},{8,10},{9,11},{10,... | collective-permute-start | bytes 983048 | tf_op jit(solution)/shard_map/ppermute | solution.py:339
  37.7 0.1 convert_element_type.133.rest_0_
  37.8 6.4 %collective-permute-done.5.rest_3_ = bf16[256,1024]{1,0:T(8,128)(2,1)S(1)} collective-permute-done((bf16[256,1024]{1,0:T(8,128)(2,1)}, bf16[256,1024]{1,0:T(8,128)(2,1)S(1)}, u32[]{:S(2)}, u32[]{:S(2)}) %collective-permute-start.5) | collective-permute-done | bytes 524320 | tf_op jit(solution)/shard_map/ppermute | solution.py:339
  44.2 2.1 %collective-permute-done.7.rest_4_ = bf16[256,1024]{1,0:T(8,128)(2,1)S(1)} collective-permute-done((bf16[256,1024]{1,0:T(8,128)(2,1)}, bf16[256,1024]{1,0:T(8,128)(2,1)S(1)}, u32[]{:S(2)}, u32[]{:S(2)}) %collective-permute-start.7) | collective-permute-done | bytes 524320 | tf_op jit(solution)/shard_map/ppermute | solution.py:339
  46.3 0.0 collective-permute-start.8
  46.4 1.9 %collective-permute-start.9 = (bf16[512,384]{1,0:T(8,128)(2,1)S(1)}, bf16[512,384]{1,0:T(8,128)(2,1)S(1)}, u32[]{:S(2)}, u32[]{:S(2)}) collective-permute-start(bf16[512,384]{1,0:T(8,128)(2,1)S(1)} %get-tuple-element.59), channel_id=1, source_target_pairs={{0,2},{1,3},{2,0},{3,1},{4,6},{5,7},{6,4},{7,5},{8,10},{9,11},{10,... | collective-permute-start | bytes 1179656 | tf_op jit(solution)/shard_map/ppermute | solution.py:339
  48.3 2.9 %collective-permute-done.11 = bf16[256,640]{1,0:T(8,128)(2,1)S(1)} collective-permute-done((bf16[256,640]{1,0:T(8,128)(2,1)S(1)}, bf16[256,640]{1,0:T(8,128)(2,1)S(1)}, u32[]{:S(2)}, u32[]{:S(2)}) %collective-permute-start.11) | collective-permute-done | bytes 327712 | tf_op jit(solution)/shard_map/ppermute | solution.py:339
  51.3 0.1 add_convert_fusion.7
  51.4 2.0 %collective-permute-done.10 = bf16[256,640]{1,0:T(8,128)(2,1)S(1)} collective-permute-done((bf16[256,640]{1,0:T(8,128)(2,1)S(1)}, bf16[256,640]{1,0:T(8,128)(2,1)S(1)}, u32[]{:S(2)}, u32[]{:S(2)}) %collective-permute-start.10) | collective-permute-done | bytes 327712 | tf_op jit(solution)/shard_map/ppermute | solution.py:339
  53.4 0.1 add_convert_fusion.6
  53.5 1.6 %collective-permute-start.15 = (bf16[128,1280]{1,0:T(8,128)(2,1)S(1)}, bf16[128,1280]{1,0:T(8,128)(2,1)S(1)}, u32[]{:S(2)}, u32[]{:S(2)}) collective-permute-start(bf16[128,1280]{1,0:T(8,128)(2,1)S(1)} %pad_maximum_fusion), channel_id=1, source_target_pairs={{0,8},{8,0},{16,24},{24,16},{1,9},{9,1},{17,25},{25,17},{2,10},{10... | collective-permute-start | bytes 983048 | tf_op jit(solution)/shard_map/ppermute | solution.py:342
  55.1 5.0 %product.2 = bf16[512,2048]{1,0:T(8,128)(2,1)S(1)} custom-call(s32[2]{0:T(128)S(1)} %pad_add_fusion.info_ref, bf16[512,2048]{1,0:T(8,128)(2,1)} %collective-permute-done.c1.context_ref, bf16[256,2048]{1,0:T(8,128)(2,1)S(1)} %convert_element_type.133.rest_0_, bf16[512,1024]{1,0:T(8,128)(2,1)S(1)} %constant_dynamic-update-slice_fusion.rest_1_, ...), custom_call_target="tpu_custom_call" | custom-call | flops 34359738368 | tf_op jit(solution)/shard_map/product/pallas_call | solution.py:201
  60.2 0.1 collective-permute-start.16
  60.3 0.4 collective-permute-done.9
  60.7 0.1 add_convert_fusion.3
  60.8 0.1 add_convert_fusion.2
  60.9 0.4 collective-permute-start.14
  61.4 1.6 %collective-permute-start.13 = (bf16[256,384]{1,0:T(8,128)(2,1)S(1)}, bf16[256,384]{1,0:T(8,128)(2,1)S(1)}, u32[]{:S(2)}, u32[]{:S(2)}) collective-permute-start(bf16[256,384]{1,0:T(8,128)(2,1)S(1)} %slice.61), channel_id=1, source_target_pairs={{0,2},{1,3},{2,0},{3,1},{4,6},{5,7},{6,4},{7,5},{8,10},{9,11},{10,... | collective-permute-start | bytes 589832 | tf_op jit(solution)/shard_map/ppermute | solution.py:339
  63.0 0.1 add_convert_fusion.5
  63.1 2.7 %collective-permute-start.17 = (bf16[128,1280]{1,0:T(8,128)(2,1)S(1)}, bf16[128,1280]{1,0:T(8,128)(2,1)S(1)}, u32[]{:S(2)}, u32[]{:S(2)}) collective-permute-start(bf16[128,1280]{1,0:T(8,128)(2,1)S(1)} %add_convert_fusion.5), channel_id=1, source_target_pairs={{0,16},{8,24},{16,0},{24,8},{1,17},{9,25},{17,1},{25,9},{2,18},{10... | collective-permute-start | bytes 983048 | tf_op jit(solution)/shard_map/ppermute | solution.py:342
  65.8 5.0 %grad_columns.2 = bf16[512,1024]{1,0:T(8,128)(2,1)S(1)} custom-call(s32[2]{0:T(128)S(1)} %pad_add_fusion.info_ref, bf16[512,2048]{1,0:T(8,128)(2,1)} %collective-permute-done.1.t1.cotangent_ref, bf16[256,2048]{1,0:T(8,128)(2,1)S(1)} %convert_element_type.133.rest_0_, bf16[512,1024]{1,0:T(8,128)(2,1)S(1)} %constant_dynamic-update-slice_fusion.rest_1_, ...), custom_call_target="tpu_custom_call" | custom-call | flops 34359738368 | tf_op jit(solution)/shard_map/grad_columns/pallas_call | solution.py:260
  70.7 0.1 collective-permute-start.19
  70.8 0.1 add_convert_fusion.11
  70.9 0.1 add_convert_fusion.10
  71.0 0.0 copy-start.1
  71.0 0.0 copy-start.2
  71.0 1.6 %collective-permute-start.18 = (bf16[128,768]{1,0:T(8,128)(2,1)S(1)}, bf16[128,768]{1,0:T(8,128)(2,1)S(1)}, u32[]{:S(2)}, u32[]{:S(2)}) collective-permute-start(bf16[128,768]{1,0:T(8,128)(2,1)S(1)} %pad_maximum_fusion.1), channel_id=1, source_target_pairs={{0,8},{8,0},{16,24},{24,16},{1,9},{9,1},{17,25},{25,17},{2,10},{10... | collective-permute-start | bytes 589832 | tf_op jit(solution)/shard_map/ppermute | solution.py:342
  72.7 4.8 %product.3 = bf16[512,2048]{1,0:T(8,128)(2,1)} custom-call(s32[2]{0:T(128)S(1)} %pad_add_fusion.info_ref, bf16[512,2048]{1,0:T(8,128)(2,1)S(1)} %copy-done.3, bf16[256,2048]{1,0:T(8,128)(2,1)S(1)} %convert_element_type.133.rest_0_, bf16[512,1024]{1,0:T(8,128)(2,1)S(1)} %constant_dynamic-update-slice_fusion.rest_1_, ...), custom_call_target="tpu_custom_call" | custom-call | tf_op jit(solution)/shard_map/product/pallas_call | solution.py:201
  77.5 2.8 %collective-permute-done.17 = bf16[128,1280]{1,0:T(8,128)(2,1)S(1)} collective-permute-done((bf16[128,1280]{1,0:T(8,128)(2,1)S(1)}, bf16[128,1280]{1,0:T(8,128)(2,1)S(1)}, u32[]{:S(2)}, u32[]{:S(2)}) %collective-permute-start.17) | collective-permute-done | bytes 327712 | tf_op jit(solution)/shard_map/ppermute | solution.py:342
  80.3 0.1 add_convert_fusion.4.rest_0_
  80.3 4.0 %collective-permute-done.18 = bf16[128,768]{1,0:T(8,128)(2,1)S(1)} collective-permute-done((bf16[128,768]{1,0:T(8,128)(2,1)S(1)}, bf16[128,768]{1,0:T(8,128)(2,1)S(1)}, u32[]{:S(2)}, u32[]{:S(2)}) %collective-permute-start.18) | collective-permute-done | bytes 196640 | tf_op jit(solution)/shard_map/ppermute | solution.py:342
  84.4 0.1 add_convert_fusion.9
  84.4 0.1 collective-permute-start.21
  84.5 1.9 %collective-permute-start.20 = (bf16[128,1280]{1,0:T(8,128)(2,1)S(1)}, bf16[128,1280]{1,0:T(8,128)(2,1)S(1)}, u32[]{:S(2)}, u32[]{:S(2)}) collective-permute-start(bf16[128,1280]{1,0:T(8,128)(2,1)S(1)} %add_convert_fusion.4.rest_0_), channel_id=1, source_target_pairs={{0,8},{8,0},{16,24},{24,16},{1,9},{9,1},{17,25},{25,17},{2,10},{10... | collective-permute-start | bytes 983048 | tf_op jit(solution)/shard_map/ppermute | solution.py:342
  86.4 2.4 %stepped.3 = (f32[256,2048]{1,0:T(8,128)}, f32[256,2048]{1,0:T(8,128)}, f32[256,2048]{1,0:T(8,128)}) custom-call(s32[2]{0:T(128)S(1)} %pad_add_fusion.info_ref, bf16[128,1280]{1,0:T(8,128)(2,1)S(1)} %add_convert_fusion.4.rest_0_, f32[256,2048]{1,0:T(8,128)S(1)} %copy-done, f32[256,2048]{1,0:T(8,128)S(1)} %copy-done.1, f32[256,2048]{1,0:T(8,128)S(1)} %copy-done.2), custom_call_target="tpu_custom_call" | custom-call | flops 2147483648 | tf_op jit(solution)/shard_map/stepped/pallas_call | solution.py:309
  88.8 4.8 %grad_columns.3 = bf16[512,2048]{1,0:T(8,128)(2,1)} custom-call(s32[2]{0:T(128)S(1)} %pad_add_fusion.info_ref, bf16[512,2048]{1,0:T(8,128)(2,1)S(1)} %copy-done.5, bf16[256,2048]{1,0:T(8,128)(2,1)S(1)} %convert_element_type.133.rest_0_, bf16[512,1024]{1,0:T(8,128)(2,1)S(1)} %constant_dynamic-update-slice_fusion.rest_1_, ...), custom_call_target="tpu_custom_call" | custom-call | flops 34359738368 | tf_op jit(solution)/shard_map/grad_columns/pallas_call | solution.py:260
  93.6 2.0 %collective-permute-done.21 = bf16[128,768]{1,0:T(8,128)(2,1)S(1)} collective-permute-done((bf16[128,768]{1,0:T(8,128)(2,1)S(1)}, bf16[128,768]{1,0:T(8,128)(2,1)S(1)}, u32[]{:S(2)}, u32[]{:S(2)}) %collective-permute-start.21) | collective-permute-done | bytes 196640 | tf_op jit(solution)/shard_map/ppermute | solution.py:342
  95.6 0.1 collective-permute-start.22
  95.7 2.0 %stepped.4 = (f32[256,2048]{1,0:T(8,128)}, f32[256,2048]{1,0:T(8,128)}, f32[256,2048]{1,0:T(8,128)}) custom-call(s32[2]{0:T(128)S(1)} %pad_add_fusion.info_ref, bf16[128,768]{1,0:T(8,128)(2,1)S(1)} %add_convert_fusion.8.rest_0_, f32[256,2048]{1,0:T(8,128)S(1)} %copy-done, ...), custom_call_target="tpu_custom_call", output_to_operand_aliasing={{0}: (5, {}), {1}: (6, {}), {2}: (7, {})} | custom-call | tf_op jit(solution)/shard_map/stepped/pallas_call | solution.py:309
  97.7 0.9 collective-permute-done.20.rest_0_
  98.6 4.1 %collective-permute-done.22.rest_1_ = bf16[128,768]{1,0:T(8,128)(2,1)S(1)} collective-permute-done((bf16[128,768]{1,0:T(8,128)(2,1)S(1)}, bf16[128,768]{1,0:T(8,128)(2,1)S(1)}, u32[]{:S(2)}, u32[]{:S(2)}) %collective-permute-start.22) | collective-permute-done | bytes 196640 | tf_op jit(solution)/shard_map/ppermute | solution.py:342
  102.7 3.0 %stepped.5 = (f32[256,2048]{1,0:T(8,128)}, f32[256,2048]{1,0:T(8,128)}, f32[256,2048]{1,0:T(8,128)}) custom-call(s32[2]{0:T(128)S(1)} %pad_add_fusion.info_ref, bf16[128,1280]{1,0:T(8,128)(2,1)S(1)} %collective-permute-done.20.rest_0_, ...), custom_call_target="tpu_custom_call", output_to_operand_aliasing={{0}: (6, {}), {1}: (7, {}), {2}: (8, {})} | custom-call | tf_op jit(solution)/shard_map/stepped/pallas_call | solution.py:309
  (26 shorter events, 0.2 us)
Async XLA Ops:
  0.6 7.7 %copy-start.3 = (bf16[512,2048]{1,0:T(8,128)(2,1)S(1)}, bf16[512,2048]{1,0:T(8,128)(2,1)}, u32[]{:S(2)}) copy-start(bf16[512,2048]{1,0:T(8,128)(2,1)} %context_ref) | copy-start | bytes 6291460
  0.6 6.9 %collective-permute-start = (bf16[512,2048]{1,0:T(8,128)(2,1)}, bf16[512,2048]{1,0:T(8,128)(2,1)}, u32[]{:S(2)}, u32[]{:S(2)}) collective-permute-start(bf16[512,2048]{1,0:T(8,128)(2,1)} %context_ref), channel_id=1, source_target_pairs={{0,1},{1,0},{2,3},{3,2},{4,5},{5,4},{6,7},{7,6},{8,9},{9,8},{10,11... | collective-permute-start | bytes 6291464 | tf_op jit(solution)/shard_map/ppermute | solution.py:339
  1.2 7.1 %collective-permute-start.1 = (bf16[512,2048]{1,0:T(8,128)(2,1)}, bf16[512,2048]{1,0:T(8,128)(2,1)}, u32[]{:S(2)}, u32[]{:S(2)}) collective-permute-start(bf16[512,2048]{1,0:T(8,128)(2,1)} %cotangent_ref), channel_id=1, source_target_pairs={{0,1},{1,0},{2,3},{3,2},{4,5},{5,4},{6,7},{7,6},{8,9},{9,8},{10,11... | collective-permute-start | bytes 6291464 | tf_op jit(solution)/shard_map/ppermute | solution.py:339
  2.9 20.7 %collective-permute-start.6 = (bf16[256,1024]{1,0:T(8,128)(2,1)S(1)}, bf16[256,1024]{1,0:T(8,128)(2,1)}, u32[]{:S(2)}, u32[]{:S(2)}) collective-permute-start(bf16[256,1024]{1,0:T(8,128)(2,1)S(1)} %get-tuple-element.85), channel_id=1, source_target_pairs={{0,4},{1,5},{2,6},{3,7},{4,0},{5,1},{6,2},{7,3},{8,12},{9,13},{10,... | collective-permute-start | bytes 1572872 | tf_op jit(solution)/shard_map/ppermute | solution.py:339
  6.0 17.7 %collective-permute-start.4 = (bf16[256,1024]{1,0:T(8,128)(2,1)S(1)}, bf16[256,1024]{1,0:T(8,128)(2,1)}, u32[]{:S(2)}, u32[]{:S(2)}) collective-permute-start(bf16[256,1024]{1,0:T(8,128)(2,1)S(1)} %get-tuple-element.86), channel_id=1, source_target_pairs={{0,2},{1,3},{2,0},{3,1},{4,6},{5,7},{6,4},{7,5},{8,10},{9,11},{10,... | collective-permute-start | bytes 1572872 | tf_op jit(solution)/shard_map/ppermute | solution.py:339
  8.3 1.6 %copy-start.4 = (bf16[512,2048]{1,0:T(8,128)(2,1)S(1)}, bf16[512,2048]{1,0:T(8,128)(2,1)}, u32[]{:S(2)}) copy-start(bf16[512,2048]{1,0:T(8,128)(2,1)} %cotangent_ref) | copy-start | bytes 6291460
  14.5 20.8 %collective-permute-start.2 = (bf16[512,640]{1,0:T(8,128)(2,1)S(1)}, bf16[512,640]{1,0:T(8,128)(2,1)S(1)}, u32[]{:S(2)}, u32[]{:S(2)}) collective-permute-start(bf16[512,640]{1,0:T(8,128)(2,1)S(1)} %get-tuple-element.49), channel_id=1, source_target_pairs={{0,4},{1,5},{2,6},{3,7},{4,0},{5,1},{6,2},{7,3},{8,12},{9,13},{10,... | collective-permute-start | bytes 1966088 | tf_op jit(solution)/shard_map/ppermute | solution.py:339
  17.5 17.6 %collective-permute-start.3 = (bf16[512,640]{1,0:T(8,128)(2,1)S(1)}, bf16[512,640]{1,0:T(8,128)(2,1)S(1)}, u32[]{:S(2)}, u32[]{:S(2)}) collective-permute-start(bf16[512,640]{1,0:T(8,128)(2,1)S(1)} %get-tuple-element.51), channel_id=1, source_target_pairs={{0,2},{1,3},{2,0},{3,1},{4,6},{5,7},{6,4},{7,5},{8,10},{9,11},{10,... | collective-permute-start | bytes 1966088 | tf_op jit(solution)/shard_map/ppermute | solution.py:339
  23.6 20.6 %collective-permute-start.5 = (bf16[256,1024]{1,0:T(8,128)(2,1)}, bf16[256,1024]{1,0:T(8,128)(2,1)S(1)}, u32[]{:S(2)}, u32[]{:S(2)}) collective-permute-start(bf16[256,1024]{1,0:T(8,128)(2,1)} %collective-permute-done.4), channel_id=1, source_target_pairs={{0,4},{1,5},{2,6},{3,7},{4,0},{5,1},{6,2},{7,3},{8,12},{9,13},{10,... | collective-permute-start | bytes 1572872 | tf_op jit(solution)/shard_map/ppermute | solution.py:339
  24.2 22.1 %collective-permute-start.7 = (bf16[256,1024]{1,0:T(8,128)(2,1)}, bf16[256,1024]{1,0:T(8,128)(2,1)S(1)}, u32[]{:S(2)}, u32[]{:S(2)}) collective-permute-start(bf16[256,1024]{1,0:T(8,128)(2,1)} %collective-permute-done.6), channel_id=1, source_target_pairs={{0,2},{1,3},{2,0},{3,1},{4,6},{5,7},{6,4},{7,5},{8,10},{9,11},{10,... | collective-permute-start | bytes 1572872 | tf_op jit(solution)/shard_map/ppermute | solution.py:339
  26.5 28.6 %collective-permute-start.12 = (bf16[512,1024]{1,0:T(8,128)(2,1)S(1)}, bf16[512,1024]{1,0:T(8,128)(2,1)S(1)}, u32[]{:S(2)}, u32[]{:S(2)}) collective-permute-start(bf16[512,1024]{1,0:T(8,128)(2,1)S(1)} %constant_dynamic-update-slice_fusion.rest_1_), channel_id=1, source_target_pairs={{0,8},{8,0},{16,24},{24,16},{1,9},{9,1},{17,25},{25,17},{2,10},{10... | collective-permute-start | bytes 3145736 | tf_op jit(solution)/shard_map/ppermute | solution.py:342
  35.3 2.4 %copy-start = (f32[256,2048]{1,0:T(8,128)S(1)}, f32[256,2048]{1,0:T(8,128)}, u32[]{:S(2)}) copy-start(f32[256,2048]{1,0:T(8,128)} %rest_2_.5) | copy-start | bytes 6291460
  35.3 15.9 %collective-permute-start.11 = (bf16[256,640]{1,0:T(8,128)(2,1)S(1)}, bf16[256,640]{1,0:T(8,128)(2,1)S(1)}, u32[]{:S(2)}, u32[]{:S(2)}) collective-permute-start(bf16[256,640]{1,0:T(8,128)(2,1)S(1)} %slice.59), channel_id=1, source_target_pairs={{0,4},{1,5},{2,6},{3,7},{4,0},{5,1},{6,2},{7,3},{8,12},{9,13},{10,... | collective-permute-start | bytes 983048 | tf_op jit(solution)/shard_map/ppermute | solution.py:339
  35.6 17.7 %collective-permute-start.10 = (bf16[256,640]{1,0:T(8,128)(2,1)S(1)}, bf16[256,640]{1,0:T(8,128)(2,1)S(1)}, u32[]{:S(2)}, u32[]{:S(2)}) collective-permute-start(bf16[256,640]{1,0:T(8,128)(2,1)S(1)} %slice.57), channel_id=1, source_target_pairs={{0,2},{1,3},{2,0},{3,1},{4,6},{5,7},{6,4},{7,5},{8,10},{9,11},{10,... | collective-permute-start | bytes 983048 | tf_op jit(solution)/shard_map/ppermute | solution.py:339
  46.3 14.5 %collective-permute-start.8 = (bf16[512,384]{1,0:T(8,128)(2,1)S(1)}, bf16[512,384]{1,0:T(8,128)(2,1)S(1)}, u32[]{:S(2)}, u32[]{:S(2)}) collective-permute-start(bf16[512,384]{1,0:T(8,128)(2,1)S(1)} %get-tuple-element.56), channel_id=1, source_target_pairs={{0,4},{1,5},{2,6},{3,7},{4,0},{5,1},{6,2},{7,3},{8,12},{9,13},{10,... | collective-permute-start | bytes 1179656 | tf_op jit(solution)/shard_map/ppermute | solution.py:339
  46.4 14.3 %collective-permute-start.9 = (bf16[512,384]{1,0:T(8,128)(2,1)S(1)}, bf16[512,384]{1,0:T(8,128)(2,1)S(1)}, u32[]{:S(2)}, u32[]{:S(2)}) collective-permute-start(bf16[512,384]{1,0:T(8,128)(2,1)S(1)} %get-tuple-element.59), channel_id=1, source_target_pairs={{0,2},{1,3},{2,0},{3,1},{4,6},{5,7},{6,4},{7,5},{8,10},{9,11},{10,... | collective-permute-start | bytes 1179656 | tf_op jit(solution)/shard_map/ppermute | solution.py:339
  53.5 9.5 %collective-permute-start.15 = (bf16[128,1280]{1,0:T(8,128)(2,1)S(1)}, bf16[128,1280]{1,0:T(8,128)(2,1)S(1)}, u32[]{:S(2)}, u32[]{:S(2)}) collective-permute-start(bf16[128,1280]{1,0:T(8,128)(2,1)S(1)} %pad_maximum_fusion), channel_id=1, source_target_pairs={{0,8},{8,0},{16,24},{24,16},{1,9},{9,1},{17,25},{25,17},{2,10},{10... | collective-permute-start | bytes 983048 | tf_op jit(solution)/shard_map/ppermute | solution.py:342
  60.2 12.5 %collective-permute-start.16 = (bf16[512,2048]{1,0:T(8,128)(2,1)S(1)}, bf16[512,2048]{1,0:T(8,128)(2,1)S(1)}, u32[]{:S(2)}, u32[]{:S(2)}) collective-permute-start(bf16[512,2048]{1,0:T(8,128)(2,1)S(1)} %product.2), channel_id=1, source_target_pairs={{0,1},{1,0},{2,3},{3,2},{4,5},{5,4},{6,7},{7,6},{8,9},{9,8},{10,11... | collective-permute-start | bytes 6291464 | tf_op jit(solution)/shard_map/ppermute | solution.py:339
  60.9 9.9 %collective-permute-start.14 = (bf16[256,384]{1,0:T(8,128)(2,1)S(1)}, bf16[256,384]{1,0:T(8,128)(2,1)S(1)}, u32[]{:S(2)}, u32[]{:S(2)}) collective-permute-start(bf16[256,384]{1,0:T(8,128)(2,1)S(1)} %slice.63), channel_id=1, source_target_pairs={{0,4},{1,5},{2,6},{3,7},{4,0},{5,1},{6,2},{7,3},{8,12},{9,13},{10,... | collective-permute-start | bytes 589832 | tf_op jit(solution)/shard_map/ppermute | solution.py:339
  61.4 9.5 %collective-permute-start.13 = (bf16[256,384]{1,0:T(8,128)(2,1)S(1)}, bf16[256,384]{1,0:T(8,128)(2,1)S(1)}, u32[]{:S(2)}, u32[]{:S(2)}) collective-permute-start(bf16[256,384]{1,0:T(8,128)(2,1)S(1)} %slice.61), channel_id=1, source_target_pairs={{0,2},{1,3},{2,0},{3,1},{4,6},{5,7},{6,4},{7,5},{8,10},{9,11},{10,... | collective-permute-start | bytes 589832 | tf_op jit(solution)/shard_map/ppermute | solution.py:339
  63.1 17.2 %collective-permute-start.17 = (bf16[128,1280]{1,0:T(8,128)(2,1)S(1)}, bf16[128,1280]{1,0:T(8,128)(2,1)S(1)}, u32[]{:S(2)}, u32[]{:S(2)}) collective-permute-start(bf16[128,1280]{1,0:T(8,128)(2,1)S(1)} %add_convert_fusion.5), channel_id=1, source_target_pairs={{0,16},{8,24},{16,0},{24,8},{1,17},{9,25},{17,1},{25,9},{2,18},{10... | collective-permute-start | bytes 983048 | tf_op jit(solution)/shard_map/ppermute | solution.py:342
  70.7 18.0 %collective-permute-start.19 = (bf16[512,1024]{1,0:T(8,128)(2,1)S(1)}, bf16[512,1024]{1,0:T(8,128)(2,1)S(1)}, u32[]{:S(2)}, u32[]{:S(2)}) collective-permute-start(bf16[512,1024]{1,0:T(8,128)(2,1)S(1)} %grad_columns.2), channel_id=1, source_target_pairs={{0,1},{1,0},{2,3},{3,2},{4,5},{5,4},{6,7},{7,6},{8,9},{9,8},{10,11... | collective-permute-start | bytes 3145736 | tf_op jit(solution)/shard_map/ppermute | solution.py:339
  71.0 15.4 %copy-start.1 = (f32[256,2048]{1,0:T(8,128)S(1)}, f32[256,2048]{1,0:T(8,128)}, u32[]{:S(2)}) copy-start(f32[256,2048]{1,0:T(8,128)} %rest_3_.5) | copy-start | bytes 6291460
  71.0 15.4 %copy-start.2 = (f32[256,2048]{1,0:T(8,128)S(1)}, f32[256,2048]{1,0:T(8,128)}, u32[]{:S(2)}) copy-start(f32[256,2048]{1,0:T(8,128)} %rest_4_.1) | copy-start | bytes 6291460
  71.0 13.4 %collective-permute-start.18 = (bf16[128,768]{1,0:T(8,128)(2,1)S(1)}, bf16[128,768]{1,0:T(8,128)(2,1)S(1)}, u32[]{:S(2)}, u32[]{:S(2)}) collective-permute-start(bf16[128,768]{1,0:T(8,128)(2,1)S(1)} %pad_maximum_fusion.1), channel_id=1, source_target_pairs={{0,8},{8,0},{16,24},{24,16},{1,9},{9,1},{17,25},{25,17},{2,10},{10... | collective-permute-start | bytes 589832 | tf_op jit(solution)/shard_map/ppermute | solution.py:342
  84.4 4.3 %copy-start.5 = (bf16[512,2048]{1,0:T(8,128)(2,1)S(1)}, bf16[512,2048]{1,0:T(8,128)(2,1)}, u32[]{:S(2)}) copy-start(bf16[512,2048]{1,0:T(8,128)(2,1)} %cotangent_ref) | copy-start | bytes 6291460
  84.4 11.1 %collective-permute-start.21 = (bf16[128,768]{1,0:T(8,128)(2,1)S(1)}, bf16[128,768]{1,0:T(8,128)(2,1)S(1)}, u32[]{:S(2)}, u32[]{:S(2)}) collective-permute-start(bf16[128,768]{1,0:T(8,128)(2,1)S(1)} %add_convert_fusion.9), channel_id=1, source_target_pairs={{0,16},{8,24},{16,0},{24,8},{1,17},{9,25},{17,1},{25,9},{2,18},{10... | collective-permute-start | bytes 589832 | tf_op jit(solution)/shard_map/ppermute | solution.py:342
  84.5 14.1 %collective-permute-start.20 = (bf16[128,1280]{1,0:T(8,128)(2,1)S(1)}, bf16[128,1280]{1,0:T(8,128)(2,1)S(1)}, u32[]{:S(2)}, u32[]{:S(2)}) collective-permute-start(bf16[128,1280]{1,0:T(8,128)(2,1)S(1)} %add_convert_fusion.4.rest_0_), channel_id=1, source_target_pairs={{0,8},{8,0},{16,24},{24,16},{1,9},{9,1},{17,25},{25,17},{2,10},{10... | collective-permute-start | bytes 983048 | tf_op jit(solution)/shard_map/ppermute | solution.py:342
  95.6 7.1 %collective-permute-start.22 = (bf16[128,768]{1,0:T(8,128)(2,1)S(1)}, bf16[128,768]{1,0:T(8,128)(2,1)S(1)}, u32[]{:S(2)}, u32[]{:S(2)}) collective-permute-start(bf16[128,768]{1,0:T(8,128)(2,1)S(1)} %add_convert_fusion.8.rest_0_), channel_id=1, source_target_pairs={{0,8},{8,0},{16,24},{24,16},{1,9},{9,1},{17,25},{25,17},{2,10},{10... | collective-permute-start | bytes 589832 | tf_op jit(solution)/shard_map/ppermute | solution.py:342

commit v4 on v3

--- a/solution.py
+++ b/solution.py
@@ -478,8 +478,8 @@
         advance("rest")
         if tiled:
             so_far = stepped(info, 0, columns_of(summed["rest"], 1), state, so_far)
-            grads = columns_of(come["first"], 0) + columns_of(come["rest"], 1)
-            return (projected, columns, *stepped(info, 1, grads, state, so_far))
+            so_far = stepped(info, 1, columns_of(come["first"], 0), state, so_far)
+            return (projected, columns, *stepped(info, 1, columns_of(come["rest"], 1), state, so_far))
         finish("first")
         finish("rest")
         named_sizes = list(zip(("first", "rest"), chunk_sizes))

time: 106 us -> 105 us (level)
  waiting for transfers between devices: 35 us -> 32.6 us
  Pallas kernels: 36.3 us -> 37.7 us
    ppermute x7, waiting for transfers between devices: 13.7 us -> 11.4 us  [swap_group(): return lax.ppermute(array, 'grp', [(i, i ^ mask) for i in range(groups)])]
    pallas_call x3 -> x4, Pallas kernels: 7.36 us -> 8.7 us  [stepped(): call(kernel, 'stepped', 512 * lines * width if so_far is None else 0, (ou...]
  transfers between devices with their start and end apart: 23 -> 23, of which waited for: 12 -> 12; matrix products, arithmetic and copies ran while one was open for 5% -> 5% of each run, Pallas kernels for 31% -> 34%
where the time goes in v4:
time: 105 us
  Pallas kernels  37.7 us (36%)
  waiting for transfers between devices  32.6 us (31%)
  starting transfers between devices  26.6 us (25%)
  local copies, waits for them, and re-layouts  3.88 us (4%)
  other arithmetic  3 us (3%)
  between operations  1.13 us (1%)
    ppermute x16, waiting for transfers between devices, swap(): return lax.ppermute(array, 'shard', [(i, i ^ mask) for i in range(shards)])  21.2 us
    ppermute x16, starting transfers between devices, swap(): return lax.ppermute(array, 'shard', [(i, i ^ mask) for i in range(shards)])  16.6 us
    ppermute x7, waiting for transfers between devices, swap_group(): return lax.ppermute(array, 'grp', [(i, i ^ mask) for i in range(groups)])  11.4 us
    ppermute x7, starting transfers between devices, swap_group(): return lax.ppermute(array, 'grp', [(i, i ^ mask) for i in range(groups)])  10 us
    pallas_call x2, Pallas kernels, product(): call(kernel, 'product', 0 if more else 2 * tokens * depth * width, jax.Sh...  9.89 us
    pallas_call x2, Pallas kernels, grad_columns(): call(kernel, 'grad_columns', 2 * tokens * depth * width, jax.ShapeDtypeSt...  9.8 us
    pallas_call x2, Pallas kernels, grad_blocks(): call(fill, 'grad_blocks', flops, outs, [SMEM] + [VMEM] * 4, (VMEM,) * len...  9.28 us
    pallas_call x4, Pallas kernels, stepped(): call(kernel, 'stepped', 512 * lines * width if so_far is None else 0, (ou...  8.7 us
  transfers between devices with their start and end apart: 23, of which 12 were waited for; matrix products, arithmetic and copies ran while one was open for 5% of the time, Pallas kernels for 34%

profile of v4, /device:TPU:0, one launch (start us, length us, event | category | flops | bytes accessed | tf_op | source)
XLA Modules:
  0.0 104.9 jit_solution(8652570652531870971)
XLA Ops:
  0.6 0.5 collective-permute-start
  1.2 0.1 collective-permute-start.1
  1.2 1.7 %select_convert_fusion = (bf16[256,1024]{1,0:T(8,128)(2,1)S(1)}, bf16[256,1024]{1,0:T(8,128)(2,1)S(1)}) fusion(f32[256,2048]{1,0:T(8,128)} %rest_1_.6, pred[]{:T(512)S(6)} %eq.4), kind=kLoop, calls=%fused_computation.2 | loop fusion | flops 524288 | bytes 2097153 | tf_op jit(solution)/shard_map/convert_element_type | solution.py:380
  2.9 3.0 %collective-permute-start.6 = (bf16[256,1024]{1,0:T(8,128)(2,1)S(1)}, bf16[256,1024]{1,0:T(8,128)(2,1)}, u32[]{:S(2)}, u32[]{:S(2)}) collective-permute-start(bf16[256,1024]{1,0:T(8,128)(2,1)S(1)} %get-tuple-element.91), channel_id=1, source_target_pairs={{0,4},{1,5},{2,6},{3,7},{4,0},{5,1},{6,2},{7,3},{8,12},{9,13},{10,... | collective-permute-start | bytes 1572872 | tf_op jit(solution)/shard_map/ppermute | solution.py:339
  6.0 1.5 %collective-permute-start.4 = (bf16[256,1024]{1,0:T(8,128)(2,1)S(1)}, bf16[256,1024]{1,0:T(8,128)(2,1)}, u32[]{:S(2)}, u32[]{:S(2)}) collective-permute-start(bf16[256,1024]{1,0:T(8,128)(2,1)S(1)} %get-tuple-element.92), channel_id=1, source_target_pairs={{0,2},{1,3},{2,0},{3,1},{4,6},{5,7},{6,4},{7,5},{8,10},{9,11},{10,... | collective-permute-start | bytes 1572872 | tf_op jit(solution)/shard_map/ppermute | solution.py:339
  7.4 0.1 pad_add_fusion.info_ref
  7.5 0.8 collective-permute-done.1.t1.cotangent_ref
  8.3 1.6 %copy-done.4 = bf16[512,2048]{1,0:T(8,128)(2,1)S(1)} copy-done((bf16[512,2048]{1,0:T(8,128)(2,1)S(1)}, bf16[512,2048]{1,0:T(8,128)(2,1)}, u32[]{:S(2)}) %copy-start.4) | copy-done | bytes 2097176
  9.9 4.6 %grad_blocks.2 = (bf16[512,640]{1,0:T(8,128)(2,1)S(1)}, bf16[512,640]{1,0:T(8,128)(2,1)S(1)}, bf16[512,384]{1,0:T(8,128)(2,1)S(1)}, bf16[512,384]{1,0:T(8,128)(2,1)S(1)}) custom-call(s32[2]{0:T(128)S(1)} %pad_add_fusion.info_ref, bf16[512,2048]{1,0:T(8,128)(2,1)S(1)} %copy-done.3, bf16[512,2048]{1,0:T(8,128)(2,1)} %collective-permute-done.c1.context_ref, ...), custom_call_target="tpu_custom_call" | custom-call | flops 34359738368 | tf_op jit(solution)/shard_map/grad_blocks/pallas_call | solution.py:116
  14.5 3.0 %collective-permute-start.2 = (bf16[512,640]{1,0:T(8,128)(2,1)S(1)}, bf16[512,640]{1,0:T(8,128)(2,1)S(1)}, u32[]{:S(2)}, u32[]{:S(2)}) collective-permute-start(bf16[512,640]{1,0:T(8,128)(2,1)S(1)} %get-tuple-element.52), channel_id=1, source_target_pairs={{0,4},{1,5},{2,6},{3,7},{4,0},{5,1},{6,2},{7,3},{8,12},{9,13},{10,... | collective-permute-start | bytes 1966088 | tf_op jit(solution)/shard_map/ppermute | solution.py:339
  17.5 1.5 %collective-permute-start.3 = (bf16[512,640]{1,0:T(8,128)(2,1)S(1)}, bf16[512,640]{1,0:T(8,128)(2,1)S(1)}, u32[]{:S(2)}, u32[]{:S(2)}) collective-permute-start(bf16[512,640]{1,0:T(8,128)(2,1)S(1)} %get-tuple-element.54), channel_id=1, source_target_pairs={{0,2},{1,3},{2,0},{3,1},{4,6},{5,7},{6,4},{7,5},{8,10},{9,11},{10,... | collective-permute-start | bytes 1966088 | tf_op jit(solution)/shard_map/ppermute | solution.py:339
  19.0 4.6 %grad_blocks.3 = (bf16[512,640]{1,0:T(8,128)(2,1)S(1)}, bf16[512,640]{1,0:T(8,128)(2,1)S(1)}, bf16[512,384]{1,0:T(8,128)(2,1)S(1)}, bf16[512,384]{1,0:T(8,128)(2,1)S(1)}) custom-call(s32[2]{0:T(128)S(1)} %pad_add_fusion.info_ref, bf16[512,2048]{1,0:T(8,128)(2,1)S(1)} %copy-done.3, bf16[512,2048]{1,0:T(8,128)(2,1)} %collective-permute-done.c1.context_ref, ...), custom_call_target="tpu_custom_call" | custom-call | flops 34359738368 | tf_op jit(solution)/shard_map/grad_blocks/pallas_call | solution.py:116
  23.6 0.6 collective-permute-start.5
  24.2 0.1 collective-permute-start.7
  24.3 1.1 %constant_dynamic-update-slice_fusion.1 = bf16[512,1024]{1,0:T(8,128)(2,1)S(1)} fusion(bf16[256,1024]{1,0:T(8,128)(2,1)} %collective-permute-done.4), kind=kLoop, calls=%fused_computation.23 | loop fusion | bytes 1048576
  25.4 1.1 %constant_dynamic-update-slice_fusion.rest_1_ = bf16[512,1024]{1,0:T(8,128)(2,1)S(1)} fusion(bf16[512,1024]{1,0:T(8,128)(2,1)S(1)} %constant_dynamic-update-slice_fusion.1, bf16[256,1024]{1,0:T(8,128)(2,1)} %collective-permute-done.6), kind=kLoop, calls=%fused_computation.22 | loop fusion | bytes 1048576 | tf_op jit(solution)/shard_map/concatenate | solution.py:398
  26.5 2.1 %collective-permute-start.12 = (bf16[512,1024]{1,0:T(8,128)(2,1)S(1)}, bf16[512,1024]{1,0:T(8,128)(2,1)S(1)}, u32[]{:S(2)}, u32[]{:S(2)}) collective-permute-start(bf16[512,1024]{1,0:T(8,128)(2,1)S(1)} %constant_dynamic-update-slice_fusion.rest_1_), channel_id=1, source_target_pairs={{0,8},{8,0},{16,24},{24,16},{1,9},{9,1},{17,25},{25,17},{2,10},{10... | collective-permute-start | bytes 3145736 | tf_op jit(solution)/shard_map/ppermute | solution.py:342
  28.6 6.5 %collective-permute-done.3 = bf16[512,640]{1,0:T(8,128)(2,1)S(1)} collective-permute-done((bf16[512,640]{1,0:T(8,128)(2,1)S(1)}, bf16[512,640]{1,0:T(8,128)(2,1)S(1)}, u32[]{:S(2)}, u32[]{:S(2)}) %collective-permute-start.3) | collective-permute-done | bytes 655392 | tf_op jit(solution)/shard_map/ppermute | solution.py:339
  35.1 0.2 add_convert_fusion.1
  35.3 0.0 copy-start
  35.3 0.1 collective-permute-start.11
  35.4 0.2 add_convert_fusion
  35.6 2.0 %collective-permute-start.10 = (bf16[256,640]{1,0:T(8,128)(2,1)S(1)}, bf16[256,640]{1,0:T(8,128)(2,1)S(1)}, u32[]{:S(2)}, u32[]{:S(2)}) collective-permute-start(bf16[256,640]{1,0:T(8,128)(2,1)S(1)} %slice.57), channel_id=1, source_target_pairs={{0,2},{1,3},{2,0},{3,1},{4,6},{5,7},{6,4},{7,5},{8,10},{9,11},{10,... | collective-permute-start | bytes 983048 | tf_op jit(solution)/shard_map/ppermute | solution.py:339
  37.7 0.1 convert_element_type.133.rest_0_
  37.8 6.4 %collective-permute-done.5.rest_3_ = bf16[256,1024]{1,0:T(8,128)(2,1)S(1)} collective-permute-done((bf16[256,1024]{1,0:T(8,128)(2,1)}, bf16[256,1024]{1,0:T(8,128)(2,1)S(1)}, u32[]{:S(2)}, u32[]{:S(2)}) %collective-permute-start.5) | collective-permute-done | bytes 524320 | tf_op jit(solution)/shard_map/ppermute | solution.py:339
  44.2 2.1 %collective-permute-done.7.rest_4_ = bf16[256,1024]{1,0:T(8,128)(2,1)S(1)} collective-permute-done((bf16[256,1024]{1,0:T(8,128)(2,1)}, bf16[256,1024]{1,0:T(8,128)(2,1)S(1)}, u32[]{:S(2)}, u32[]{:S(2)}) %collective-permute-start.7) | collective-permute-done | bytes 524320 | tf_op jit(solution)/shard_map/ppermute | solution.py:339
  46.3 0.0 collective-permute-start.8
  46.4 1.9 %collective-permute-start.9 = (bf16[512,384]{1,0:T(8,128)(2,1)S(1)}, bf16[512,384]{1,0:T(8,128)(2,1)S(1)}, u32[]{:S(2)}, u32[]{:S(2)}) collective-permute-start(bf16[512,384]{1,0:T(8,128)(2,1)S(1)} %get-tuple-element.62), channel_id=1, source_target_pairs={{0,2},{1,3},{2,0},{3,1},{4,6},{5,7},{6,4},{7,5},{8,10},{9,11},{10,... | collective-permute-start | bytes 1179656 | tf_op jit(solution)/shard_map/ppermute | solution.py:339
  48.3 2.9 %collective-permute-done.11 = bf16[256,640]{1,0:T(8,128)(2,1)S(1)} collective-permute-done((bf16[256,640]{1,0:T(8,128)(2,1)S(1)}, bf16[256,640]{1,0:T(8,128)(2,1)S(1)}, u32[]{:S(2)}, u32[]{:S(2)}) %collective-permute-start.11) | collective-permute-done | bytes 327712 | tf_op jit(solution)/shard_map/ppermute | solution.py:339
  51.3 0.1 add_convert_fusion.7
  51.4 2.0 %collective-permute-done.10 = bf16[256,640]{1,0:T(8,128)(2,1)S(1)} collective-permute-done((bf16[256,640]{1,0:T(8,128)(2,1)S(1)}, bf16[256,640]{1,0:T(8,128)(2,1)S(1)}, u32[]{:S(2)}, u32[]{:S(2)}) %collective-permute-start.10) | collective-permute-done | bytes 327712 | tf_op jit(solution)/shard_map/ppermute | solution.py:339
  53.4 0.1 add_convert_fusion.6
  53.5 1.6 %collective-permute-start.15 = (bf16[128,1280]{1,0:T(8,128)(2,1)S(1)}, bf16[128,1280]{1,0:T(8,128)(2,1)S(1)}, u32[]{:S(2)}, u32[]{:S(2)}) collective-permute-start(bf16[128,1280]{1,0:T(8,128)(2,1)S(1)} %pad_maximum_fusion), channel_id=1, source_target_pairs={{0,8},{8,0},{16,24},{24,16},{1,9},{9,1},{17,25},{25,17},{2,10},{10... | collective-permute-start | bytes 983048 | tf_op jit(solution)/shard_map/ppermute | solution.py:342
  55.1 5.0 %product.2 = bf16[512,2048]{1,0:T(8,128)(2,1)S(1)} custom-call(s32[2]{0:T(128)S(1)} %pad_add_fusion.info_ref, bf16[512,2048]{1,0:T(8,128)(2,1)} %collective-permute-done.c1.context_ref, bf16[256,2048]{1,0:T(8,128)(2,1)S(1)} %convert_element_type.133.rest_0_, bf16[512,1024]{1,0:T(8,128)(2,1)S(1)} %constant_dynamic-update-slice_fusion.rest_1_, ...), custom_call_target="tpu_custom_call" | custom-call | flops 34359738368 | tf_op jit(solution)/shard_map/product/pallas_call | solution.py:201
  60.2 0.1 collective-permute-start.16
  60.3 0.4 collective-permute-done.9
  60.7 0.1 add_convert_fusion.3
  60.8 0.1 add_convert_fusion.2
  60.9 0.4 collective-permute-start.14
  61.4 1.6 %collective-permute-start.13 = (bf16[256,384]{1,0:T(8,128)(2,1)S(1)}, bf16[256,384]{1,0:T(8,128)(2,1)S(1)}, u32[]{:S(2)}, u32[]{:S(2)}) collective-permute-start(bf16[256,384]{1,0:T(8,128)(2,1)S(1)} %slice.61), channel_id=1, source_target_pairs={{0,2},{1,3},{2,0},{3,1},{4,6},{5,7},{6,4},{7,5},{8,10},{9,11},{10,... | collective-permute-start | bytes 589832 | tf_op jit(solution)/shard_map/ppermute | solution.py:339
  63.0 0.1 add_convert_fusion.5
  63.1 2.7 %collective-permute-start.17 = (bf16[128,1280]{1,0:T(8,128)(2,1)S(1)}, bf16[128,1280]{1,0:T(8,128)(2,1)S(1)}, u32[]{:S(2)}, u32[]{:S(2)}) collective-permute-start(bf16[128,1280]{1,0:T(8,128)(2,1)S(1)} %add_convert_fusion.5), channel_id=1, source_target_pairs={{0,16},{8,24},{16,0},{24,8},{1,17},{9,25},{17,1},{25,9},{2,18},{10... | collective-permute-start | bytes 983048 | tf_op jit(solution)/shard_map/ppermute | solution.py:342
  65.8 5.0 %grad_columns.2 = bf16[512,1024]{1,0:T(8,128)(2,1)S(1)} custom-call(s32[2]{0:T(128)S(1)} %pad_add_fusion.info_ref, bf16[512,2048]{1,0:T(8,128)(2,1)} %collective-permute-done.1.t1.cotangent_ref, bf16[256,2048]{1,0:T(8,128)(2,1)S(1)} %convert_element_type.133.rest_0_, bf16[512,1024]{1,0:T(8,128)(2,1)S(1)} %constant_dynamic-update-slice_fusion.rest_1_, ...), custom_call_target="tpu_custom_call" | custom-call | flops 34359738368 | tf_op jit(solution)/shard_map/grad_columns/pallas_call | solution.py:260
  70.7 0.1 collective-permute-start.19
  70.8 0.1 add_convert_fusion.11
  70.9 0.1 add_convert_fusion.10
  71.0 1.6 %collective-permute-start.18 = (bf16[128,768]{1,0:T(8,128)(2,1)S(1)}, bf16[128,768]{1,0:T(8,128)(2,1)S(1)}, u32[]{:S(2)}, u32[]{:S(2)}) collective-permute-start(bf16[128,768]{1,0:T(8,128)(2,1)S(1)} %pad_maximum_fusion.1), channel_id=1, source_target_pairs={{0,8},{8,0},{16,24},{24,16},{1,9},{9,1},{17,25},{25,17},{2,10},{10... | collective-permute-start | bytes 589832 | tf_op jit(solution)/shard_map/ppermute | solution.py:342
  72.7 4.8 %product.3 = bf16[512,2048]{1,0:T(8,128)(2,1)} custom-call(s32[2]{0:T(128)S(1)} %pad_add_fusion.info_ref, bf16[512,2048]{1,0:T(8,128)(2,1)S(1)} %copy-done.3, bf16[256,2048]{1,0:T(8,128)(2,1)S(1)} %convert_element_type.133.rest_0_, bf16[512,1024]{1,0:T(8,128)(2,1)S(1)} %constant_dynamic-update-slice_fusion.rest_1_, ...), custom_call_target="tpu_custom_call" | custom-call | tf_op jit(solution)/shard_map/product/pallas_call | solution.py:201
  77.5 2.8 %collective-permute-done.17 = bf16[128,1280]{1,0:T(8,128)(2,1)S(1)} collective-permute-done((bf16[128,1280]{1,0:T(8,128)(2,1)S(1)}, bf16[128,1280]{1,0:T(8,128)(2,1)S(1)}, u32[]{:S(2)}, u32[]{:S(2)}) %collective-permute-start.17) | collective-permute-done | bytes 327712 | tf_op jit(solution)/shard_map/ppermute | solution.py:342
  80.3 0.1 add_convert_fusion.4.rest_0_
  80.3 4.0 %collective-permute-done.18 = bf16[128,768]{1,0:T(8,128)(2,1)S(1)} collective-permute-done((bf16[128,768]{1,0:T(8,128)(2,1)S(1)}, bf16[128,768]{1,0:T(8,128)(2,1)S(1)}, u32[]{:S(2)}, u32[]{:S(2)}) %collective-permute-start.18) | collective-permute-done | bytes 196640 | tf_op jit(solution)/shard_map/ppermute | solution.py:342
  84.4 0.1 add_convert_fusion.9
  84.4 0.0 copy-start.5
  84.4 0.1 collective-permute-start.20
  84.5 1.9 %collective-permute-start.22 = (bf16[128,1280]{1,0:T(8,128)(2,1)S(1)}, bf16[128,1280]{1,0:T(8,128)(2,1)S(1)}, u32[]{:S(2)}, u32[]{:S(2)}) collective-permute-start(bf16[128,1280]{1,0:T(8,128)(2,1)S(1)} %add_convert_fusion.4.rest_0_), channel_id=1, source_target_pairs={{0,8},{8,0},{16,24},{24,16},{1,9},{9,1},{17,25},{25,17},{2,10},{10... | collective-permute-start | bytes 983048 | tf_op jit(solution)/shard_map/ppermute | solution.py:342
  86.4 2.4 %stepped.4 = (f32[256,2048]{1,0:T(8,128)}, f32[256,2048]{1,0:T(8,128)}, f32[256,2048]{1,0:T(8,128)}) custom-call(s32[2]{0:T(128)S(1)} %pad_add_fusion.info_ref, bf16[128,1280]{1,0:T(8,128)(2,1)S(1)} %add_convert_fusion.4.rest_0_, f32[256,2048]{1,0:T(8,128)S(1)} %copy-done, f32[256,2048]{1,0:T(8,128)S(1)} %copy-done.1, f32[256,2048]{1,0:T(8,128)S(1)} %copy-done.2), custom_call_target="tpu_custom_call" | custom-call | flops 2147483648 | tf_op jit(solution)/shard_map/stepped/pallas_call | solution.py:309
  88.8 4.8 %grad_columns.3 = bf16[512,2048]{1,0:T(8,128)(2,1)} custom-call(s32[2]{0:T(128)S(1)} %pad_add_fusion.info_ref, bf16[512,2048]{1,0:T(8,128)(2,1)S(1)} %copy-done.5, bf16[256,2048]{1,0:T(8,128)(2,1)S(1)} %convert_element_type.133.rest_0_, bf16[512,1024]{1,0:T(8,128)(2,1)S(1)} %constant_dynamic-update-slice_fusion.rest_1_, ...), custom_call_target="tpu_custom_call" | custom-call | flops 34359738368 | tf_op jit(solution)/shard_map/grad_columns/pallas_call | solution.py:260
  93.6 2.0 %collective-permute-done.20 = bf16[128,768]{1,0:T(8,128)(2,1)S(1)} collective-permute-done((bf16[128,768]{1,0:T(8,128)(2,1)S(1)}, bf16[128,768]{1,0:T(8,128)(2,1)S(1)}, u32[]{:S(2)}, u32[]{:S(2)}) %collective-permute-start.20) | collective-permute-done | bytes 196640 | tf_op jit(solution)/shard_map/ppermute | solution.py:342
  95.6 0.1 collective-permute-start.21
  95.7 2.0 %stepped.5 = (f32[256,2048]{1,0:T(8,128)}, f32[256,2048]{1,0:T(8,128)}, f32[256,2048]{1,0:T(8,128)}) custom-call(s32[2]{0:T(128)S(1)} %pad_add_fusion.info_ref, bf16[128,768]{1,0:T(8,128)(2,1)S(1)} %add_convert_fusion.8.rest_0_, f32[256,2048]{1,0:T(8,128)S(1)} %copy-done, ...), custom_call_target="tpu_custom_call", output_to_operand_aliasing={{0}: (5, {}), {1}: (6, {}), {2}: (7, {})} | custom-call | tf_op jit(solution)/shard_map/stepped/pallas_call | solution.py:309
  97.7 0.9 collective-permute-done.22.rest_0_
  98.6 2.4 %stepped.6 = (f32[256,2048]{1,0:T(8,128)}, f32[256,2048]{1,0:T(8,128)}, f32[256,2048]{1,0:T(8,128)}) custom-call(s32[2]{0:T(128)S(1)} %pad_add_fusion.info_ref, bf16[128,1280]{1,0:T(8,128)(2,1)S(1)} %collective-permute-done.22.rest_0_, f32[256,2048]{1,0:T(8,128)S(1)} %copy-done, ...), custom_call_target="tpu_custom_call", output_to_operand_aliasing={{0}: (5, {}), {1}: (6, {}), {2}: (7, {})} | custom-call | tf_op jit(solution)/shard_map/stepped/pallas_call | solution.py:309
  101.0 1.7 %collective-permute-done.21.rest_0_ = bf16[128,768]{1,0:T(8,128)(2,1)S(1)} collective-permute-done((bf16[128,768]{1,0:T(8,128)(2,1)S(1)}, bf16[128,768]{1,0:T(8,128)(2,1)S(1)}, u32[]{:S(2)}, u32[]{:S(2)}) %collective-permute-start.21) | collective-permute-done | bytes 196640 | tf_op jit(solution)/shard_map/ppermute | solution.py:342
  102.7 2.0 %stepped.7 = (f32[256,2048]{1,0:T(8,128)}, f32[256,2048]{1,0:T(8,128)}, f32[256,2048]{1,0:T(8,128)}) custom-call(s32[2]{0:T(128)S(1)} %pad_add_fusion.info_ref, bf16[128,768]{1,0:T(8,128)(2,1)S(1)} %collective-permute-done.21.rest_0_, f32[256,2048]{1,0:T(8,128)S(1)} %copy-done, ...), custom_call_target="tpu_custom_call", output_to_operand_aliasing={{0}: (5, {}), {1}: (6, {}), {2}: (7, {})} | custom-call | tf_op jit(solution)/shard_map/stepped/pallas_call | solution.py:309
  (27 shorter events, 0.2 us)
Async XLA Ops:
  0.6 7.7 %copy-start.3 = (bf16[512,2048]{1,0:T(8,128)(2,1)S(1)}, bf16[512,2048]{1,0:T(8,128)(2,1)}, u32[]{:S(2)}) copy-start(bf16[512,2048]{1,0:T(8,128)(2,1)} %context_ref) | copy-start | bytes 6291460
  0.6 6.9 %collective-permute-start = (bf16[512,2048]{1,0:T(8,128)(2,1)}, bf16[512,2048]{1,0:T(8,128)(2,1)}, u32[]{:S(2)}, u32[]{:S(2)}) collective-permute-start(bf16[512,2048]{1,0:T(8,128)(2,1)} %context_ref), channel_id=1, source_target_pairs={{0,1},{1,0},{2,3},{3,2},{4,5},{5,4},{6,7},{7,6},{8,9},{9,8},{10,11... | collective-permute-start | bytes 6291464 | tf_op jit(solution)/shard_map/ppermute | solution.py:339
  1.2 7.1 %collective-permute-start.1 = (bf16[512,2048]{1,0:T(8,128)(2,1)}, bf16[512,2048]{1,0:T(8,128)(2,1)}, u32[]{:S(2)}, u32[]{:S(2)}) collective-permute-start(bf16[512,2048]{1,0:T(8,128)(2,1)} %cotangent_ref), channel_id=1, source_target_pairs={{0,1},{1,0},{2,3},{3,2},{4,5},{5,4},{6,7},{7,6},{8,9},{9,8},{10,11... | collective-permute-start | bytes 6291464 | tf_op jit(solution)/shard_map/ppermute | solution.py:339
  2.9 20.7 %collective-permute-start.6 = (bf16[256,1024]{1,0:T(8,128)(2,1)S(1)}, bf16[256,1024]{1,0:T(8,128)(2,1)}, u32[]{:S(2)}, u32[]{:S(2)}) collective-permute-start(bf16[256,1024]{1,0:T(8,128)(2,1)S(1)} %get-tuple-element.91), channel_id=1, source_target_pairs={{0,4},{1,5},{2,6},{3,7},{4,0},{5,1},{6,2},{7,3},{8,12},{9,13},{10,... | collective-permute-start | bytes 1572872 | tf_op jit(solution)/shard_map/ppermute | solution.py:339
  6.0 17.7 %collective-permute-start.4 = (bf16[256,1024]{1,0:T(8,128)(2,1)S(1)}, bf16[256,1024]{1,0:T(8,128)(2,1)}, u32[]{:S(2)}, u32[]{:S(2)}) collective-permute-start(bf16[256,1024]{1,0:T(8,128)(2,1)S(1)} %get-tuple-element.92), channel_id=1, source_target_pairs={{0,2},{1,3},{2,0},{3,1},{4,6},{5,7},{6,4},{7,5},{8,10},{9,11},{10,... | collective-permute-start | bytes 1572872 | tf_op jit(solution)/shard_map/ppermute | solution.py:339
  8.3 1.6 %copy-start.4 = (bf16[512,2048]{1,0:T(8,128)(2,1)S(1)}, bf16[512,2048]{1,0:T(8,128)(2,1)}, u32[]{:S(2)}) copy-start(bf16[512,2048]{1,0:T(8,128)(2,1)} %cotangent_ref) | copy-start | bytes 6291460
  14.5 20.8 %collective-permute-start.2 = (bf16[512,640]{1,0:T(8,128)(2,1)S(1)}, bf16[512,640]{1,0:T(8,128)(2,1)S(1)}, u32[]{:S(2)}, u32[]{:S(2)}) collective-permute-start(bf16[512,640]{1,0:T(8,128)(2,1)S(1)} %get-tuple-element.52), channel_id=1, source_target_pairs={{0,4},{1,5},{2,6},{3,7},{4,0},{5,1},{6,2},{7,3},{8,12},{9,13},{10,... | collective-permute-start | bytes 1966088 | tf_op jit(solution)/shard_map/ppermute | solution.py:339
  17.5 17.6 %collective-permute-start.3 = (bf16[512,640]{1,0:T(8,128)(2,1)S(1)}, bf16[512,640]{1,0:T(8,128)(2,1)S(1)}, u32[]{:S(2)}, u32[]{:S(2)}) collective-permute-start(bf16[512,640]{1,0:T(8,128)(2,1)S(1)} %get-tuple-element.54), channel_id=1, source_target_pairs={{0,2},{1,3},{2,0},{3,1},{4,6},{5,7},{6,4},{7,5},{8,10},{9,11},{10,... | collective-permute-start | bytes 1966088 | tf_op jit(solution)/shard_map/ppermute | solution.py:339
  23.6 20.6 %collective-permute-start.5 = (bf16[256,1024]{1,0:T(8,128)(2,1)}, bf16[256,1024]{1,0:T(8,128)(2,1)S(1)}, u32[]{:S(2)}, u32[]{:S(2)}) collective-permute-start(bf16[256,1024]{1,0:T(8,128)(2,1)} %collective-permute-done.4), channel_id=1, source_target_pairs={{0,4},{1,5},{2,6},{3,7},{4,0},{5,1},{6,2},{7,3},{8,12},{9,13},{10,... | collective-permute-start | bytes 1572872 | tf_op jit(solution)/shard_map/ppermute | solution.py:339
  24.2 22.1 %collective-permute-start.7 = (bf16[256,1024]{1,0:T(8,128)(2,1)}, bf16[256,1024]{1,0:T(8,128)(2,1)S(1)}, u32[]{:S(2)}, u32[]{:S(2)}) collective-permute-start(bf16[256,1024]{1,0:T(8,128)(2,1)} %collective-permute-done.6), channel_id=1, source_target_pairs={{0,2},{1,3},{2,0},{3,1},{4,6},{5,7},{6,4},{7,5},{8,10},{9,11},{10,... | collective-permute-start | bytes 1572872 | tf_op jit(solution)/shard_map/ppermute | solution.py:339
  26.5 28.6 %collective-permute-start.12 = (bf16[512,1024]{1,0:T(8,128)(2,1)S(1)}, bf16[512,1024]{1,0:T(8,128)(2,1)S(1)}, u32[]{:S(2)}, u32[]{:S(2)}) collective-permute-start(bf16[512,1024]{1,0:T(8,128)(2,1)S(1)} %constant_dynamic-update-slice_fusion.rest_1_), channel_id=1, source_target_pairs={{0,8},{8,0},{16,24},{24,16},{1,9},{9,1},{17,25},{25,17},{2,10},{10... | collective-permute-start | bytes 3145736 | tf_op jit(solution)/shard_map/ppermute | solution.py:342
  35.3 2.4 %copy-start = (f32[256,2048]{1,0:T(8,128)S(1)}, f32[256,2048]{1,0:T(8,128)}, u32[]{:S(2)}) copy-start(f32[256,2048]{1,0:T(8,128)} %rest_1_.6) | copy-start | bytes 6291460
  35.3 15.9 %collective-permute-start.11 = (bf16[256,640]{1,0:T(8,128)(2,1)S(1)}, bf16[256,640]{1,0:T(8,128)(2,1)S(1)}, u32[]{:S(2)}, u32[]{:S(2)}) collective-permute-start(bf16[256,640]{1,0:T(8,128)(2,1)S(1)} %slice.59), channel_id=1, source_target_pairs={{0,4},{1,5},{2,6},{3,7},{4,0},{5,1},{6,2},{7,3},{8,12},{9,13},{10,... | collective-permute-start | bytes 983048 | tf_op jit(solution)/shard_map/ppermute | solution.py:339
  35.6 17.7 %collective-permute-start.10 = (bf16[256,640]{1,0:T(8,128)(2,1)S(1)}, bf16[256,640]{1,0:T(8,128)(2,1)S(1)}, u32[]{:S(2)}, u32[]{:S(2)}) collective-permute-start(bf16[256,640]{1,0:T(8,128)(2,1)S(1)} %slice.57), channel_id=1, source_target_pairs={{0,2},{1,3},{2,0},{3,1},{4,6},{5,7},{6,4},{7,5},{8,10},{9,11},{10,... | collective-permute-start | bytes 983048 | tf_op jit(solution)/shard_map/ppermute | solution.py:339
  46.3 14.5 %collective-permute-start.8 = (bf16[512,384]{1,0:T(8,128)(2,1)S(1)}, bf16[512,384]{1,0:T(8,128)(2,1)S(1)}, u32[]{:S(2)}, u32[]{:S(2)}) collective-permute-start(bf16[512,384]{1,0:T(8,128)(2,1)S(1)} %get-tuple-element.59), channel_id=1, source_target_pairs={{0,4},{1,5},{2,6},{3,7},{4,0},{5,1},{6,2},{7,3},{8,12},{9,13},{10,... | collective-permute-start | bytes 1179656 | tf_op jit(solution)/shard_map/ppermute | solution.py:339
  46.4 14.3 %collective-permute-start.9 = (bf16[512,384]{1,0:T(8,128)(2,1)S(1)}, bf16[512,384]{1,0:T(8,128)(2,1)S(1)}, u32[]{:S(2)}, u32[]{:S(2)}) collective-permute-start(bf16[512,384]{1,0:T(8,128)(2,1)S(1)} %get-tuple-element.62), channel_id=1, source_target_pairs={{0,2},{1,3},{2,0},{3,1},{4,6},{5,7},{6,4},{7,5},{8,10},{9,11},{10,... | collective-permute-start | bytes 1179656 | tf_op jit(solution)/shard_map/ppermute | solution.py:339
  53.5 9.5 %collective-permute-start.15 = (bf16[128,1280]{1,0:T(8,128)(2,1)S(1)}, bf16[128,1280]{1,0:T(8,128)(2,1)S(1)}, u32[]{:S(2)}, u32[]{:S(2)}) collective-permute-start(bf16[128,1280]{1,0:T(8,128)(2,1)S(1)} %pad_maximum_fusion), channel_id=1, source_target_pairs={{0,8},{8,0},{16,24},{24,16},{1,9},{9,1},{17,25},{25,17},{2,10},{10... | collective-permute-start | bytes 983048 | tf_op jit(solution)/shard_map/ppermute | solution.py:342
  60.2 12.5 %collective-permute-start.16 = (bf16[512,2048]{1,0:T(8,128)(2,1)S(1)}, bf16[512,2048]{1,0:T(8,128)(2,1)S(1)}, u32[]{:S(2)}, u32[]{:S(2)}) collective-permute-start(bf16[512,2048]{1,0:T(8,128)(2,1)S(1)} %product.2), channel_id=1, source_target_pairs={{0,1},{1,0},{2,3},{3,2},{4,5},{5,4},{6,7},{7,6},{8,9},{9,8},{10,11... | collective-permute-start | bytes 6291464 | tf_op jit(solution)/shard_map/ppermute | solution.py:339
  60.9 9.9 %collective-permute-start.14 = (bf16[256,384]{1,0:T(8,128)(2,1)S(1)}, bf16[256,384]{1,0:T(8,128)(2,1)S(1)}, u32[]{:S(2)}, u32[]{:S(2)}) collective-permute-start(bf16[256,384]{1,0:T(8,128)(2,1)S(1)} %slice.63), channel_id=1, source_target_pairs={{0,4},{1,5},{2,6},{3,7},{4,0},{5,1},{6,2},{7,3},{8,12},{9,13},{10,... | collective-permute-start | bytes 589832 | tf_op jit(solution)/shard_map/ppermute | solution.py:339
  61.4 9.5 %collective-permute-start.13 = (bf16[256,384]{1,0:T(8,128)(2,1)S(1)}, bf16[256,384]{1,0:T(8,128)(2,1)S(1)}, u32[]{:S(2)}, u32[]{:S(2)}) collective-permute-start(bf16[256,384]{1,0:T(8,128)(2,1)S(1)} %slice.61), channel_id=1, source_target_pairs={{0,2},{1,3},{2,0},{3,1},{4,6},{5,7},{6,4},{7,5},{8,10},{9,11},{10,... | collective-permute-start | bytes 589832 | tf_op jit(solution)/shard_map/ppermute | solution.py:339
  63.1 17.2 %collective-permute-start.17 = (bf16[128,1280]{1,0:T(8,128)(2,1)S(1)}, bf16[128,1280]{1,0:T(8,128)(2,1)S(1)}, u32[]{:S(2)}, u32[]{:S(2)}) collective-permute-start(bf16[128,1280]{1,0:T(8,128)(2,1)S(1)} %add_convert_fusion.5), channel_id=1, source_target_pairs={{0,16},{8,24},{16,0},{24,8},{1,17},{9,25},{17,1},{25,9},{2,18},{10... | collective-permute-start | bytes 983048 | tf_op jit(solution)/shard_map/ppermute | solution.py:342
  70.7 18.0 %collective-permute-start.19 = (bf16[512,1024]{1,0:T(8,128)(2,1)S(1)}, bf16[512,1024]{1,0:T(8,128)(2,1)S(1)}, u32[]{:S(2)}, u32[]{:S(2)}) collective-permute-start(bf16[512,1024]{1,0:T(8,128)(2,1)S(1)} %grad_columns.2), channel_id=1, source_target_pairs={{0,1},{1,0},{2,3},{3,2},{4,5},{5,4},{6,7},{7,6},{8,9},{9,8},{10,11... | collective-permute-start | bytes 3145736 | tf_op jit(solution)/shard_map/ppermute | solution.py:339
  71.0 15.4 %copy-start.1 = (f32[256,2048]{1,0:T(8,128)S(1)}, f32[256,2048]{1,0:T(8,128)}, u32[]{:S(2)}) copy-start(f32[256,2048]{1,0:T(8,128)} %rest_2_.7) | copy-start | bytes 6291460
  71.0 15.4 %copy-start.2 = (f32[256,2048]{1,0:T(8,128)S(1)}, f32[256,2048]{1,0:T(8,128)}, u32[]{:S(2)}) copy-start(f32[256,2048]{1,0:T(8,128)} %rest_3_.7) | copy-start | bytes 6291460
  71.0 13.4 %collective-permute-start.18 = (bf16[128,768]{1,0:T(8,128)(2,1)S(1)}, bf16[128,768]{1,0:T(8,128)(2,1)S(1)}, u32[]{:S(2)}, u32[]{:S(2)}) collective-permute-start(bf16[128,768]{1,0:T(8,128)(2,1)S(1)} %pad_maximum_fusion.1), channel_id=1, source_target_pairs={{0,8},{8,0},{16,24},{24,16},{1,9},{9,1},{17,25},{25,17},{2,10},{10... | collective-permute-start | bytes 589832 | tf_op jit(solution)/shard_map/ppermute | solution.py:342
  84.4 4.3 %copy-start.5 = (bf16[512,2048]{1,0:T(8,128)(2,1)S(1)}, bf16[512,2048]{1,0:T(8,128)(2,1)}, u32[]{:S(2)}) copy-start(bf16[512,2048]{1,0:T(8,128)(2,1)} %cotangent_ref) | copy-start | bytes 6291460
  84.4 11.1 %collective-permute-start.20 = (bf16[128,768]{1,0:T(8,128)(2,1)S(1)}, bf16[128,768]{1,0:T(8,128)(2,1)S(1)}, u32[]{:S(2)}, u32[]{:S(2)}) collective-permute-start(bf16[128,768]{1,0:T(8,128)(2,1)S(1)} %add_convert_fusion.9), channel_id=1, source_target_pairs={{0,16},{8,24},{16,0},{24,8},{1,17},{9,25},{17,1},{25,9},{2,18},{10... | collective-permute-start | bytes 589832 | tf_op jit(solution)/shard_map/ppermute | solution.py:342
  84.5 14.1 %collective-permute-start.22 = (bf16[128,1280]{1,0:T(8,128)(2,1)S(1)}, bf16[128,1280]{1,0:T(8,128)(2,1)S(1)}, u32[]{:S(2)}, u32[]{:S(2)}) collective-permute-start(bf16[128,1280]{1,0:T(8,128)(2,1)S(1)} %add_convert_fusion.4.rest_0_), channel_id=1, source_target_pairs={{0,8},{8,0},{16,24},{24,16},{1,9},{9,1},{17,25},{25,17},{2,10},{10... | collective-permute-start | bytes 983048 | tf_op jit(solution)/shard_map/ppermute | solution.py:342
  95.6 7.1 %collective-permute-start.21 = (bf16[128,768]{1,0:T(8,128)(2,1)S(1)}, bf16[128,768]{1,0:T(8,128)(2,1)S(1)}, u32[]{:S(2)}, u32[]{:S(2)}) collective-permute-start(bf16[128,768]{1,0:T(8,128)(2,1)S(1)} %add_convert_fusion.8.rest_0_), channel_id=1, source_target_pairs={{0,8},{8,0},{16,24},{24,16},{1,9},{9,1},{17,25},{25,17},{2,10},{10... | collective-permute-start | bytes 589832 | tf_op jit(solution)/shard_map/ppermute | solution.py:342
